TPU v7x, 32 devices: a whole 2x2x4 slice. The times are simulated.
32 devices in a mesh: groups: 2 (over y), fsdp: 4 (over z), tp: 2 (over x), sub: 2 (over core).
Axes of the slice: x: 2, y: 2, z: 4, core: 2. Of those that a mesh axis runs over, the one named last changes fastest.
Arguments:
- hidden_acts: bfloat16 [2048, 11008], P(('groups', 'fsdp', 'sub'), 'tp'), parts along dimension 0, may hold values from -6 to 6
- cotangent: bfloat16 [2048, 4096], P(('groups', 'fsdp', 'sub'), 'tp'), parts along dimension 0, may hold values from -6 to 6
- w_down: bfloat16 [11008, 4096], P(('tp', 'fsdp')), may hold values from -0.0546875 to 0.0546875
- projector: bfloat16 [4096, 256], P('tp'), may hold values from -0.09375 to 0.09375
- first_moment: float32 [22016, 256], P(('groups', 'tp', 'fsdp')), parts along dimension 0, may hold values from -0.06 to 0.06
- second_moment: float32 [22016, 256], P(('groups', 'tp', 'fsdp')), parts along dimension 0, may hold values from 1e-06 to 0.0001
Outputs:
- block_out: bfloat16 [2048, 4096], P(('groups', 'fsdp', 'sub'), 'tp'), parts along dimension 0
- acts_grad: bfloat16 [2048, 11008], P(('groups', 'fsdp', 'sub'), 'tp'), parts along dimension 0
- weight_step: float32 [22016, 4096], P(('groups', 'tp', 'fsdp')), parts along dimension 0
- new_first: float32 [22016, 256], P(('groups', 'tp', 'fsdp')), parts along dimension 0
- new_second: float32 [22016, 256], P(('groups', 'tp', 'fsdp')), parts along dimension 0
There are 2 independent parts, one for each index of `groups`. A program takes and returns all parts, laid end to end along the dimension named above; an argument that names none is the same for every part. Nothing has to cross between parts.
All inputs are finite; a program needn't handle non-finite values.
Results may differ from a plain program's by a relative error of at most 0.0052.
Values may be sent and summed in bfloat16 or wider, within the bound.
No kernel may reach another device: no remote copies, remote signals or barrier semaphores. Data moves between devices by JAX's collectives and lax.ppermute only.
A program may use at most 192 MiB of HBM per device.

v0:
```python
import jax
import jax.numpy as jnp
from jax import lax
from jax.experimental import pallas as pl
from jax.experimental.pallas import tpu as pltpu
from jax.sharding import PartitionSpec as P

first_decay = 0.9
second_decay = 0.999
first_fix = 1.0 - 0.9**10
second_fix = 1.0 - 0.999**10
epsilon = 1e-08

f32 = jnp.float32
bf16 = jnp.bfloat16


def swap(x, axis, bit, name="swap"):
    n = lax.axis_size(axis)
    with jax.named_scope(name):
        return lax.ppermute(x, axis, [(i, i ^ bit) for i in range(n)])


def mm(a, b):
    return jnp.dot(a, b, preferred_element_type=f32)


def mm_t(a, b):
    return lax.dot_general(a, b, (((1,), (1,)), ((), ())), preferred_element_type=f32)


def mm_tn(a, b):
    return lax.dot_general(a, b, (((0,), (0,)), ((), ())), preferred_element_type=f32)


def adam_rows(gradient, first_rows, second_rows):
    new_first = first_decay * first_rows + (1.0 - first_decay) * gradient
    new_second = second_decay * second_rows + (1.0 - second_decay) * gradient * gradient
    direction = (new_first / first_fix / (jnp.sqrt(new_second / second_fix) + epsilon)).astype(bf16)
    return direction, new_first, new_second


def halves(x, axis, t):
    n = x.shape[axis] // 2
    return (
        lax.dynamic_slice_in_dim(x, t * n, n, axis),
        lax.dynamic_slice_in_dim(x, (1 - t) * n, n, axis),
    )


def in_order(mine, other, index, axis):
    return jnp.concatenate(
        [jnp.where(index == 0, mine, other), jnp.where(index == 0, other, mine)], axis=axis
    )


def full_basis_of(projector):
    if lax.axis_size("tp") != 2:
        return lax.all_gather(projector, "tp", axis=0, tiled=True)
    t, c = lax.axis_index("tp"), lax.axis_index("sub")
    mine = halves(projector, 0, c)[0]
    got = swap(mine, "tp", 1)
    other = in_order(got, swap(got, "sub", 1), c, 0)
    return in_order(projector, other, t, 0)


def shards_any(hidden_acts, cotangent, w_down, projector, first_moment, second_moment):
    nz, nx = lax.axis_size("fsdp"), lax.axis_size("tp")
    z, t = lax.axis_index("fsdp"), lax.axis_index("tp")
    rows, width = hidden_acts.shape[0], w_down.shape[0]
    bits = [1 << b for b in range(nz.bit_length() - 1)]
    two = nx == 2

    cot = {0: cotangent}
    for bit in reversed(bits):
        for k in list(cot):
            cot[k ^ bit] = swap(cot[k], "fsdp", bit)
    hid = {}
    for k in range(nz):
        part = lax.dynamic_slice_in_dim(hidden_acts, (z ^ k) * width, width, 1)
        hid[k] = swap(part, "fsdp", k) if k else part

    basis = full_basis_of(projector)
    if two:
        w_mine, w_other = halves(w_down, 1, t)
        b_mine, b_other = halves(basis, 0, t)
        pairs = {k: ((cot[k], w_mine, b_mine), (swap(cot[k], "tp", 1), w_other, b_other)) for k in cot}
    else:
        pairs = {
            k: ((lax.all_gather(cot[k], "tp", axis=1, tiled=True), w_down, basis),) for k in cot
        }

    grads, coords = {}, {}
    for k in cot:
        back = sum(mm_t(c, w) for c, w, _ in pairs[k]).astype(bf16)
        grads[k] = swap(back, "fsdp", k) if k else back
        coords[k] = sum(mm(c, b) for c, _, b in pairs[k]).astype(bf16)
    order = jnp.stack([grads[k] for k in range(nz)])
    acts_grad = jnp.concatenate(
        [lax.dynamic_index_in_dim(order, z ^ j, 0, keepdims=False) for j in range(nz)], axis=1
    )

    outs = {}
    for k in range(nz):
        if two:
            away = mm(hid[k], w_other).astype(bf16)
            outs[k] = mm(hid[k], w_mine) + swap(away, "tp", 1).astype(f32)
        else:
            outs[k] = lax.psum_scatter(
                mm(hid[k], w_down).astype(bf16), "tp", scatter_dimension=1, tiled=True
            ).astype(f32)
    for bit in bits:
        for k in [k for k in outs if k & bit]:
            got = swap(outs.pop(k).astype(bf16), "fsdp", bit)
            outs[k ^ bit] = outs[k ^ bit] + got.astype(f32)
    block_out = outs[0].astype(bf16)

    all_hid = jnp.concatenate([hid[k] for k in range(nz)], axis=0)
    all_coords = jnp.concatenate([coords[k] for k in range(nz)], axis=0)
    local = mm_tn(all_hid, all_coords)
    owned = local + swap(local, "sub", 1)
    token_count = f32(rows * nz * lax.axis_size("sub"))
    direction, new_first, new_second = adam_rows(owned / token_count, first_moment, second_moment)
    weight_step = mm_t(direction, basis)
    return (block_out, acts_grad, weight_step, new_first, new_second)


light = pl.CostEstimate(flops=1, bytes_accessed=1, transcendentals=0)
strip = 512


def in_vmem(kernel, name, at, ins, outs, mib=12):
    vmem = pl.BlockSpec(memory_space=pltpu.VMEM)
    return pl.pallas_call(
        kernel,
        in_specs=[pl.BlockSpec(memory_space=pltpu.SMEM)] + [vmem] * len(ins),
        out_specs=[vmem] * len(outs),
        out_shape=outs,
        compiler_params=pltpu.CompilerParams(vmem_limit_bytes=mib << 20),
        cost_estimate=light,
        name=name,
    )(at, *ins)


def forward(at, h, w):
    rows, width = h.shape[0], w.shape[1]
    half = width // 2

    def kernel(at, h, w, p, m):
        mine, far = at[0] * half, (1 - at[0]) * half
        for j in range(0, half, strip):
            p[:, j : j + strip] = mm(h[...], w[:, pl.ds(pl.multiple_of(far + j, strip), strip)]).astype(bf16)
        for j in range(0, half, strip):
            m[:, j : j + strip] = mm(h[...], w[:, pl.ds(pl.multiple_of(mine + j, strip), strip)])

    return in_vmem(
        kernel, "forward", at, (h, w),
        [jax.ShapeDtypeStruct((rows, half), bf16), jax.ShapeDtypeStruct((rows, half), f32)],
    )


def backward(at, c, x, w, projector, got, shared):
    rows, half = c.shape
    units = w.shape[0]
    part = half // 2
    tall = 352

    def kernel(at, c, x, w, basis, got, shared, g, coords):
        mine = pl.multiple_of(at[0] * half, half)
        far = pl.multiple_of((1 - at[0]) * half, half)
        first = pl.multiple_of(at[1] * part, part)
        second = pl.multiple_of((1 - at[1]) * part, part)
        for j in range(0, units, tall):
            k = min(j + tall, units)
            g[j:k, :] = (
                mm_t(w[j:k, pl.ds(mine, half)], c[...]) + mm_t(w[j:k, pl.ds(far, half)], x[...])
            ).astype(bf16)
        coords[...] = (
            mm(c[...], basis[...])
            + mm(x[:, pl.ds(first, part)], got[...])
            + mm(x[:, pl.ds(second, part)], shared[...])
        ).astype(bf16)

    return in_vmem(
        kernel, "backward", at, (c, x, w, projector, got, shared),
        [
            jax.ShapeDtypeStruct((units, rows), bf16),
            jax.ShapeDtypeStruct((rows, projector.shape[1]), bf16),
        ],
    )


def project(at, hs, coords):
    n, units, rank = len(hs), hs[0].shape[1], coords[0].shape[1]
    tall = units // 2

    def kernel(at, *refs):
        upper, lower = refs[2 * n :]
        total = sum(mm_tn(h[...], c[...]) for h, c in zip(refs[:n], refs[n : 2 * n]))
        upper[...], lower[...] = total[:tall], total[tall:]

    return in_vmem(
        kernel, "project", at, (*hs, *coords), [jax.ShapeDtypeStruct((tall, rank), f32)] * 2
    )


def adam_step(at, here, there, tokens, first_moment, second_moment, projector, got, shared):
    units, rank = first_moment.shape
    half = projector.shape[0]
    part, width = half // 2, 2 * half
    tall = units // 4

    def kernel(at, h_up, h_low, t_up, t_low, first, second, basis, got, shared, step, new_first, new_second):
        upper = pl.program_id(0) < 2
        gradient = jnp.where(upper, h_up[...] + t_up[...], h_low[...] + t_low[...]) / f32(tokens)
        direction, new_first[...], new_second[...] = adam_rows(gradient, first[...], second[...])
        t, c = at[0], at[1]
        mine = pl.multiple_of(t * half, half)
        one = pl.multiple_of((1 - t) * half + c * part, part)
        two = pl.multiple_of((1 - t) * half + (1 - c) * part, part)
        step[:, pl.ds(mine, half)] = mm_t(direction, basis[...])
        step[:, pl.ds(one, part)] = mm_t(direction, got[...])
        step[:, pl.ds(two, part)] = mm_t(direction, shared[...])

    def block(index):
        return pl.BlockSpec((tall, rank), index)

    def up(i):
        return (jnp.minimum(i, 1), 0)

    def low(i):
        return (jnp.maximum(i, 2) - 2, 0)

    def row(i):
        return (i, 0)

    def whole(v):
        return pl.BlockSpec(v.shape, lambda i: (0, 0))

    small = jax.ShapeDtypeStruct((units, rank), f32)
    return pl.pallas_call(
        kernel,
        grid=(4,),
        in_specs=[pl.BlockSpec(memory_space=pltpu.SMEM)]
        + [block(up), block(low), block(up), block(low), block(row), block(row)]
        + [whole(projector), whole(got), whole(shared)],
        out_specs=[pl.BlockSpec((tall, width), row), block(row), block(row)],
        out_shape=[jax.ShapeDtypeStruct((units, width), f32), small, small],
        compiler_params=pltpu.CompilerParams(vmem_limit_bytes=24 << 20),
        cost_estimate=light,
        name="adam_step",
    )(at, *here, *there, first_moment, second_moment, projector, got, shared)


class Order:
    def __init__(self):
        self.last = ()

    def go(self, x):
        return lax.optimization_barrier((x, *self.last))[0]

    def seen(self, *done):
        self.last = done


def shards_line(hidden_acts, cotangent, w_down, projector, first_moment, second_moment):
    z, t, c = lax.axis_index("fsdp"), lax.axis_index("tp"), lax.axis_index("sub")
    rows, width = hidden_acts.shape[0], w_down.shape[0]
    at = jnp.stack([t, c]).astype(jnp.int32)
    tokens = rows * lax.axis_size("fsdp") * lax.axis_size("sub")
    order = Order()
    go, seen = order.go, order.seen

    def own_units(k):
        return lax.dynamic_slice_in_dim(hidden_acts, (z ^ k) * width, width, 1)

    c0 = cotangent
    c2 = swap(c0, "fsdp", 2, "c2")
    x0 = swap(c0, "tp", 1, "x0")
    half = swap(halves(projector, 0, c)[0], "tp", 1, "half")
    c1 = swap(c0, "fsdp", 1, "c1")
    h0, h1, h2, h3 = (own_units(k) for k in range(4))
    h1 = swap(h1, "fsdp", 1, "h1")
    p0, m0 = forward(at, h0, w_down)
    seen(p0, c2, half, c1)
    x2 = swap(go(c2), "tp", 1, "x2")
    h3 = swap(go(h3), "fsdp", 3, "h3")
    c3 = swap(go(c2), "fsdp", 1, "c3")
    basis = swap(go(half), "sub", 1, "basis")
    seen(p0, c1, x0, basis)
    g0, k0 = backward(at, go(c0), x0, w_down, projector, half, basis)
    seen(g0)
    x1 = swap(go(c1), "tp", 1, "x1")
    seen(g0, h1)
    p1, m1 = forward(at, go(h1), w_down)
    seen(p1)
    h2 = swap(go(h2), "fsdp", 2, "h2")
    seen(p1, x2)
    g2, k2 = backward(at, go(c2), x2, w_down, projector, half, basis)
    seen(g2, h3)
    p3, m3 = forward(at, go(h3), w_down)
    seen(p3, c3)
    x3 = swap(go(c3), "tp", 1, "x3")
    seen(p3, c3, x1)
    g1, k1 = backward(at, go(c1), x1, w_down, projector, half, basis)
    a1 = swap(g1, "fsdp", 1, "a1")
    seen(g1, h2)
    y3 = swap(go(p3), "tp", 1, "y3")
    a2 = swap(go(g2), "fsdp", 2, "a2")
    seen(g1, h2)
    p2, m2 = forward(at, go(h2), w_down)
    seen(p2, x3)
    y2 = swap(go(p2), "tp", 1, "y2")
    g3, k3 = backward(at, go(c3), x3, w_down, projector, half, basis)
    a3 = swap(g3, "fsdp", 3, "a3")
    seen(g3, y3, a2, a1)
    o3 = (go(m3) + y3.astype(f32)).astype(bf16)
    r3 = swap(o3, "fsdp", 1, "r3")
    y1 = swap(go(p1), "tp", 1, "y1")
    seen(o3)
    local = project(at, (h0, h1, h2, h3), (go(k0), k1, k2, k3))
    other = [swap(v, "sub", 1, "rows") for v in local]
    seen(local[0], y2, r3, a3)
    o2 = (go(m2) + y2.astype(f32) + r3.astype(f32)).astype(bf16)
    r2 = swap(o2, "fsdp", 2, "r2")
    y0 = swap(go(p0), "tp", 1, "y0")
    by_owner = jnp.stack([go(g0), a1, a2, a3])
    acts_grad = jnp.concatenate(
        [lax.dynamic_index_in_dim(by_owner, z ^ j, 0, keepdims=False) for j in range(4)], axis=0
    ).T
    seen(o2, acts_grad, y1)
    o1 = (go(m1) + y1.astype(f32)).astype(bf16)
    r1 = swap(o1, "fsdp", 1, "r1")
    seen(o1)
    weight_step, new_first, new_second = adam_step(
        at, local, (go(other[0]), other[1]), tokens, first_moment, second_moment, projector, half, basis
    )
    seen(weight_step)
    block_out = (
        go(m0) + y0.astype(f32) + r1.astype(f32) + r2.astype(f32)
    ).astype(bf16)
    return (block_out, acts_grad, weight_step, new_first, new_second)


def solution(mesh):
    in_specs = (
        P(("groups", "fsdp", "sub"), "tp"),
        P(("groups", "fsdp", "sub"), "tp"),
        P(("tp", "fsdp"), None),
        P("tp", None),
        P(("groups", "tp", "fsdp"), None),
        P(("groups", "tp", "fsdp"), None),
    )
    out_specs = (
        P(("groups", "fsdp", "sub"), "tp"),
        P(("groups", "fsdp", "sub"), "tp"),
        P(("groups", "tp", "fsdp"), None),
        P(("groups", "tp", "fsdp"), None),
        P(("groups", "tp", "fsdp"), None),
    )
    line = mesh.shape["fsdp"] == 4 and mesh.shape["tp"] == 2
    shards = shards_line if line else shards_any
    return jax.shard_map(shards, mesh=mesh, in_specs=in_specs, out_specs=out_specs, check_vma=False)
```

profile of v0, /device:TPU:0, one launch (start us, length us, event | category | flops | bytes accessed | tf_op | source)
XLA Modules:
  0.0 149.9 jit_solution(7998936322846283410)
XLA Ops:
  0.6 1.9 %constant_dynamic-slice_fusion.1 = bf16[1024,256]{1,0:T(8,128)(2,1)} fusion(bf16[2048,256]{1,0:T(8,128)(2,1)} %basis.9, s32[]{:T(128)S(6)} %select_n.31), kind=kLoop, calls=%fused_computation.11 | loop fusion | bytes 1048580 | tf_op jit(solution)/shard_map/dynamic_slice | solution.py:46
  2.5 2.9 %collective-permute-start.3 = (bf16[1024,256]{1,0:T(8,128)(2,1)}, bf16[1024,256]{1,0:T(8,128)(2,1)S(1)}, u32[]{:S(2)}, u32[]{:S(2)}) collective-permute-start(bf16[1024,256]{1,0:T(8,128)(2,1)} %constant_dynamic-slice_fusion.1), channel_id=1, source_target_pairs={{0,2},{2,0},{1,3},{3,1},{4,6},{6,4},{5,7},{7,5},{8,10},{10,8},{9,1... | collective-permute-start | bytes 1572872 | tf_op jit(solution)/shard_map/half/ppermute | solution.py:21
  5.4 1.6 %collective-permute-start.1 = (bf16[128,2048]{1,0:T(8,128)(2,1)}, bf16[128,2048]{1,0:T(8,128)(2,1)}, u32[]{:S(2)}, u32[]{:S(2)}) collective-permute-start(bf16[128,2048]{1,0:T(8,128)(2,1)} %c), channel_id=1, source_target_pairs={{0,4},{4,0},{8,12},{12,8},{1,5},{5,1},{9,13},{13,9},{2,6},{6,2},{1... | collective-permute-start | bytes 1572872 | tf_op jit(solution)/shard_map/c1/ppermute | solution.py:21
  7.0 2.6 %collective-permute-start.4 = (bf16[128,2048]{1,0:T(8,128)(2,1)}, bf16[128,2048]{1,0:T(8,128)(2,1)}, u32[]{:S(2)}, u32[]{:S(2)}) collective-permute-start(bf16[128,2048]{1,0:T(8,128)(2,1)} %c), channel_id=1, source_target_pairs={{0,8},{4,12},{8,0},{12,4},{1,9},{5,13},{9,1},{13,5},{2,10},{6,14},... | collective-permute-start | bytes 1572872 | tf_op jit(solution)/shard_map/c2/ppermute | solution.py:21
  9.6 0.5 collective-permute-start.2
  10.1 0.1 pad_add_fusion.at
  10.2 2.2 %constant_dynamic-slice_fusion.2 = (bf16[128,1376]{1,0:T(8,128)(2,1)S(1)}, bf16[128,1376]{1,0:T(8,128)(2,1)S(1)}, bf16[128,1376]{1,0:T(8,128)(2,1)S(1)}, bf16[128,1376]{1,0:T(8,128)(2,1)S(1)}) fusion(bf16[128,5504]{1,0:T(8,128)(2,1)} %param.6, s32[]{:T(128)S(6)} %select_n.30, s32[]{:T(128)S(6)} %select_n.29, s32[]{:T(128)S(6)} %select_n.28, s32[]{:T(128)S(6)} %select_n.32), kind=kLoop, calls=%fused_computation.12 | loop fusion | bytes 2818064 | tf_op jit(solution)/shard_map/dynamic_slice | solution.py:275
  12.5 0.0 copy-start
  12.5 4.2 %copy-done = bf16[1376,4096]{1,0:T(8,128)(2,1)S(1)} copy-done((bf16[1376,4096]{1,0:T(8,128)(2,1)S(1)}, bf16[1376,4096]{1,0:T(8,128)(2,1)}, u32[]{:S(2)}) %copy-start) | copy-done | bytes 11272216
  16.7 2.4 %forward.4 = (bf16[128,2048]{1,0:T(8,128)(2,1)}, f32[128,2048]{1,0:T(8,128)S(1)}) custom-call(s32[2]{0:T(128)S(1)} %pad_add_fusion.at, bf16[128,1376]{1,0:T(8,128)(2,1)S(1)} %get-tuple-element.108.h.refs_0_, bf16[1376,4096]{1,0:T(8,128)(2,1)S(1)} %copy-done), custom_call_target="tpu_custom_call" | custom-call | flops 1 | bytes 1 | tf_op jit(solution)/shard_map/forward/pallas_call | solution.py:134
  19.1 11.2 %collective-permute-done.1.c = bf16[128,2048]{1,0:T(8,128)(2,1)} collective-permute-done((bf16[128,2048]{1,0:T(8,128)(2,1)}, bf16[128,2048]{1,0:T(8,128)(2,1)}, u32[]{:S(2)}, u32[]{:S(2)}) %collective-permute-start.1) | collective-permute-done | bytes 524320 | tf_op jit(solution)/shard_map/c1/ppermute | solution.py:21
  30.3 2.4 %collective-permute-done.4.c = bf16[128,2048]{1,0:T(8,128)(2,1)} collective-permute-done((bf16[128,2048]{1,0:T(8,128)(2,1)}, bf16[128,2048]{1,0:T(8,128)(2,1)}, u32[]{:S(2)}, u32[]{:S(2)}) %collective-permute-start.4) | collective-permute-done | bytes 524320 | tf_op jit(solution)/shard_map/c2/ppermute | solution.py:21
  32.6 0.4 collective-permute-start
  33.1 0.5 collective-permute-start.8
  33.6 1.6 %collective-permute-start.9 = (bf16[128,2048]{1,0:T(8,128)(2,1)}, bf16[128,2048]{1,0:T(8,128)(2,1)S(1)}, u32[]{:S(2)}, u32[]{:S(2)}) collective-permute-start(bf16[128,2048]{1,0:T(8,128)(2,1)} %collective-permute-done.4.c), channel_id=1, source_target_pairs={{0,4},{4,0},{8,12},{12,8},{1,5},{5,1},{9,13},{13,9},{2,6},{6,2},{1... | collective-permute-start | bytes 1572872 | tf_op jit(solution)/shard_map/c3/ppermute | solution.py:21
  35.2 3.9 %backward.4 = (bf16[1376,128]{1,0:T(8,128)(2,1)S(1)}, bf16[128,256]{1,0:T(8,128)(2,1)S(1)}) custom-call(s32[2]{0:T(128)S(1)} %pad_add_fusion.at, bf16[128,2048]{1,0:T(8,128)(2,1)S(1)} %copy-done.10, bf16[128,2048]{1,0:T(8,128)(2,1)S(1)} %collective-permute-done.2.x, bf16[1376,4096]{1,0:T(8,128)(2,1)S(1)} %copy-done, bf16[2048,256]{1,0:T(8,128)(2,1)S(1)} %copy-done.1, ...), custom_call_target="tpu_custom_call" | custom-call | flops 1 | bytes 1 | tf_op jit(solution)/shard_map/backward/pallas_call | solution.py:134
  39.1 0.7 copy-done.11
  39.9 0.6 copy-done.13
  40.5 1.5 collective-permute-start.10
  42.0 2.5 %collective-permute-start.7 = (bf16[128,1376]{1,0:T(8,128)(2,1)S(1)}, bf16[128,1376]{1,0:T(8,128)(2,1)S(1)}, u32[]{:S(2)}, u32[]{:S(2)}) collective-permute-start(bf16[128,1376]{1,0:T(8,128)(2,1)S(1)} %get-tuple-element.59), channel_id=1, source_target_pairs={{0,12},{4,8},{8,4},{12,0},{1,13},{5,9},{9,5},{13,1},{2,14},{6,10},... | collective-permute-start | bytes 1056776 | tf_op jit(solution)/shard_map/h3/ppermute | solution.py:21
  44.5 2.4 %forward.5 = (bf16[128,2048]{1,0:T(8,128)(2,1)S(1)}, f32[128,2048]{1,0:T(8,128)S(1)}) custom-call(s32[2]{0:T(128)S(1)} %pad_add_fusion.at, bf16[128,1376]{1,0:T(8,128)(2,1)S(1)} %collective-permute-done.h.refs_1_, bf16[1376,4096]{1,0:T(8,128)(2,1)S(1)} %copy-done), custom_call_target="tpu_custom_call" | custom-call | flops 1 | bytes 1 | tf_op jit(solution)/shard_map/forward/pallas_call | solution.py:134
  46.9 0.0 copy-start.21
  46.9 0.8 copy-done.21
  47.7 0.5 collective-permute-start.6
  48.1 5.0 %backward.5 = (bf16[1376,128]{1,0:T(8,128)(2,1)S(1)}, bf16[128,256]{1,0:T(8,128)(2,1)S(1)}) custom-call(s32[2]{0:T(128)S(1)} %pad_add_fusion.at, bf16[128,2048]{1,0:T(8,128)(2,1)} %collective-permute-done.4.c, bf16[128,2048]{1,0:T(8,128)(2,1)S(1)} %collective-permute-done.8.x, bf16[1376,4096]{1,0:T(8,128)(2,1)S(1)} %copy-done, ...), custom_call_target="tpu_custom_call" | custom-call | flops 1 | bytes 1 | tf_op jit(solution)/shard_map/backward/pallas_call | solution.py:134
  53.1 10.3 %collective-permute-done.7.h.refs_3_ = bf16[128,1376]{1,0:T(8,128)(2,1)S(1)} collective-permute-done((bf16[128,1376]{1,0:T(8,128)(2,1)S(1)}, bf16[128,1376]{1,0:T(8,128)(2,1)S(1)}, u32[]{:S(2)}, u32[]{:S(2)}) %collective-permute-start.7) | collective-permute-done | bytes 352288 | tf_op jit(solution)/shard_map/h3/ppermute | solution.py:21
  63.4 2.4 %forward.6 = (bf16[128,2048]{1,0:T(8,128)(2,1)S(1)}, f32[128,2048]{1,0:T(8,128)S(1)}) custom-call(s32[2]{0:T(128)S(1)} %pad_add_fusion.at, bf16[128,1376]{1,0:T(8,128)(2,1)S(1)} %collective-permute-done.7.h.refs_3_, bf16[1376,4096]{1,0:T(8,128)(2,1)S(1)} %bitcast.17), custom_call_target="tpu_custom_call" | custom-call | flops 1 | bytes 1 | tf_op jit(solution)/shard_map/forward/pallas_call | solution.py:134
  65.8 0.5 collective-permute-done.9.c
  66.3 0.5 collective-permute-start.11
  66.9 4.6 %backward.6 = (bf16[1376,128]{1,0:T(8,128)(2,1)S(1)}, bf16[128,256]{1,0:T(8,128)(2,1)S(1)}) custom-call(s32[2]{0:T(128)S(1)} %pad_add_fusion.at, bf16[128,2048]{1,0:T(8,128)(2,1)} %collective-permute-done.1.c, bf16[128,2048]{1,0:T(8,128)(2,1)S(1)} %collective-permute-done.10.x, bf16[1376,4096]{1,0:T(8,128)(2,1)S(1)} %bitcast.17, ...), custom_call_target="tpu_custom_call" | custom-call | flops 1 | bytes 1 | tf_op jit(solution)/shard_map/backward/pallas_call | solution.py:134
  71.5 3.3 %collective-permute-done.6.h.refs_2_ = bf16[128,1376]{1,0:T(8,128)(2,1)S(1)} collective-permute-done((bf16[128,1376]{1,0:T(8,128)(2,1)S(1)}, bf16[128,1376]{1,0:T(8,128)(2,1)S(1)}, u32[]{:S(2)}, u32[]{:S(2)}) %collective-permute-start.6) | collective-permute-done | bytes 352288 | tf_op jit(solution)/shard_map/h2/ppermute | solution.py:21
  74.8 0.5 collective-permute-start.12
  75.3 2.9 %collective-permute-start.14 = (bf16[1376,128]{1,0:T(8,128)(2,1)S(1)}, bf16[1376,128]{1,0:T(8,128)(2,1)S(1)}, u32[]{:S(2)}, u32[]{:S(2)}) collective-permute-start(bf16[1376,128]{1,0:T(8,128)(2,1)S(1)} %get-tuple-element.69), channel_id=1, source_target_pairs={{0,4},{4,0},{8,12},{12,8},{1,5},{5,1},{9,13},{13,9},{2,6},{6,2},{1... | collective-permute-start | bytes 1056776 | tf_op jit(solution)/shard_map/a1/ppermute | solution.py:21
  78.2 2.4 %forward.7 = (bf16[128,2048]{1,0:T(8,128)(2,1)}, f32[128,2048]{1,0:T(8,128)S(1)}) custom-call(s32[2]{0:T(128)S(1)} %pad_add_fusion.at, bf16[128,1376]{1,0:T(8,128)(2,1)S(1)} %collective-permute-done.6.h.refs_2_, bf16[1376,4096]{1,0:T(8,128)(2,1)S(1)} %bitcast.17), custom_call_target="tpu_custom_call" | custom-call | flops 1 | bytes 1 | tf_op jit(solution)/shard_map/forward/pallas_call | solution.py:134
  80.6 1.0 copy-done.8
  81.6 1.5 collective-permute-start.16
  83.1 4.6 %backward.7 = (bf16[1376,128]{1,0:T(8,128)(2,1)}, bf16[128,256]{1,0:T(8,128)(2,1)S(1)}) custom-call(s32[2]{0:T(128)S(1)} %pad_add_fusion.at, bf16[128,2048]{1,0:T(8,128)(2,1)S(1)} %collective-permute-done.9.c, bf16[128,2048]{1,0:T(8,128)(2,1)S(1)} %collective-permute-done.11.x, bf16[1376,4096]{1,0:T(8,128)(2,1)S(1)} %bitcast.17, ...), custom_call_target="tpu_custom_call" | custom-call | flops 1 | bytes 1 | tf_op jit(solution)/shard_map/backward/pallas_call | solution.py:134
  87.7 4.5 %collective-permute-done.13 = bf16[1376,128]{1,0:T(8,128)(2,1)S(1)} collective-permute-done((bf16[1376,128]{1,0:T(8,128)(2,1)S(1)}, bf16[1376,128]{1,0:T(8,128)(2,1)S(1)}, u32[]{:S(2)}, u32[]{:S(2)}) %collective-permute-start.13) | collective-permute-done | bytes 352288 | tf_op jit(solution)/shard_map/a2/ppermute | solution.py:21
  92.2 0.2 collective-permute-done.14
  92.4 0.0 collective-permute-done.12
  92.4 0.9 add_convert_fusion.3
  93.3 1.8 %collective-permute-start.18 = (bf16[1376,128]{1,0:T(8,128)(2,1)}, bf16[1376,128]{1,0:T(8,128)(2,1)}, u32[]{:S(2)}, u32[]{:S(2)}) collective-permute-start(bf16[1376,128]{1,0:T(8,128)(2,1)} %get-tuple-element.74), channel_id=1, source_target_pairs={{0,12},{4,8},{8,4},{12,0},{1,13},{5,9},{9,5},{13,1},{2,14},{6,10},... | collective-permute-start | bytes 1056776 | tf_op jit(solution)/shard_map/a3/ppermute | solution.py:21
  95.1 1.5 %collective-permute-start.19 = (bf16[128,2048]{1,0:T(8,128)(2,1)}, bf16[128,2048]{1,0:T(8,128)(2,1)S(1)}, u32[]{:S(2)}, u32[]{:S(2)}) collective-permute-start(bf16[128,2048]{1,0:T(8,128)(2,1)} %copy-done.21), channel_id=1, source_target_pairs={{0,2},{2,0},{1,3},{3,1},{4,6},{6,4},{5,7},{7,5},{8,10},{10,8},{9,1... | collective-permute-start | bytes 1572872 | tf_op jit(solution)/shard_map/y1/ppermute | solution.py:21
  96.6 0.8 copy-done.14
  97.4 0.8 copy-done.16
  98.3 0.8 copy-done.18
  99.1 0.8 copy-done.20
  99.9 2.4 %project.1 = (f32[688,256]{1,0:T(8,128)}, f32[688,256]{1,0:T(8,128)}) custom-call(s32[2]{0:T(128)S(1)} %pad_add_fusion.at, bf16[128,1376]{1,0:T(8,128)(2,1)S(1)} %get-tuple-element.108.h.refs_0_, bf16[128,1376]{1,0:T(8,128)(2,1)S(1)} %collective-permute-done.h.refs_1_, bf16[128,1376]{1,0:T(8,128)(2,1)S(1)} %collective-permute-done.6.h.refs_2_, ...), custom_call_target="tpu_custom_call" | custom-call | flops 1 | bytes 1 | tf_op jit(solution)/shard_map/project/pallas_call | solution.py:134
  102.3 0.0 collective-permute-start.20
  102.3 12.5 %collective-permute-done.18 = bf16[1376,128]{1,0:T(8,128)(2,1)} collective-permute-done((bf16[1376,128]{1,0:T(8,128)(2,1)}, bf16[1376,128]{1,0:T(8,128)(2,1)}, u32[]{:S(2)}, u32[]{:S(2)}) %collective-permute-start.18) | collective-permute-done | bytes 352288 | tf_op jit(solution)/shard_map/a3/ppermute | solution.py:21
  114.8 0.0 collective-permute-done.17
  114.9 2.2 %add_convert_fusion.2 = bf16[128,2048]{1,0:T(8,128)(2,1)} fusion(bf16[128,2048]{1,0:T(8,128)(2,1)} %collective-permute-done.17, f32[128,2048]{1,0:T(8,128)S(1)} %copy-done.9, bf16[128,2048]{1,0:T(8,128)(2,1)} %collective-permute-done.16), kind=kLoop, calls=%fused_computation.4 | loop fusion | flops 1310720 | bytes 2621440 | tf_op jit(solution)/shard_map/convert_element_type | solution.py:324
  117.1 1.2 pad_maximum_fusion
  118.2 0.1 dynamic-slice_bitcast_fusion.3
  118.4 1.2 maximum_bitcast_fusion
  119.6 0.5 copy-done.7
  120.1 0.9 add_convert_fusion.1
  121.0 2.7 %collective-permute-start.22 = (bf16[128,2048]{1,0:T(8,128)(2,1)}, bf16[128,2048]{1,0:T(8,128)(2,1)}, u32[]{:S(2)}, u32[]{:S(2)}) collective-permute-start(bf16[128,2048]{1,0:T(8,128)(2,1)} %add_convert_fusion.1), channel_id=1, source_target_pairs={{0,4},{4,0},{8,12},{12,8},{1,5},{5,1},{9,13},{13,9},{2,6},{6,2},{1... | collective-permute-start | bytes 1572872 | tf_op jit(solution)/shard_map/r1/ppermute | solution.py:21
  123.6 1.5 %collective-permute-start.21 = (bf16[128,2048]{1,0:T(8,128)(2,1)}, bf16[128,2048]{1,0:T(8,128)(2,1)}, u32[]{:S(2)}, u32[]{:S(2)}) collective-permute-start(bf16[128,2048]{1,0:T(8,128)(2,1)} %get-tuple-element.94), channel_id=1, source_target_pairs={{0,2},{2,0},{1,3},{3,1},{4,6},{6,4},{5,7},{7,5},{8,10},{10,8},{9,1... | collective-permute-start | bytes 1572872 | tf_op jit(solution)/shard_map/y0/ppermute | solution.py:21
  125.1 2.5 %copy.11 = bf16[128,5504]{1,0:T(8,128)(2,1)} copy(bf16[128,5504]{0,1:T(8,128)(2,1)} %maximum_bitcast_fusion) | data formatting | bytes 2818048
  127.7 1.3 copy-done.3
  129.0 10.9 %adam_step.1 = (f32[1376,4096]{1,0:T(8,128)}, f32[1376,256]{1,0:T(8,128)}, f32[1376,256]{1,0:T(8,128)}) custom-call(s32[2]{0:T(128)S(1)} %pad_add_fusion.at, f32[688,256]{1,0:T(8,128)} %get-tuple-element.82.h_up, f32[688,256]{1,0:T(8,128)} %get-tuple-element.83.h_low, f32[688,256]{1,0:T(8,128)} %collective-permute-done.15.t_up, ...), custom_call_target="tpu_custom_call" | custom-call | flops 1 | bytes 1 | tf_op jit(solution)/shard_map/adam_step/pallas_call | solution.py:241
  140.0 7.4 %collective-permute-done.22 = bf16[128,2048]{1,0:T(8,128)(2,1)} collective-permute-done((bf16[128,2048]{1,0:T(8,128)(2,1)}, bf16[128,2048]{1,0:T(8,128)(2,1)}, u32[]{:S(2)}, u32[]{:S(2)}) %collective-permute-start.22) | collective-permute-done | bytes 524320 | tf_op jit(solution)/shard_map/r1/ppermute | solution.py:21
  147.4 2.5 %add_convert_fusion = bf16[128,2048]{1,0:T(8,128)(2,1)} fusion(bf16[128,2048]{1,0:T(8,128)(2,1)} %collective-permute-done.23, bf16[128,2048]{1,0:T(8,128)(2,1)} %collective-permute-done.22, f32[128,2048]{1,0:T(8,128)S(1)} %copy-done.5, bf16[128,2048]{1,0:T(8,128)(2,1)} %collective-permute-done.21), kind=kLoop, calls=%fused_computation.2 | loop fusion | flops 1835008 | bytes 3145728 | tf_op jit(solution)/shard_map/convert_element_type | solution.py:341
  (64 shorter events, 0.1 us)
Async XLA Ops:
  2.5 16.6 %collective-permute-start.3 = (bf16[1024,256]{1,0:T(8,128)(2,1)}, bf16[1024,256]{1,0:T(8,128)(2,1)S(1)}, u32[]{:S(2)}, u32[]{:S(2)}) collective-permute-start(bf16[1024,256]{1,0:T(8,128)(2,1)} %constant_dynamic-slice_fusion.1), channel_id=1, source_target_pairs={{0,2},{2,0},{1,3},{3,1},{4,6},{6,4},{5,7},{7,5},{8,10},{10,8},{9,1... | collective-permute-start | bytes 1572872 | tf_op jit(solution)/shard_map/half/ppermute | solution.py:21
  5.4 24.8 %collective-permute-start.1 = (bf16[128,2048]{1,0:T(8,128)(2,1)}, bf16[128,2048]{1,0:T(8,128)(2,1)}, u32[]{:S(2)}, u32[]{:S(2)}) collective-permute-start(bf16[128,2048]{1,0:T(8,128)(2,1)} %c), channel_id=1, source_target_pairs={{0,4},{4,0},{8,12},{12,8},{1,5},{5,1},{9,13},{13,9},{2,6},{6,2},{1... | collective-permute-start | bytes 1572872 | tf_op jit(solution)/shard_map/c1/ppermute | solution.py:21
  7.0 25.6 %collective-permute-start.4 = (bf16[128,2048]{1,0:T(8,128)(2,1)}, bf16[128,2048]{1,0:T(8,128)(2,1)}, u32[]{:S(2)}, u32[]{:S(2)}) collective-permute-start(bf16[128,2048]{1,0:T(8,128)(2,1)} %c), channel_id=1, source_target_pairs={{0,8},{4,12},{8,0},{12,4},{1,9},{5,13},{9,1},{13,5},{2,10},{6,14},... | collective-permute-start | bytes 1572872 | tf_op jit(solution)/shard_map/c2/ppermute | solution.py:21
  9.6 25.6 %collective-permute-start.2 = (bf16[128,2048]{1,0:T(8,128)(2,1)}, bf16[128,2048]{1,0:T(8,128)(2,1)S(1)}, u32[]{:S(2)}, u32[]{:S(2)}) collective-permute-start(bf16[128,2048]{1,0:T(8,128)(2,1)} %c), channel_id=1, source_target_pairs={{0,2},{2,0},{1,3},{3,1},{4,6},{6,4},{5,7},{7,5},{8,10},{10,8},{9,1... | collective-permute-start | bytes 1572872 | tf_op jit(solution)/shard_map/x0/ppermute | solution.py:21
  12.5 4.2 %copy-start = (bf16[1376,4096]{1,0:T(8,128)(2,1)S(1)}, bf16[1376,4096]{1,0:T(8,128)(2,1)}, u32[]{:S(2)}) copy-start(bf16[1376,4096]{1,0:T(8,128)(2,1)} %w.15) | copy-start | bytes 33816580
  16.7 18.5 %copy-start.1 = (bf16[2048,256]{1,0:T(8,128)(2,1)S(1)}, bf16[2048,256]{1,0:T(8,128)(2,1)}, u32[]{:S(2)}) copy-start(bf16[2048,256]{1,0:T(8,128)(2,1)} %basis.9) | copy-start | bytes 3145732
  16.7 18.5 %copy-start.10 = (bf16[128,2048]{1,0:T(8,128)(2,1)S(1)}, bf16[128,2048]{1,0:T(8,128)(2,1)}, u32[]{:S(2)}) copy-start(bf16[128,2048]{1,0:T(8,128)(2,1)} %c) | copy-start | bytes 1572868
  19.1 20.1 %copy-start.4 = (f32[128,2048]{1,0:T(8,128)}, f32[128,2048]{1,0:T(8,128)S(1)}, u32[]{:S(2)}) copy-start(f32[128,2048]{1,0:T(8,128)S(1)} %get-tuple-element.93) | copy-start | bytes 3145732
  32.6 2.6 %collective-permute-start.5 = (bf16[1024,256]{1,0:T(8,128)(2,1)S(1)}, bf16[1024,256]{1,0:T(8,128)(2,1)S(1)}, u32[]{:S(2)}, u32[]{:S(2)}) collective-permute-start(bf16[1024,256]{1,0:T(8,128)(2,1)S(1)} %collective-permute-done.3.got), channel_id=1, source_target_pairs={{0,1},{1,0},{2,3},{3,2},{4,5},{5,4},{6,7},{7,6},{8,9},{9,8},{10,11... | collective-permute-start | bytes 1572872 | tf_op jit(solution)/shard_map/basis/ppermute | solution.py:21
  32.6 11.8 %collective-permute-start = (bf16[128,1376]{1,0:T(8,128)(2,1)S(1)}, bf16[128,1376]{1,0:T(8,128)(2,1)S(1)}, u32[]{:S(2)}, u32[]{:S(2)}) collective-permute-start(bf16[128,1376]{1,0:T(8,128)(2,1)S(1)} %get-tuple-element.107), channel_id=1, source_target_pairs={{0,4},{4,0},{8,12},{12,8},{1,5},{5,1},{9,13},{13,9},{2,6},{6,2},{1... | collective-permute-start | bytes 1056776 | tf_op jit(solution)/shard_map/h1/ppermute | solution.py:21
  33.1 15.0 %collective-permute-start.8 = (bf16[128,2048]{1,0:T(8,128)(2,1)}, bf16[128,2048]{1,0:T(8,128)(2,1)S(1)}, u32[]{:S(2)}, u32[]{:S(2)}) collective-permute-start(bf16[128,2048]{1,0:T(8,128)(2,1)} %collective-permute-done.4.c), channel_id=1, source_target_pairs={{0,2},{2,0},{1,3},{3,1},{4,6},{6,4},{5,7},{7,5},{8,10},{10,8},{9,1... | collective-permute-start | bytes 1572872 | tf_op jit(solution)/shard_map/x2/ppermute | solution.py:21
  33.6 32.7 %collective-permute-start.9 = (bf16[128,2048]{1,0:T(8,128)(2,1)}, bf16[128,2048]{1,0:T(8,128)(2,1)S(1)}, u32[]{:S(2)}, u32[]{:S(2)}) collective-permute-start(bf16[128,2048]{1,0:T(8,128)(2,1)} %collective-permute-done.4.c), channel_id=1, source_target_pairs={{0,4},{4,0},{8,12},{12,8},{1,5},{5,1},{9,13},{13,9},{2,6},{6,2},{1... | collective-permute-start | bytes 1572872 | tf_op jit(solution)/shard_map/c3/ppermute | solution.py:21
  39.1 0.7 copy-start.11
  39.9 0.6 copy-start.13
  40.5 26.3 %collective-permute-start.10 = (bf16[128,2048]{1,0:T(8,128)(2,1)}, bf16[128,2048]{1,0:T(8,128)(2,1)S(1)}, u32[]{:S(2)}, u32[]{:S(2)}) collective-permute-start(bf16[128,2048]{1,0:T(8,128)(2,1)} %collective-permute-done.1.c), channel_id=1, source_target_pairs={{0,2},{2,0},{1,3},{3,1},{4,6},{6,4},{5,7},{7,5},{8,10},{10,8},{9,1... | collective-permute-start | bytes 1572872 | tf_op jit(solution)/shard_map/x1/ppermute | solution.py:21
  42.0 21.4 %collective-permute-start.7 = (bf16[128,1376]{1,0:T(8,128)(2,1)S(1)}, bf16[128,1376]{1,0:T(8,128)(2,1)S(1)}, u32[]{:S(2)}, u32[]{:S(2)}) collective-permute-start(bf16[128,1376]{1,0:T(8,128)(2,1)S(1)} %get-tuple-element.59), channel_id=1, source_target_pairs={{0,12},{4,8},{8,4},{12,0},{1,13},{5,9},{9,5},{13,1},{2,14},{6,10},... | collective-permute-start | bytes 1056776 | tf_op jit(solution)/shard_map/h3/ppermute | solution.py:21
  44.5 19.0 %slice-start = ((s8[11272192]{0:T(1024)(128)(4,1)}), s8[4194304]{0:T(1024)(128)(4,1)S(1)}, s32[]{:S(2)}) async-start(s8[11272192]{0:T(1024)(128)(4,1)} %bitcast.16), calls=%async_computation | async-start | bytes 8388608
  44.5 19.0 %slice-start.1 = ((s8[11272192]{0:T(1024)(128)(4,1)}), s8[4194304]{0:T(1024)(128)(4,1)S(1)}, s32[]{:S(2)}) async-start(s8[11272192]{0:T(1024)(128)(4,1)} %bitcast.16), calls=%async_computation.1 | async-start | bytes 8388608
  46.9 0.8 copy-start.21
  47.6 5.5 %copy-start.6 = (f32[128,2048]{1,0:T(8,128)}, f32[128,2048]{1,0:T(8,128)S(1)}, u32[]{:S(2)}) copy-start(f32[128,2048]{1,0:T(8,128)S(1)} %get-tuple-element.90) | copy-start | bytes 3145732
  47.6 15.8 %slice-start.2 = ((s8[11272192]{0:T(1024)(128)(4,1)}), s8[2883584]{0:T(1024)(128)(4,1)S(1)}, s32[]{:S(2)}) async-start(s8[11272192]{0:T(1024)(128)(4,1)} %bitcast.16), calls=%async_computation.2 | async-start | bytes 5767168
  47.7 27.1 %collective-permute-start.6 = (bf16[128,1376]{1,0:T(8,128)(2,1)S(1)}, bf16[128,1376]{1,0:T(8,128)(2,1)S(1)}, u32[]{:S(2)}, u32[]{:S(2)}) collective-permute-start(bf16[128,1376]{1,0:T(8,128)(2,1)S(1)} %get-tuple-element.58), channel_id=1, source_target_pairs={{0,8},{4,12},{8,0},{12,4},{1,9},{5,13},{9,1},{13,5},{2,10},{6,14},... | collective-permute-start | bytes 1056776 | tf_op jit(solution)/shard_map/h2/ppermute | solution.py:21
  53.1 12.7 %copy-start.15 = (bf16[128,256]{1,0:T(8,128)(2,1)}, bf16[128,256]{1,0:T(8,128)(2,1)S(1)}, u32[]{:S(2)}) copy-start(bf16[128,256]{1,0:T(8,128)(2,1)S(1)} %get-tuple-element.80.refs_6_) | copy-start | bytes 196612
  66.3 15.3 %collective-permute-start.11 = (bf16[128,2048]{1,0:T(8,128)(2,1)S(1)}, bf16[128,2048]{1,0:T(8,128)(2,1)S(1)}, u32[]{:S(2)}, u32[]{:S(2)}) collective-permute-start(bf16[128,2048]{1,0:T(8,128)(2,1)S(1)} %collective-permute-done.9.c), channel_id=1, source_target_pairs={{0,2},{2,0},{1,3},{3,1},{4,6},{6,4},{5,7},{7,5},{8,10},{10,8},{9,1... | collective-permute-start | bytes 1572872 | tf_op jit(solution)/shard_map/x3/ppermute | solution.py:21
  71.5 9.1 %copy-start.17 = (bf16[128,256]{1,0:T(8,128)(2,1)}, bf16[128,256]{1,0:T(8,128)(2,1)S(1)}, u32[]{:S(2)}) copy-start(bf16[128,256]{1,0:T(8,128)(2,1)S(1)} %get-tuple-element.79.refs_5_) | copy-start | bytes 196612
  74.8 17.6 %collective-permute-start.12 = (bf16[128,2048]{1,0:T(8,128)(2,1)S(1)}, bf16[128,2048]{1,0:T(8,128)(2,1)S(1)}, u32[]{:S(2)}, u32[]{:S(2)}) collective-permute-start(bf16[128,2048]{1,0:T(8,128)(2,1)S(1)} %get-tuple-element.75), channel_id=1, source_target_pairs={{0,2},{2,0},{1,3},{3,1},{4,6},{6,4},{5,7},{7,5},{8,10},{10,8},{9,1... | collective-permute-start | bytes 1572872 | tf_op jit(solution)/shard_map/y3/ppermute | solution.py:21
  75.3 16.9 %collective-permute-start.13 = (bf16[1376,128]{1,0:T(8,128)(2,1)S(1)}, bf16[1376,128]{1,0:T(8,128)(2,1)S(1)}, u32[]{:S(2)}, u32[]{:S(2)}) collective-permute-start(bf16[1376,128]{1,0:T(8,128)(2,1)S(1)} %get-tuple-element.76), channel_id=1, source_target_pairs={{0,8},{4,12},{8,0},{12,4},{1,9},{5,13},{9,1},{13,5},{2,10},{6,14},... | collective-permute-start | bytes 1056776 | tf_op jit(solution)/shard_map/a2/ppermute | solution.py:21
  75.3 17.0 %collective-permute-start.14 = (bf16[1376,128]{1,0:T(8,128)(2,1)S(1)}, bf16[1376,128]{1,0:T(8,128)(2,1)S(1)}, u32[]{:S(2)}, u32[]{:S(2)}) collective-permute-start(bf16[1376,128]{1,0:T(8,128)(2,1)S(1)} %get-tuple-element.69), channel_id=1, source_target_pairs={{0,4},{4,0},{8,12},{12,8},{1,5},{5,1},{9,13},{13,9},{2,6},{6,2},{1... | collective-permute-start | bytes 1056776 | tf_op jit(solution)/shard_map/a1/ppermute | solution.py:21
  80.6 1.0 copy-start.8
  81.6 33.2 %collective-permute-start.16 = (bf16[128,2048]{1,0:T(8,128)(2,1)}, bf16[128,2048]{1,0:T(8,128)(2,1)}, u32[]{:S(2)}, u32[]{:S(2)}) collective-permute-start(bf16[128,2048]{1,0:T(8,128)(2,1)} %get-tuple-element.86), channel_id=1, source_target_pairs={{0,2},{2,0},{1,3},{3,1},{4,6},{6,4},{5,7},{7,5},{8,10},{10,8},{9,1... | collective-permute-start | bytes 1572872 | tf_op jit(solution)/shard_map/y2/ppermute | solution.py:21
  87.7 5.6 %copy-start.19 = (bf16[128,256]{1,0:T(8,128)(2,1)}, bf16[128,256]{1,0:T(8,128)(2,1)S(1)}, u32[]{:S(2)}) copy-start(bf16[128,256]{1,0:T(8,128)(2,1)S(1)} %get-tuple-element.81.refs_7_) | copy-start | bytes 196612
  92.2 1.1 copy-start.22
  92.4 0.9 copy-start.24
  93.3 21.6 %collective-permute-start.17 = (bf16[128,2048]{1,0:T(8,128)(2,1)}, bf16[128,2048]{1,0:T(8,128)(2,1)}, u32[]{:S(2)}, u32[]{:S(2)}) collective-permute-start(bf16[128,2048]{1,0:T(8,128)(2,1)} %add_convert_fusion.3), channel_id=1, source_target_pairs={{0,4},{4,0},{8,12},{12,8},{1,5},{5,1},{9,13},{13,9},{2,6},{6,2},{1... | collective-permute-start | bytes 1572872 | tf_op jit(solution)/shard_map/r3/ppermute | solution.py:21
  93.3 21.5 %collective-permute-start.18 = (bf16[1376,128]{1,0:T(8,128)(2,1)}, bf16[1376,128]{1,0:T(8,128)(2,1)}, u32[]{:S(2)}, u32[]{:S(2)}) collective-permute-start(bf16[1376,128]{1,0:T(8,128)(2,1)} %get-tuple-element.74), channel_id=1, source_target_pairs={{0,12},{4,8},{8,4},{12,0},{1,13},{5,9},{9,5},{13,1},{2,14},{6,10},... | collective-permute-start | bytes 1056776 | tf_op jit(solution)/shard_map/a3/ppermute | solution.py:21
  95.1 19.8 %copy-start.9 = (f32[128,2048]{1,0:T(8,128)S(1)}, f32[128,2048]{1,0:T(8,128)}, u32[]{:S(2)}) copy-start(f32[128,2048]{1,0:T(8,128)} %copy-done.8) | copy-start | bytes 3145732
  95.1 24.5 %collective-permute-start.19 = (bf16[128,2048]{1,0:T(8,128)(2,1)}, bf16[128,2048]{1,0:T(8,128)(2,1)S(1)}, u32[]{:S(2)}, u32[]{:S(2)}) collective-permute-start(bf16[128,2048]{1,0:T(8,128)(2,1)} %copy-done.21), channel_id=1, source_target_pairs={{0,2},{2,0},{1,3},{3,1},{4,6},{6,4},{5,7},{7,5},{8,10},{10,8},{9,1... | collective-permute-start | bytes 1572872 | tf_op jit(solution)/shard_map/y1/ppermute | solution.py:21
  96.6 0.8 copy-start.14
  97.4 0.8 copy-start.16
  98.3 0.8 copy-start.18
  99.1 0.8 copy-start.20
  102.3 14.8 %copy-start.12 = (bf16[1376,128]{1,0:T(8,128)(2,1)S(1)}, bf16[1376,128]{1,0:T(8,128)(2,1)}, u32[]{:S(2)}) copy-start(bf16[1376,128]{1,0:T(8,128)(2,1)} %copy-done.11) | copy-start | bytes 1056772
  102.3 14.8 %copy-start.23 = (bf16[1376,128]{1,0:T(8,128)(2,1)S(1)}, bf16[1376,128]{1,0:T(8,128)(2,1)}, u32[]{:S(2)}) copy-start(bf16[1376,128]{1,0:T(8,128)(2,1)} %copy-done.22) | copy-start | bytes 1056772
  102.3 14.8 %copy-start.25 = (bf16[1376,128]{1,0:T(8,128)(2,1)S(1)}, bf16[1376,128]{1,0:T(8,128)(2,1)}, u32[]{:S(2)}) copy-start(bf16[1376,128]{1,0:T(8,128)(2,1)} %copy-done.24) | copy-start | bytes 1056772
  102.3 25.3 %collective-permute-start.20 = (f32[688,256]{1,0:T(8,128)}, f32[688,256]{1,0:T(8,128)}, u32[]{:S(2)}, u32[]{:S(2)}) collective-permute-start(f32[688,256]{1,0:T(8,128)} %get-tuple-element.83.h_low), channel_id=1, source_target_pairs={{0,1},{1,0},{2,3},{3,2},{4,5},{5,4},{6,7},{7,6},{8,9},{9,8},{10,11... | collective-permute-start | bytes 2113544 | tf_op jit(solution)/shard_map/rows/ppermute | solution.py:21
  114.8 12.8 %collective-permute-start.15 = (f32[688,256]{1,0:T(8,128)}, f32[688,256]{1,0:T(8,128)}, u32[]{:S(2)}, u32[]{:S(2)}) collective-permute-start(f32[688,256]{1,0:T(8,128)} %get-tuple-element.82.h_up), channel_id=1, source_target_pairs={{0,1},{1,0},{2,3},{3,2},{4,5},{5,4},{6,7},{7,6},{8,9},{9,8},{10,11... | collective-permute-start | bytes 2113544 | tf_op jit(solution)/shard_map/rows/ppermute | solution.py:21
  117.1 30.3 %collective-permute-start.23 = (bf16[128,2048]{1,0:T(8,128)(2,1)}, bf16[128,2048]{1,0:T(8,128)(2,1)}, u32[]{:S(2)}, u32[]{:S(2)}) collective-permute-start(bf16[128,2048]{1,0:T(8,128)(2,1)} %add_convert_fusion.2), channel_id=1, source_target_pairs={{0,8},{4,12},{8,0},{12,4},{1,9},{5,13},{9,1},{13,5},{2,10},{6,14},... | collective-permute-start | bytes 1572872 | tf_op jit(solution)/shard_map/r2/ppermute | solution.py:21
  118.4 1.7 %copy-start.7 = (f32[128,2048]{1,0:T(8,128)S(1)}, f32[128,2048]{1,0:T(8,128)}, u32[]{:S(2)}) copy-start(f32[128,2048]{1,0:T(8,128)} %copy-done.6) | copy-start | bytes 3145732
  121.0 6.7 %copy-start.2 = (f32[1376,256]{1,0:T(8,128)S(1)}, f32[1376,256]{1,0:T(8,128)}, u32[]{:S(2)}) copy-start(f32[1376,256]{1,0:T(8,128)} %first.1) | copy-start | bytes 4227076
  121.0 26.4 %collective-permute-start.22 = (bf16[128,2048]{1,0:T(8,128)(2,1)}, bf16[128,2048]{1,0:T(8,128)(2,1)}, u32[]{:S(2)}, u32[]{:S(2)}) collective-permute-start(bf16[128,2048]{1,0:T(8,128)(2,1)} %add_convert_fusion.1), channel_id=1, source_target_pairs={{0,4},{4,0},{8,12},{12,8},{1,5},{5,1},{9,13},{13,9},{2,6},{6,2},{1... | collective-permute-start | bytes 1572872 | tf_op jit(solution)/shard_map/r1/ppermute | solution.py:21
  123.6 23.8 %collective-permute-start.21 = (bf16[128,2048]{1,0:T(8,128)(2,1)}, bf16[128,2048]{1,0:T(8,128)(2,1)}, u32[]{:S(2)}, u32[]{:S(2)}) collective-permute-start(bf16[128,2048]{1,0:T(8,128)(2,1)} %get-tuple-element.94), channel_id=1, source_target_pairs={{0,2},{2,0},{1,3},{3,1},{4,6},{6,4},{5,7},{7,5},{8,10},{10,8},{9,1... | collective-permute-start | bytes 1572872 | tf_op jit(solution)/shard_map/y0/ppermute | solution.py:21
  127.7 1.4 copy-start.3
  129.0 18.4 %copy-start.5 = (f32[128,2048]{1,0:T(8,128)S(1)}, f32[128,2048]{1,0:T(8,128)}, u32[]{:S(2)}) copy-start(f32[128,2048]{1,0:T(8,128)} %copy-done.4) | copy-start | bytes 3145732
where the time goes:
time: 151 us; the launch traced here: 150 us
  waiting for transfers between devices  52.3 us (35%)
  Pallas kernels  40.9 us (27%)
  starting transfers between devices  27.5 us (18%)
  local copies, waits for them, and re-layouts  19.4 us (13%)
  other arithmetic  8.9 us (6%)
    ppermute x24, waiting for transfers between devices, swap(): return lax.ppermute(x, axis, [(i, i ^ bit) for i in range(n)])  52.3 us
    pallas_call x9, Pallas kernels, in_vmem(): pl.pallas_call(kernel, in_specs=[pl.BlockSpec(memory_space=pltpu.SMEM)] +...  30 us
    ppermute x24, starting transfers between devices, swap(): return lax.ppermute(x, axis, [(i, i ^ bit) for i in range(n)])  27.5 us
    unnamed x59, local copies, waits for them, and re-layouts  15.1 us
    pallas_call x1, Pallas kernels, adam_step(): pl.pallas_call(kernel, grid=(4,), in_specs=[pl.BlockSpec(memory_space=plt...  10.9 us
  transfers between devices with their start and end apart: 24, of which 9 were waited for; matrix products, arithmetic and copies ran while one was open for 8% of the time, Pallas kernels for 27%

commit v1 on v0

--- a/solution.py
+++ b/solution.py
@@ -276,40 +276,38 @@
 
     c0 = cotangent
     c2 = swap(c0, "fsdp", 2, "c2")
+    c1 = swap(c0, "fsdp", 1, "c1")
     x0 = swap(c0, "tp", 1, "x0")
-    half = swap(halves(projector, 0, c)[0], "tp", 1, "half")
-    c1 = swap(c0, "fsdp", 1, "c1")
     h0, h1, h2, h3 = (own_units(k) for k in range(4))
-    h1 = swap(h1, "fsdp", 1, "h1")
+    seen(h0)
+    half = swap(halves(go(projector), 0, c)[0], "tp", 1, "half")
     p0, m0 = forward(at, h0, w_down)
-    seen(p0, c2, half, c1)
+    seen(p0, c2, half, c1, x0)
     x2 = swap(go(c2), "tp", 1, "x2")
     h3 = swap(go(h3), "fsdp", 3, "h3")
     c3 = swap(go(c2), "fsdp", 1, "c3")
     basis = swap(go(half), "sub", 1, "basis")
     seen(p0, c1, x0, basis)
+    x1 = swap(go(c1), "tp", 1, "x1")
     g0, k0 = backward(at, go(c0), x0, w_down, projector, half, basis)
-    seen(g0)
-    x1 = swap(go(c1), "tp", 1, "x1")
-    seen(g0, h1)
-    p1, m1 = forward(at, go(h1), w_down)
-    seen(p1)
-    h2 = swap(go(h2), "fsdp", 2, "h2")
-    seen(p1, x2)
+    seen(g0, x2)
     g2, k2 = backward(at, go(c2), x2, w_down, projector, half, basis)
     seen(g2, h3)
+    h2 = swap(go(h2), "fsdp", 2, "h2")
+    h1 = swap(go(h1), "fsdp", 1, "h1")
     p3, m3 = forward(at, go(h3), w_down)
     seen(p3, c3)
     x3 = swap(go(c3), "tp", 1, "x3")
     seen(p3, c3, x1)
     g1, k1 = backward(at, go(c1), x1, w_down, projector, half, basis)
-    a1 = swap(g1, "fsdp", 1, "a1")
     seen(g1, h2)
     y3 = swap(go(p3), "tp", 1, "y3")
     a2 = swap(go(g2), "fsdp", 2, "a2")
-    seen(g1, h2)
     p2, m2 = forward(at, go(h2), w_down)
-    seen(p2, x3)
+    seen(p2, h1)
+    a1 = swap(go(g1), "fsdp", 1, "a1")
+    p1, m1 = forward(at, go(h1), w_down)
+    seen(p1, x3)
     y2 = swap(go(p2), "tp", 1, "y2")
     g3, k3 = backward(at, go(c3), x3, w_down, projector, half, basis)
     a3 = swap(g3, "fsdp", 3, "a3")
@@ -320,10 +318,11 @@
     seen(o3)
     local = project(at, (h0, h1, h2, h3), (go(k0), k1, k2, k3))
     other = [swap(v, "sub", 1, "rows") for v in local]
-    seen(local[0], y2, r3, a3)
+    seen(local[0], y2, r3)
     o2 = (go(m2) + y2.astype(f32) + r3.astype(f32)).astype(bf16)
     r2 = swap(o2, "fsdp", 2, "r2")
     y0 = swap(go(p0), "tp", 1, "y0")
+    seen(o2, a3)
     by_owner = jnp.stack([go(g0), a1, a2, a3])
     acts_grad = jnp.concatenate(
         [lax.dynamic_index_in_dim(by_owner, z ^ j, 0, keepdims=False) for j in range(4)], axis=0

time: 151 us -> 140 us (0.927)
  waiting for transfers between devices: 52.3 us -> 47.3 us
  starting transfers between devices: 27.5 us -> 24.4 us
    ppermute x24, waiting for transfers between devices: 52.3 us -> 47.3 us  [swap(): return lax.ppermute(x, axis, [(i, i ^ bit) for i in range(n)])]
    ppermute x24, starting transfers between devices: 27.5 us -> 24.4 us  [swap(): return lax.ppermute(x, axis, [(i, i ^ bit) for i in range(n)])]
    unnamed x59 -> x67, local copies, waits for them, and re-layouts: 15.1 us -> 14.6 us
  transfers between devices with their start and end apart: 24 -> 24, of which waited for: 9 -> 11; matrix products, arithmetic and copies ran while one was open for 8% -> 9% of each run, Pallas kernels for 27% -> 29%
where the time goes in v1:
time: 140 us; the launch traced here: 139 us
  waiting for transfers between devices  47.3 us (34%)
  Pallas kernels  39.8 us (28%)
  starting transfers between devices  24.4 us (17%)
  local copies, waits for them, and re-layouts  18.8 us (13%)
  other arithmetic  7.92 us (6%)
    ppermute x24, waiting for transfers between devices, swap(): return lax.ppermute(x, axis, [(i, i ^ bit) for i in range(n)])  47.3 us
    pallas_call x9, Pallas kernels, in_vmem(): pl.pallas_call(kernel, in_specs=[pl.BlockSpec(memory_space=pltpu.SMEM)] +...  28.8 us
    ppermute x24, starting transfers between devices, swap(): return lax.ppermute(x, axis, [(i, i ^ bit) for i in range(n)])  24.4 us
    unnamed x67, local copies, waits for them, and re-layouts  14.6 us
    pallas_call x1, Pallas kernels, adam_step(): pl.pallas_call(kernel, grid=(4,), in_specs=[pl.BlockSpec(memory_space=plt...  11 us
    dynamic_slice x1, local copies, waits for them, and re-layouts, own_units(): return lax.dynamic_slice_in_dim(hidden_acts, (z ^ k) * width, width, 1)  3.25 us
  transfers between devices with their start and end apart: 24, of which 11 were waited for; matrix products, arithmetic and copies ran while one was open for 9% of the time, Pallas kernels for 29%

profile of v1, /device:TPU:0, one launch (start us, length us, event | category | flops | bytes accessed | tf_op | source)
XLA Modules:
  0.0 139.1 jit_solution(496735766684067260)
XLA Ops:
  0.6 3.1 %collective-permute-start.1 = (bf16[128,2048]{1,0:T(8,128)(2,1)}, bf16[128,2048]{1,0:T(8,128)(2,1)}, u32[]{:S(2)}, u32[]{:S(2)}) collective-permute-start(bf16[128,2048]{1,0:T(8,128)(2,1)} %c), channel_id=1, source_target_pairs={{0,4},{4,0},{8,12},{12,8},{1,5},{5,1},{9,13},{13,9},{2,6},{6,2},{1... | collective-permute-start | bytes 1572872 | tf_op jit(solution)/shard_map/c1/ppermute | solution.py:21
  3.7 2.6 %collective-permute-start = (bf16[128,2048]{1,0:T(8,128)(2,1)}, bf16[128,2048]{1,0:T(8,128)(2,1)}, u32[]{:S(2)}, u32[]{:S(2)}) collective-permute-start(bf16[128,2048]{1,0:T(8,128)(2,1)} %c), channel_id=1, source_target_pairs={{0,8},{4,12},{8,0},{12,4},{1,9},{5,13},{9,1},{13,5},{2,10},{6,14},... | collective-permute-start | bytes 1572872 | tf_op jit(solution)/shard_map/c2/ppermute | solution.py:21
  6.3 1.5 %collective-permute-start.2 = (bf16[128,2048]{1,0:T(8,128)(2,1)}, bf16[128,2048]{1,0:T(8,128)(2,1)S(1)}, u32[]{:S(2)}, u32[]{:S(2)}) collective-permute-start(bf16[128,2048]{1,0:T(8,128)(2,1)} %c), channel_id=1, source_target_pairs={{0,2},{2,0},{1,3},{3,1},{4,6},{6,4},{5,7},{7,5},{8,10},{10,8},{9,1... | collective-permute-start | bytes 1572872 | tf_op jit(solution)/shard_map/x0/ppermute | solution.py:21
  7.8 3.2 %constant_dynamic-slice_fusion = (bf16[128,1376]{1,0:T(8,128)(2,1)}, bf16[128,1376]{1,0:T(8,128)(2,1)}, bf16[128,1376]{1,0:T(8,128)(2,1)S(1)}, bf16[128,1376]{1,0:T(8,128)(2,1)}) fusion(bf16[128,5504]{1,0:T(8,128)(2,1)} %param.6, s32[]{:T(128)S(6)} %select_n.32, s32[]{:T(128)S(6)} %select_n.29, s32[]{:T(128)S(6)} %select_n.28, s32[]{:T(128)S(6)} %select_n.31), kind=kLoop, calls=%fused_computation.10 | loop fusion | bytes 2818064 | tf_op jit(solution)/shard_map/dynamic_slice | solution.py:275
  11.1 0.8 constant_dynamic-slice_fusion.2
  11.9 0.5 collective-permute-start.3
  12.4 0.1 pad_add_fusion.at
  12.5 4.2 %copy-done = bf16[1376,4096]{1,0:T(8,128)(2,1)S(1)} copy-done((bf16[1376,4096]{1,0:T(8,128)(2,1)S(1)}, bf16[1376,4096]{1,0:T(8,128)(2,1)}, u32[]{:S(2)}) %copy-start) | copy-done | bytes 11272216
  16.7 2.4 %forward.4 = (bf16[128,2048]{1,0:T(8,128)(2,1)}, f32[128,2048]{1,0:T(8,128)S(1)}) custom-call(s32[2]{0:T(128)S(1)} %pad_add_fusion.at, bf16[128,1376]{1,0:T(8,128)(2,1)S(1)} %get-tuple-element.114.h.refs_0_, bf16[1376,4096]{1,0:T(8,128)(2,1)S(1)} %copy-done), custom_call_target="tpu_custom_call" | custom-call | flops 1 | bytes 1 | tf_op jit(solution)/shard_map/forward/pallas_call | solution.py:134
  19.1 8.0 %collective-permute-done.1.c = bf16[128,2048]{1,0:T(8,128)(2,1)} collective-permute-done((bf16[128,2048]{1,0:T(8,128)(2,1)}, bf16[128,2048]{1,0:T(8,128)(2,1)}, u32[]{:S(2)}, u32[]{:S(2)}) %collective-permute-start.1) | collective-permute-done | bytes 524320 | tf_op jit(solution)/shard_map/c1/ppermute | solution.py:21
  27.1 2.5 %collective-permute-done.c = bf16[128,2048]{1,0:T(8,128)(2,1)} collective-permute-done((bf16[128,2048]{1,0:T(8,128)(2,1)}, bf16[128,2048]{1,0:T(8,128)(2,1)}, u32[]{:S(2)}, u32[]{:S(2)}) %collective-permute-start) | collective-permute-done | bytes 524320 | tf_op jit(solution)/shard_map/c2/ppermute | solution.py:21
  29.6 1.2 collective-permute-done.3.got
  30.9 1.5 %collective-permute-start.5 = (bf16[128,2048]{1,0:T(8,128)(2,1)}, bf16[128,2048]{1,0:T(8,128)(2,1)S(1)}, u32[]{:S(2)}, u32[]{:S(2)}) collective-permute-start(bf16[128,2048]{1,0:T(8,128)(2,1)} %collective-permute-done.c), channel_id=1, source_target_pairs={{0,2},{2,0},{1,3},{3,1},{4,6},{6,4},{5,7},{7,5},{8,10},{10,8},{9,1... | collective-permute-start | bytes 1572872 | tf_op jit(solution)/shard_map/x2/ppermute | solution.py:21
  32.4 1.3 collective-permute-start.6
  33.7 0.6 collective-permute-start.10
  34.3 3.9 %backward.4 = (bf16[1376,128]{1,0:T(8,128)(2,1)S(1)}, bf16[128,256]{1,0:T(8,128)(2,1)S(1)}) custom-call(s32[2]{0:T(128)S(1)} %pad_add_fusion.at, bf16[128,2048]{1,0:T(8,128)(2,1)S(1)} %copy-done.10, bf16[128,2048]{1,0:T(8,128)(2,1)S(1)} %collective-permute-done.2.x, bf16[1376,4096]{1,0:T(8,128)(2,1)S(1)} %copy-done, bf16[2048,256]{1,0:T(8,128)(2,1)S(1)} %copy-done.1, ...), custom_call_target="tpu_custom_call" | custom-call | flops 1 | bytes 1 | tf_op jit(solution)/shard_map/backward/pallas_call | solution.py:134
  38.2 0.6 copy-done.13
  38.8 7.0 %collective-permute-done.5.x = bf16[128,2048]{1,0:T(8,128)(2,1)S(1)} collective-permute-done((bf16[128,2048]{1,0:T(8,128)(2,1)}, bf16[128,2048]{1,0:T(8,128)(2,1)S(1)}, u32[]{:S(2)}, u32[]{:S(2)}) %collective-permute-start.5) | collective-permute-done | bytes 524320 | tf_op jit(solution)/shard_map/x2/ppermute | solution.py:21
  45.8 4.6 %backward.5 = (bf16[1376,128]{1,0:T(8,128)(2,1)S(1)}, bf16[128,256]{1,0:T(8,128)(2,1)S(1)}) custom-call(s32[2]{0:T(128)S(1)} %pad_add_fusion.at, bf16[128,2048]{1,0:T(8,128)(2,1)} %collective-permute-done.c, bf16[128,2048]{1,0:T(8,128)(2,1)S(1)} %collective-permute-done.5.x, bf16[1376,4096]{1,0:T(8,128)(2,1)S(1)} %copy-done, ...), custom_call_target="tpu_custom_call" | custom-call | flops 1 | bytes 1 | tf_op jit(solution)/shard_map/backward/pallas_call | solution.py:134
  50.4 0.6 collective-permute-start.8
  51.0 1.4 collective-permute-start.7
  52.4 2.4 %forward.5 = (bf16[128,2048]{1,0:T(8,128)(2,1)S(1)}, f32[128,2048]{1,0:T(8,128)S(1)}) custom-call(s32[2]{0:T(128)S(1)} %pad_add_fusion.at, bf16[128,1376]{1,0:T(8,128)(2,1)S(1)} %collective-permute-done.6.h.refs_3_, bf16[1376,4096]{1,0:T(8,128)(2,1)S(1)} %bitcast.17), custom_call_target="tpu_custom_call" | custom-call | flops 1 | bytes 1 | tf_op jit(solution)/shard_map/forward/pallas_call | solution.py:134
  54.7 4.1 %collective-permute-done.9.c = bf16[128,2048]{1,0:T(8,128)(2,1)S(1)} collective-permute-done((bf16[128,2048]{1,0:T(8,128)(2,1)}, bf16[128,2048]{1,0:T(8,128)(2,1)S(1)}, u32[]{:S(2)}, u32[]{:S(2)}) %collective-permute-start.9) | collective-permute-done | bytes 524320 | tf_op jit(solution)/shard_map/c3/ppermute | solution.py:21
  58.8 4.4 %backward.6 = (bf16[1376,128]{1,0:T(8,128)(2,1)S(1)}, bf16[128,256]{1,0:T(8,128)(2,1)S(1)}) custom-call(s32[2]{0:T(128)S(1)} %pad_add_fusion.at, bf16[128,2048]{1,0:T(8,128)(2,1)} %collective-permute-done.1.c, bf16[128,2048]{1,0:T(8,128)(2,1)S(1)} %collective-permute-done.10.x, bf16[1376,4096]{1,0:T(8,128)(2,1)S(1)} %bitcast.17, ...), custom_call_target="tpu_custom_call" | custom-call | flops 1 | bytes 1 | tf_op jit(solution)/shard_map/backward/pallas_call | solution.py:134
  63.3 5.7 %collective-permute-done.8.h.refs_2_ = bf16[128,1376]{1,0:T(8,128)(2,1)S(1)} collective-permute-done((bf16[128,1376]{1,0:T(8,128)(2,1)S(1)}, bf16[128,1376]{1,0:T(8,128)(2,1)S(1)}, u32[]{:S(2)}, u32[]{:S(2)}) %collective-permute-start.8) | collective-permute-done | bytes 352288 | tf_op jit(solution)/shard_map/h2/ppermute | solution.py:21
  68.9 1.5 %collective-permute-start.12 = (bf16[128,2048]{1,0:T(8,128)(2,1)S(1)}, bf16[128,2048]{1,0:T(8,128)(2,1)S(1)}, u32[]{:S(2)}, u32[]{:S(2)}) collective-permute-start(bf16[128,2048]{1,0:T(8,128)(2,1)S(1)} %get-tuple-element.80), channel_id=1, source_target_pairs={{0,2},{2,0},{1,3},{3,1},{4,6},{6,4},{5,7},{7,5},{8,10},{10,8},{9,1... | collective-permute-start | bytes 1572872 | tf_op jit(solution)/shard_map/y3/ppermute | solution.py:21
  70.4 2.5 %forward.6 = (bf16[128,2048]{1,0:T(8,128)(2,1)}, f32[128,2048]{1,0:T(8,128)S(1)}) custom-call(s32[2]{0:T(128)S(1)} %pad_add_fusion.at, bf16[128,1376]{1,0:T(8,128)(2,1)S(1)} %collective-permute-done.8.h.refs_2_, bf16[1376,4096]{1,0:T(8,128)(2,1)S(1)} %bitcast.17), custom_call_target="tpu_custom_call" | custom-call | flops 1 | bytes 1 | tf_op jit(solution)/shard_map/forward/pallas_call | solution.py:134
  73.0 0.0 copy-start.8
  73.0 1.0 copy-done.8
  73.9 1.7 %collective-permute-start.14 = (bf16[1376,128]{1,0:T(8,128)(2,1)S(1)}, bf16[1376,128]{1,0:T(8,128)(2,1)S(1)}, u32[]{:S(2)}, u32[]{:S(2)}) collective-permute-start(bf16[1376,128]{1,0:T(8,128)(2,1)S(1)} %get-tuple-element.82), channel_id=1, source_target_pairs={{0,4},{4,0},{8,12},{12,8},{1,5},{5,1},{9,13},{13,9},{2,6},{6,2},{1... | collective-permute-start | bytes 1056776 | tf_op jit(solution)/shard_map/a1/ppermute | solution.py:21
  75.6 2.4 %forward.7 = (bf16[128,2048]{1,0:T(8,128)(2,1)S(1)}, f32[128,2048]{1,0:T(8,128)S(1)}) custom-call(s32[2]{0:T(128)S(1)} %pad_add_fusion.at, bf16[128,1376]{1,0:T(8,128)(2,1)S(1)} %collective-permute-done.7.h.refs_1_, bf16[1376,4096]{1,0:T(8,128)(2,1)S(1)} %bitcast.17), custom_call_target="tpu_custom_call" | custom-call | flops 1 | bytes 1 | tf_op jit(solution)/shard_map/forward/pallas_call | solution.py:134
  78.0 0.0 copy-start.6
  78.0 1.0 copy-done.6
  79.0 0.5 collective-permute-start.16
  79.5 3.9 %backward.7 = (bf16[1376,128]{1,0:T(8,128)(2,1)S(1)}, bf16[128,256]{1,0:T(8,128)(2,1)S(1)}) custom-call(s32[2]{0:T(128)S(1)} %pad_add_fusion.at, bf16[128,2048]{1,0:T(8,128)(2,1)S(1)} %collective-permute-done.9.c, bf16[128,2048]{1,0:T(8,128)(2,1)S(1)} %collective-permute-done.11.x, bf16[1376,4096]{1,0:T(8,128)(2,1)S(1)} %bitcast.17, ...), custom_call_target="tpu_custom_call" | custom-call | flops 1 | bytes 1 | tf_op jit(solution)/shard_map/backward/pallas_call | solution.py:134
  83.5 3.2 %collective-permute-done.13 = bf16[1376,128]{1,0:T(8,128)(2,1)S(1)} collective-permute-done((bf16[1376,128]{1,0:T(8,128)(2,1)S(1)}, bf16[1376,128]{1,0:T(8,128)(2,1)S(1)}, u32[]{:S(2)}, u32[]{:S(2)}) %collective-permute-start.13) | collective-permute-done | bytes 352288 | tf_op jit(solution)/shard_map/a2/ppermute | solution.py:21
  86.7 3.3 %collective-permute-done.14 = bf16[1376,128]{1,0:T(8,128)(2,1)S(1)} collective-permute-done((bf16[1376,128]{1,0:T(8,128)(2,1)S(1)}, bf16[1376,128]{1,0:T(8,128)(2,1)S(1)}, u32[]{:S(2)}, u32[]{:S(2)}) %collective-permute-start.14) | collective-permute-done | bytes 352288 | tf_op jit(solution)/shard_map/a1/ppermute | solution.py:21
  90.0 0.9 add_convert_fusion.3
  90.9 0.1 collective-permute-start.17
  91.0 2.3 %collective-permute-start.18 = (bf16[1376,128]{1,0:T(8,128)(2,1)}, bf16[1376,128]{1,0:T(8,128)(2,1)S(1)}, u32[]{:S(2)}, u32[]{:S(2)}) collective-permute-start(bf16[1376,128]{1,0:T(8,128)(2,1)} %copy-done.22), channel_id=1, source_target_pairs={{0,12},{4,8},{8,4},{12,0},{1,13},{5,9},{9,5},{13,1},{2,14},{6,10},... | collective-permute-start | bytes 1056776 | tf_op jit(solution)/shard_map/a3/ppermute | solution.py:21
  93.3 0.3 collective-permute-start.19
  93.6 0.8 copy-done.14
  94.4 0.8 copy-done.16
  95.3 0.8 copy-done.18
  96.1 0.8 copy-done.20
  96.9 2.4 %project.1 = (f32[688,256]{1,0:T(8,128)}, f32[688,256]{1,0:T(8,128)}) custom-call(s32[2]{0:T(128)S(1)} %pad_add_fusion.at, bf16[128,1376]{1,0:T(8,128)(2,1)S(1)} %get-tuple-element.114.h.refs_0_, bf16[128,1376]{1,0:T(8,128)(2,1)S(1)} %collective-permute-done.7.h.refs_1_, bf16[128,1376]{1,0:T(8,128)(2,1)S(1)} %collective-permute-done.8.h.refs_2_, ...), custom_call_target="tpu_custom_call" | custom-call | flops 1 | bytes 1 | tf_op jit(solution)/shard_map/project/pallas_call | solution.py:134
  99.3 0.0 collective-permute-start.20
  99.4 0.5 collective-permute-start.15
  99.8 4.6 %collective-permute-done.17 = bf16[128,2048]{1,0:T(8,128)(2,1)} collective-permute-done((bf16[128,2048]{1,0:T(8,128)(2,1)}, bf16[128,2048]{1,0:T(8,128)(2,1)}, u32[]{:S(2)}, u32[]{:S(2)}) %collective-permute-start.17) | collective-permute-done | bytes 524320 | tf_op jit(solution)/shard_map/r3/ppermute | solution.py:21
  104.5 2.2 %add_convert_fusion.2 = bf16[128,2048]{1,0:T(8,128)(2,1)} fusion(bf16[128,2048]{1,0:T(8,128)(2,1)} %collective-permute-done.17, f32[128,2048]{1,0:T(8,128)S(1)} %copy-done.9, bf16[128,2048]{1,0:T(8,128)(2,1)} %collective-permute-done.16), kind=kLoop, calls=%fused_computation.4 | loop fusion | flops 1310720 | bytes 2621440 | tf_op jit(solution)/shard_map/convert_element_type | solution.py:322
  106.7 4.0 %collective-permute-start.23 = (bf16[128,2048]{1,0:T(8,128)(2,1)}, bf16[128,2048]{1,0:T(8,128)(2,1)}, u32[]{:S(2)}, u32[]{:S(2)}) collective-permute-start(bf16[128,2048]{1,0:T(8,128)(2,1)} %add_convert_fusion.2), channel_id=1, source_target_pairs={{0,8},{4,12},{8,0},{12,4},{1,9},{5,13},{9,1},{13,5},{2,10},{6,14},... | collective-permute-start | bytes 1572872 | tf_op jit(solution)/shard_map/r2/ppermute | solution.py:21
  110.6 3.2 %collective-permute-done.18 = bf16[1376,128]{1,0:T(8,128)(2,1)S(1)} collective-permute-done((bf16[1376,128]{1,0:T(8,128)(2,1)}, bf16[1376,128]{1,0:T(8,128)(2,1)S(1)}, u32[]{:S(2)}, u32[]{:S(2)}) %collective-permute-start.18) | collective-permute-done | bytes 352288 | tf_op jit(solution)/shard_map/a3/ppermute | solution.py:21
  113.9 0.2 pad_maximum_fusion
  114.1 0.1 dynamic-slice_bitcast_fusion.3
  114.2 1.2 maximum_bitcast_fusion
  115.4 0.5 copy-done.7
  115.9 0.9 add_convert_fusion.1
  116.8 0.5 collective-permute-start.21
  117.3 2.5 %copy.11 = bf16[128,5504]{1,0:T(8,128)(2,1)} copy(bf16[128,5504]{0,1:T(8,128)(2,1)} %maximum_bitcast_fusion) | data formatting | bytes 2818048
  119.8 0.0 copy-start.3
  119.8 1.3 copy-done.3
  121.2 11.0 %adam_step.1 = (f32[1376,4096]{1,0:T(8,128)}, f32[1376,256]{1,0:T(8,128)}, f32[1376,256]{1,0:T(8,128)}) custom-call(s32[2]{0:T(128)S(1)} %pad_add_fusion.at, f32[688,256]{1,0:T(8,128)} %get-tuple-element.88.h_up, f32[688,256]{1,0:T(8,128)} %get-tuple-element.89.h_low, f32[688,256]{1,0:T(8,128)} %collective-permute-done.15.t_up, ...), custom_call_target="tpu_custom_call" | custom-call | flops 1 | bytes 1 | tf_op jit(solution)/shard_map/adam_step/pallas_call | solution.py:241
  132.1 4.5 %collective-permute-done.22 = bf16[128,2048]{1,0:T(8,128)(2,1)} collective-permute-done((bf16[128,2048]{1,0:T(8,128)(2,1)}, bf16[128,2048]{1,0:T(8,128)(2,1)}, u32[]{:S(2)}, u32[]{:S(2)}) %collective-permute-start.22) | collective-permute-done | bytes 524320 | tf_op jit(solution)/shard_map/r1/ppermute | solution.py:21
  136.6 2.5 %add_convert_fusion = bf16[128,2048]{1,0:T(8,128)(2,1)} fusion(bf16[128,2048]{1,0:T(8,128)(2,1)} %collective-permute-done.23, bf16[128,2048]{1,0:T(8,128)(2,1)} %collective-permute-done.22, f32[128,2048]{1,0:T(8,128)S(1)} %copy-done.5, bf16[128,2048]{1,0:T(8,128)(2,1)} %collective-permute-done.21), kind=kLoop, calls=%fused_computation.2 | loop fusion | flops 1835008 | bytes 3145728 | tf_op jit(solution)/shard_map/convert_element_type | solution.py:340
  (72 shorter events, 0.2 us)
Async XLA Ops:
  0.6 26.4 %collective-permute-start.1 = (bf16[128,2048]{1,0:T(8,128)(2,1)}, bf16[128,2048]{1,0:T(8,128)(2,1)}, u32[]{:S(2)}, u32[]{:S(2)}) collective-permute-start(bf16[128,2048]{1,0:T(8,128)(2,1)} %c), channel_id=1, source_target_pairs={{0,4},{4,0},{8,12},{12,8},{1,5},{5,1},{9,13},{13,9},{2,6},{6,2},{1... | collective-permute-start | bytes 1572872 | tf_op jit(solution)/shard_map/c1/ppermute | solution.py:21
  3.7 25.9 %collective-permute-start = (bf16[128,2048]{1,0:T(8,128)(2,1)}, bf16[128,2048]{1,0:T(8,128)(2,1)}, u32[]{:S(2)}, u32[]{:S(2)}) collective-permute-start(bf16[128,2048]{1,0:T(8,128)(2,1)} %c), channel_id=1, source_target_pairs={{0,8},{4,12},{8,0},{12,4},{1,9},{5,13},{9,1},{13,5},{2,10},{6,14},... | collective-permute-start | bytes 1572872 | tf_op jit(solution)/shard_map/c2/ppermute | solution.py:21
  6.3 23.3 %collective-permute-start.2 = (bf16[128,2048]{1,0:T(8,128)(2,1)}, bf16[128,2048]{1,0:T(8,128)(2,1)S(1)}, u32[]{:S(2)}, u32[]{:S(2)}) collective-permute-start(bf16[128,2048]{1,0:T(8,128)(2,1)} %c), channel_id=1, source_target_pairs={{0,2},{2,0},{1,3},{3,1},{4,6},{6,4},{5,7},{7,5},{8,10},{10,8},{9,1... | collective-permute-start | bytes 1572872 | tf_op jit(solution)/shard_map/x0/ppermute | solution.py:21
  7.8 3.2 %copy-start.1 = (bf16[2048,256]{1,0:T(8,128)(2,1)S(1)}, bf16[2048,256]{1,0:T(8,128)(2,1)}, u32[]{:S(2)}) copy-start(bf16[2048,256]{1,0:T(8,128)(2,1)} %basis.9) | copy-start | bytes 3145732
  11.9 19.0 %collective-permute-start.3 = (bf16[1024,256]{1,0:T(8,128)(2,1)}, bf16[1024,256]{1,0:T(8,128)(2,1)S(1)}, u32[]{:S(2)}, u32[]{:S(2)}) collective-permute-start(bf16[1024,256]{1,0:T(8,128)(2,1)} %constant_dynamic-slice_fusion.2), channel_id=1, source_target_pairs={{0,2},{2,0},{1,3},{3,1},{4,6},{6,4},{5,7},{7,5},{8,10},{10,8},{9,1... | collective-permute-start | bytes 1572872 | tf_op jit(solution)/shard_map/half/ppermute | solution.py:21
  12.5 4.2 %copy-start = (bf16[1376,4096]{1,0:T(8,128)(2,1)S(1)}, bf16[1376,4096]{1,0:T(8,128)(2,1)}, u32[]{:S(2)}) copy-start(bf16[1376,4096]{1,0:T(8,128)(2,1)} %w.15) | copy-start | bytes 33816580
  16.7 15.7 %copy-start.25 = (bf16[128,1376]{1,0:T(8,128)(2,1)S(1)}, bf16[128,1376]{1,0:T(8,128)(2,1)}, u32[]{:S(2)}) copy-start(bf16[128,1376]{1,0:T(8,128)(2,1)} %get-tuple-element.63) | copy-start | bytes 1056772
  16.7 17.6 %copy-start.10 = (bf16[128,2048]{1,0:T(8,128)(2,1)S(1)}, bf16[128,2048]{1,0:T(8,128)(2,1)}, u32[]{:S(2)}) copy-start(bf16[128,2048]{1,0:T(8,128)(2,1)} %c) | copy-start | bytes 1572868
  19.1 19.1 %copy-start.4 = (f32[128,2048]{1,0:T(8,128)}, f32[128,2048]{1,0:T(8,128)S(1)}, u32[]{:S(2)}) copy-start(f32[128,2048]{1,0:T(8,128)S(1)} %get-tuple-element.99) | copy-start | bytes 3145732
  30.9 2.8 %collective-permute-start.4 = (bf16[1024,256]{1,0:T(8,128)(2,1)S(1)}, bf16[1024,256]{1,0:T(8,128)(2,1)S(1)}, u32[]{:S(2)}, u32[]{:S(2)}) collective-permute-start(bf16[1024,256]{1,0:T(8,128)(2,1)S(1)} %collective-permute-done.3.got), channel_id=1, source_target_pairs={{0,1},{1,0},{2,3},{3,2},{4,5},{5,4},{6,7},{7,6},{8,9},{9,8},{10,11... | collective-permute-start | bytes 1572872 | tf_op jit(solution)/shard_map/basis/ppermute | solution.py:21
  30.9 14.9 %collective-permute-start.5 = (bf16[128,2048]{1,0:T(8,128)(2,1)}, bf16[128,2048]{1,0:T(8,128)(2,1)S(1)}, u32[]{:S(2)}, u32[]{:S(2)}) collective-permute-start(bf16[128,2048]{1,0:T(8,128)(2,1)} %collective-permute-done.c), channel_id=1, source_target_pairs={{0,2},{2,0},{1,3},{3,1},{4,6},{6,4},{5,7},{7,5},{8,10},{10,8},{9,1... | collective-permute-start | bytes 1572872 | tf_op jit(solution)/shard_map/x2/ppermute | solution.py:21
  32.4 18.0 %collective-permute-start.6 = (bf16[128,1376]{1,0:T(8,128)(2,1)S(1)}, bf16[128,1376]{1,0:T(8,128)(2,1)S(1)}, u32[]{:S(2)}, u32[]{:S(2)}) collective-permute-start(bf16[128,1376]{1,0:T(8,128)(2,1)S(1)} %copy-done.25), channel_id=1, source_target_pairs={{0,12},{4,8},{8,4},{12,0},{1,13},{5,9},{9,5},{13,1},{2,14},{6,10},... | collective-permute-start | bytes 1056776 | tf_op jit(solution)/shard_map/h3/ppermute | solution.py:21
  33.6 25.2 %collective-permute-start.9 = (bf16[128,2048]{1,0:T(8,128)(2,1)}, bf16[128,2048]{1,0:T(8,128)(2,1)S(1)}, u32[]{:S(2)}, u32[]{:S(2)}) collective-permute-start(bf16[128,2048]{1,0:T(8,128)(2,1)} %collective-permute-done.c), channel_id=1, source_target_pairs={{0,4},{4,0},{8,12},{12,8},{1,5},{5,1},{9,13},{13,9},{2,6},{6,2},{1... | collective-permute-start | bytes 1572872 | tf_op jit(solution)/shard_map/c3/ppermute | solution.py:21
  33.7 25.2 %collective-permute-start.10 = (bf16[128,2048]{1,0:T(8,128)(2,1)}, bf16[128,2048]{1,0:T(8,128)(2,1)S(1)}, u32[]{:S(2)}, u32[]{:S(2)}) collective-permute-start(bf16[128,2048]{1,0:T(8,128)(2,1)} %collective-permute-done.1.c), channel_id=1, source_target_pairs={{0,2},{2,0},{1,3},{3,1},{4,6},{6,4},{5,7},{7,5},{8,10},{10,8},{9,1... | collective-permute-start | bytes 1572872 | tf_op jit(solution)/shard_map/x1/ppermute | solution.py:21
  34.3 18.1 %slice-start = ((s8[11272192]{0:T(1024)(128)(4,1)}), s8[4194304]{0:T(1024)(128)(4,1)S(1)}, s32[]{:S(2)}) async-start(s8[11272192]{0:T(1024)(128)(4,1)} %bitcast.16), calls=%async_computation | async-start | bytes 8388608
  34.3 18.1 %slice-start.1 = ((s8[11272192]{0:T(1024)(128)(4,1)}), s8[4194304]{0:T(1024)(128)(4,1)S(1)}, s32[]{:S(2)}) async-start(s8[11272192]{0:T(1024)(128)(4,1)} %bitcast.16), calls=%async_computation.1 | async-start | bytes 8388608
  38.2 0.6 copy-start.13
  38.8 11.6 %copy-start.11 = (bf16[1376,128]{1,0:T(8,128)(2,1)}, bf16[1376,128]{1,0:T(8,128)(2,1)S(1)}, u32[]{:S(2)}) copy-start(bf16[1376,128]{1,0:T(8,128)(2,1)S(1)} %get-tuple-element.94) | copy-start | bytes 1056772
  45.8 4.6 %copy-start.24 = (bf16[128,1376]{1,0:T(8,128)(2,1)S(1)}, bf16[128,1376]{1,0:T(8,128)(2,1)}, u32[]{:S(2)}) copy-start(bf16[128,1376]{1,0:T(8,128)(2,1)} %get-tuple-element.65) | copy-start | bytes 1056772
  45.8 5.2 %copy-start.23 = (bf16[128,1376]{1,0:T(8,128)(2,1)S(1)}, bf16[128,1376]{1,0:T(8,128)(2,1)}, u32[]{:S(2)}) copy-start(bf16[128,1376]{1,0:T(8,128)(2,1)} %get-tuple-element.64) | copy-start | bytes 1056772
  45.8 6.5 %slice-start.2 = ((s8[11272192]{0:T(1024)(128)(4,1)}), s8[2883584]{0:T(1024)(128)(4,1)S(1)}, s32[]{:S(2)}) async-start(s8[11272192]{0:T(1024)(128)(4,1)} %bitcast.16), calls=%async_computation.2 | async-start | bytes 5767168
  50.4 4.3 %copy-start.15 = (bf16[128,256]{1,0:T(8,128)(2,1)}, bf16[128,256]{1,0:T(8,128)(2,1)S(1)}, u32[]{:S(2)}) copy-start(bf16[128,256]{1,0:T(8,128)(2,1)S(1)} %get-tuple-element.86.refs_6_) | copy-start | bytes 196612
  50.4 18.5 %collective-permute-start.8 = (bf16[128,1376]{1,0:T(8,128)(2,1)S(1)}, bf16[128,1376]{1,0:T(8,128)(2,1)S(1)}, u32[]{:S(2)}, u32[]{:S(2)}) collective-permute-start(bf16[128,1376]{1,0:T(8,128)(2,1)S(1)} %copy-done.24), channel_id=1, source_target_pairs={{0,8},{4,12},{8,0},{12,4},{1,9},{5,13},{9,1},{13,5},{2,10},{6,14},... | collective-permute-start | bytes 1056776 | tf_op jit(solution)/shard_map/h2/ppermute | solution.py:21
  51.0 23.0 %collective-permute-start.7 = (bf16[128,1376]{1,0:T(8,128)(2,1)S(1)}, bf16[128,1376]{1,0:T(8,128)(2,1)S(1)}, u32[]{:S(2)}, u32[]{:S(2)}) collective-permute-start(bf16[128,1376]{1,0:T(8,128)(2,1)S(1)} %copy-done.23), channel_id=1, source_target_pairs={{0,4},{4,0},{8,12},{12,8},{1,5},{5,1},{9,13},{13,9},{2,6},{6,2},{1... | collective-permute-start | bytes 1056776 | tf_op jit(solution)/shard_map/h1/ppermute | solution.py:21
  58.8 20.2 %collective-permute-start.11 = (bf16[128,2048]{1,0:T(8,128)(2,1)S(1)}, bf16[128,2048]{1,0:T(8,128)(2,1)S(1)}, u32[]{:S(2)}, u32[]{:S(2)}) collective-permute-start(bf16[128,2048]{1,0:T(8,128)(2,1)S(1)} %collective-permute-done.9.c), channel_id=1, source_target_pairs={{0,2},{2,0},{1,3},{3,1},{4,6},{6,4},{5,7},{7,5},{8,10},{10,8},{9,1... | collective-permute-start | bytes 1572872 | tf_op jit(solution)/shard_map/x3/ppermute | solution.py:21
  63.2 9.7 %copy-start.17 = (bf16[128,256]{1,0:T(8,128)(2,1)}, bf16[128,256]{1,0:T(8,128)(2,1)S(1)}, u32[]{:S(2)}) copy-start(bf16[128,256]{1,0:T(8,128)(2,1)S(1)} %get-tuple-element.85.refs_5_) | copy-start | bytes 196612
  68.9 21.1 %collective-permute-start.12 = (bf16[128,2048]{1,0:T(8,128)(2,1)S(1)}, bf16[128,2048]{1,0:T(8,128)(2,1)S(1)}, u32[]{:S(2)}, u32[]{:S(2)}) collective-permute-start(bf16[128,2048]{1,0:T(8,128)(2,1)S(1)} %get-tuple-element.80), channel_id=1, source_target_pairs={{0,2},{2,0},{1,3},{3,1},{4,6},{6,4},{5,7},{7,5},{8,10},{10,8},{9,1... | collective-permute-start | bytes 1572872 | tf_op jit(solution)/shard_map/y3/ppermute | solution.py:21
  70.4 16.3 %collective-permute-start.13 = (bf16[1376,128]{1,0:T(8,128)(2,1)S(1)}, bf16[1376,128]{1,0:T(8,128)(2,1)S(1)}, u32[]{:S(2)}, u32[]{:S(2)}) collective-permute-start(bf16[1376,128]{1,0:T(8,128)(2,1)S(1)} %get-tuple-element.81), channel_id=1, source_target_pairs={{0,8},{4,12},{8,0},{12,4},{1,9},{5,13},{9,1},{13,5},{2,10},{6,14},... | collective-permute-start | bytes 1056776 | tf_op jit(solution)/shard_map/a2/ppermute | solution.py:21
  73.0 1.0 copy-start.8
  73.9 16.0 %collective-permute-start.14 = (bf16[1376,128]{1,0:T(8,128)(2,1)S(1)}, bf16[1376,128]{1,0:T(8,128)(2,1)S(1)}, u32[]{:S(2)}, u32[]{:S(2)}) collective-permute-start(bf16[1376,128]{1,0:T(8,128)(2,1)S(1)} %get-tuple-element.82), channel_id=1, source_target_pairs={{0,4},{4,0},{8,12},{12,8},{1,5},{5,1},{9,13},{13,9},{2,6},{6,2},{1... | collective-permute-start | bytes 1056776 | tf_op jit(solution)/shard_map/a1/ppermute | solution.py:21
  78.0 1.0 copy-start.6
  79.0 4.5 %copy-start.21 = (bf16[128,2048]{1,0:T(8,128)(2,1)}, bf16[128,2048]{1,0:T(8,128)(2,1)S(1)}, u32[]{:S(2)}) copy-start(bf16[128,2048]{1,0:T(8,128)(2,1)S(1)} %get-tuple-element.95) | copy-start | bytes 1572868
  79.0 20.4 %collective-permute-start.16 = (bf16[128,2048]{1,0:T(8,128)(2,1)}, bf16[128,2048]{1,0:T(8,128)(2,1)}, u32[]{:S(2)}, u32[]{:S(2)}) collective-permute-start(bf16[128,2048]{1,0:T(8,128)(2,1)} %get-tuple-element.92), channel_id=1, source_target_pairs={{0,2},{2,0},{1,3},{3,1},{4,6},{6,4},{5,7},{7,5},{8,10},{10,8},{9,1... | collective-permute-start | bytes 1572872 | tf_op jit(solution)/shard_map/y2/ppermute | solution.py:21
  83.4 7.4 %copy-start.19 = (bf16[128,256]{1,0:T(8,128)(2,1)}, bf16[128,256]{1,0:T(8,128)(2,1)S(1)}, u32[]{:S(2)}) copy-start(bf16[128,256]{1,0:T(8,128)(2,1)S(1)} %get-tuple-element.87.refs_7_) | copy-start | bytes 196612
  83.5 7.4 %copy-start.22 = (bf16[1376,128]{1,0:T(8,128)(2,1)}, bf16[1376,128]{1,0:T(8,128)(2,1)S(1)}, u32[]{:S(2)}) copy-start(bf16[1376,128]{1,0:T(8,128)(2,1)S(1)} %get-tuple-element.79) | copy-start | bytes 1056772
  86.7 4.2 %copy-start.26 = (bf16[1376,128]{1,0:T(8,128)(2,1)}, bf16[1376,128]{1,0:T(8,128)(2,1)S(1)}, u32[]{:S(2)}) copy-start(bf16[1376,128]{1,0:T(8,128)(2,1)S(1)} %collective-permute-done.13) | copy-start | bytes 1056772
  90.0 0.9 copy-start.28
  90.9 13.6 %collective-permute-start.17 = (bf16[128,2048]{1,0:T(8,128)(2,1)}, bf16[128,2048]{1,0:T(8,128)(2,1)}, u32[]{:S(2)}, u32[]{:S(2)}) collective-permute-start(bf16[128,2048]{1,0:T(8,128)(2,1)} %add_convert_fusion.3), channel_id=1, source_target_pairs={{0,4},{4,0},{8,12},{12,8},{1,5},{5,1},{9,13},{13,9},{2,6},{6,2},{1... | collective-permute-start | bytes 1572872 | tf_op jit(solution)/shard_map/r3/ppermute | solution.py:21
  91.0 13.5 %copy-start.9 = (f32[128,2048]{1,0:T(8,128)S(1)}, f32[128,2048]{1,0:T(8,128)}, u32[]{:S(2)}) copy-start(f32[128,2048]{1,0:T(8,128)} %copy-done.8) | copy-start | bytes 3145732
  91.0 22.9 %collective-permute-start.18 = (bf16[1376,128]{1,0:T(8,128)(2,1)}, bf16[1376,128]{1,0:T(8,128)(2,1)S(1)}, u32[]{:S(2)}, u32[]{:S(2)}) collective-permute-start(bf16[1376,128]{1,0:T(8,128)(2,1)} %copy-done.22), channel_id=1, source_target_pairs={{0,12},{4,8},{8,4},{12,0},{1,13},{5,9},{9,5},{13,1},{2,14},{6,10},... | collective-permute-start | bytes 1056776 | tf_op jit(solution)/shard_map/a3/ppermute | solution.py:21
  93.3 22.1 %collective-permute-start.19 = (bf16[128,2048]{1,0:T(8,128)(2,1)}, bf16[128,2048]{1,0:T(8,128)(2,1)S(1)}, u32[]{:S(2)}, u32[]{:S(2)}) collective-permute-start(bf16[128,2048]{1,0:T(8,128)(2,1)} %copy-done.21), channel_id=1, source_target_pairs={{0,2},{2,0},{1,3},{3,1},{4,6},{6,4},{5,7},{7,5},{8,10},{10,8},{9,1... | collective-permute-start | bytes 1572872 | tf_op jit(solution)/shard_map/y1/ppermute | solution.py:21
  93.6 0.8 copy-start.14
  94.4 0.8 copy-start.16
  95.3 0.8 copy-start.18
  96.1 0.8 copy-start.20
  99.3 14.6 %copy-start.12 = (bf16[1376,128]{1,0:T(8,128)(2,1)S(1)}, bf16[1376,128]{1,0:T(8,128)(2,1)}, u32[]{:S(2)}) copy-start(bf16[1376,128]{1,0:T(8,128)(2,1)} %copy-done.11) | copy-start | bytes 1056772
  99.3 14.6 %copy-start.27 = (bf16[1376,128]{1,0:T(8,128)(2,1)S(1)}, bf16[1376,128]{1,0:T(8,128)(2,1)}, u32[]{:S(2)}) copy-start(bf16[1376,128]{1,0:T(8,128)(2,1)} %copy-done.26) | copy-start | bytes 1056772
  99.3 14.6 %copy-start.29 = (bf16[1376,128]{1,0:T(8,128)(2,1)S(1)}, bf16[1376,128]{1,0:T(8,128)(2,1)}, u32[]{:S(2)}) copy-start(bf16[1376,128]{1,0:T(8,128)(2,1)} %copy-done.28) | copy-start | bytes 1056772
  99.3 20.5 %collective-permute-start.20 = (f32[688,256]{1,0:T(8,128)}, f32[688,256]{1,0:T(8,128)}, u32[]{:S(2)}, u32[]{:S(2)}) collective-permute-start(f32[688,256]{1,0:T(8,128)} %get-tuple-element.89.h_low), channel_id=1, source_target_pairs={{0,1},{1,0},{2,3},{3,2},{4,5},{5,4},{6,7},{7,6},{8,9},{9,8},{10,11... | collective-permute-start | bytes 2113544 | tf_op jit(solution)/shard_map/rows/ppermute | solution.py:21
  99.4 20.5 %collective-permute-start.15 = (f32[688,256]{1,0:T(8,128)}, f32[688,256]{1,0:T(8,128)}, u32[]{:S(2)}, u32[]{:S(2)}) collective-permute-start(f32[688,256]{1,0:T(8,128)} %get-tuple-element.88.h_up), channel_id=1, source_target_pairs={{0,1},{1,0},{2,3},{3,2},{4,5},{5,4},{6,7},{7,6},{8,9},{9,8},{10,11... | collective-permute-start | bytes 2113544 | tf_op jit(solution)/shard_map/rows/ppermute | solution.py:21
  106.7 29.9 %collective-permute-start.23 = (bf16[128,2048]{1,0:T(8,128)(2,1)}, bf16[128,2048]{1,0:T(8,128)(2,1)}, u32[]{:S(2)}, u32[]{:S(2)}) collective-permute-start(bf16[128,2048]{1,0:T(8,128)(2,1)} %add_convert_fusion.2), channel_id=1, source_target_pairs={{0,8},{4,12},{8,0},{12,4},{1,9},{5,13},{9,1},{13,5},{2,10},{6,14},... | collective-permute-start | bytes 1572872 | tf_op jit(solution)/shard_map/r2/ppermute | solution.py:21
  114.2 1.7 %copy-start.7 = (f32[128,2048]{1,0:T(8,128)S(1)}, f32[128,2048]{1,0:T(8,128)}, u32[]{:S(2)}) copy-start(f32[128,2048]{1,0:T(8,128)} %copy-done.6) | copy-start | bytes 3145732
  116.8 3.0 %copy-start.2 = (f32[1376,256]{1,0:T(8,128)S(1)}, f32[1376,256]{1,0:T(8,128)}, u32[]{:S(2)}) copy-start(f32[1376,256]{1,0:T(8,128)} %first.1) | copy-start | bytes 4227076
  116.8 19.8 %collective-permute-start.22 = (bf16[128,2048]{1,0:T(8,128)(2,1)}, bf16[128,2048]{1,0:T(8,128)(2,1)}, u32[]{:S(2)}, u32[]{:S(2)}) collective-permute-start(bf16[128,2048]{1,0:T(8,128)(2,1)} %add_convert_fusion.1), channel_id=1, source_target_pairs={{0,4},{4,0},{8,12},{12,8},{1,5},{5,1},{9,13},{13,9},{2,6},{6,2},{1... | collective-permute-start | bytes 1572872 | tf_op jit(solution)/shard_map/r1/ppermute | solution.py:21
  116.8 19.8 %collective-permute-start.21 = (bf16[128,2048]{1,0:T(8,128)(2,1)}, bf16[128,2048]{1,0:T(8,128)(2,1)}, u32[]{:S(2)}, u32[]{:S(2)}) collective-permute-start(bf16[128,2048]{1,0:T(8,128)(2,1)} %get-tuple-element.100), channel_id=1, source_target_pairs={{0,2},{2,0},{1,3},{3,1},{4,6},{6,4},{5,7},{7,5},{8,10},{10,8},{9,1... | collective-permute-start | bytes 1572872 | tf_op jit(solution)/shard_map/y0/ppermute | solution.py:21
  119.8 1.4 copy-start.3
  121.2 15.4 %copy-start.5 = (f32[128,2048]{1,0:T(8,128)S(1)}, f32[128,2048]{1,0:T(8,128)}, u32[]{:S(2)}) copy-start(f32[128,2048]{1,0:T(8,128)} %copy-done.4) | copy-start | bytes 3145732

commit v2 on v1

--- a/solution.py
+++ b/solution.py
@@ -318,7 +318,10 @@
     seen(o3)
     local = project(at, (h0, h1, h2, h3), (go(k0), k1, k2, k3))
     other = [swap(v, "sub", 1, "rows") for v in local]
-    seen(local[0], y2, r3)
+    seen(local[0], y1, y2)
+    o1 = (go(m1) + y1.astype(f32)).astype(bf16)
+    r1 = swap(o1, "fsdp", 1, "r1")
+    seen(o1, r3)
     o2 = (go(m2) + y2.astype(f32) + r3.astype(f32)).astype(bf16)
     r2 = swap(o2, "fsdp", 2, "r2")
     y0 = swap(go(p0), "tp", 1, "y0")
@@ -327,10 +330,7 @@
     acts_grad = jnp.concatenate(
         [lax.dynamic_index_in_dim(by_owner, z ^ j, 0, keepdims=False) for j in range(4)], axis=0
     ).T
-    seen(o2, acts_grad, y1)
-    o1 = (go(m1) + y1.astype(f32)).astype(bf16)
-    r1 = swap(o1, "fsdp", 1, "r1")
-    seen(o1)
+    seen(acts_grad)
     weight_step, new_first, new_second = adam_step(
         at, local, (go(other[0]), other[1]), tokens, first_moment, second_moment, projector, half, basis
     )

time: 140 us -> 138 us (0.986)
  waiting for transfers between devices: 47.3 us -> 43.2 us
  starting transfers between devices: 24.4 us -> 26.1 us
    ppermute x24, waiting for transfers between devices: 47.3 us -> 43.2 us  [swap(): return lax.ppermute(x, axis, [(i, i ^ bit) for i in range(n)])]
    ppermute x24, starting transfers between devices: 24.4 us -> 26.1 us  [swap(): return lax.ppermute(x, axis, [(i, i ^ bit) for i in range(n)])]
    unnamed x67 -> x65, local copies, waits for them, and re-layouts: 14.6 us -> 14.2 us
  transfers between devices with their start and end apart: 24 -> 24, of which waited for: 11 -> 10; matrix products, arithmetic and copies ran while one was open for 9% -> 10% of each run, Pallas kernels for 29% -> 29%
where the time goes in v2:
time: 138 us; the launch traced here: 137 us
  waiting for transfers between devices  43.2 us (31%)
  Pallas kernels  39.8 us (29%)
  starting transfers between devices  26.1 us (19%)
  local copies, waits for them, and re-layouts  18.4 us (13%)
  other arithmetic  9.11 us (7%)
    ppermute x24, waiting for transfers between devices, swap(): return lax.ppermute(x, axis, [(i, i ^ bit) for i in range(n)])  43.2 us
    pallas_call x9, Pallas kernels, in_vmem(): pl.pallas_call(kernel, in_specs=[pl.BlockSpec(memory_space=pltpu.SMEM)] +...  28.8 us
    ppermute x24, starting transfers between devices, swap(): return lax.ppermute(x, axis, [(i, i ^ bit) for i in range(n)])  26.1 us
    unnamed x65, local copies, waits for them, and re-layouts  14.2 us
    pallas_call x1, Pallas kernels, adam_step(): pl.pallas_call(kernel, grid=(4,), in_specs=[pl.BlockSpec(memory_space=plt...  11 us
    dynamic_slice x1, local copies, waits for them, and re-layouts, own_units(): return lax.dynamic_slice_in_dim(hidden_acts, (z ^ k) * width, width, 1)  3.25 us
  transfers between devices with their start and end apart: 24, of which 10 were waited for; matrix products, arithmetic and copies ran while one was open for 10% of the time, Pallas kernels for 29%

profile of v2, /device:TPU:0, one launch (start us, length us, event | category | flops | bytes accessed | tf_op | source)
XLA Modules:
  0.0 137.4 jit_solution(9357476747118584278)
XLA Ops:
  0.6 3.1 %collective-permute-start.1 = (bf16[128,2048]{1,0:T(8,128)(2,1)}, bf16[128,2048]{1,0:T(8,128)(2,1)}, u32[]{:S(2)}, u32[]{:S(2)}) collective-permute-start(bf16[128,2048]{1,0:T(8,128)(2,1)} %c), channel_id=1, source_target_pairs={{0,4},{4,0},{8,12},{12,8},{1,5},{5,1},{9,13},{13,9},{2,6},{6,2},{1... | collective-permute-start | bytes 1572872 | tf_op jit(solution)/shard_map/c1/ppermute | solution.py:21
  3.7 2.6 %collective-permute-start = (bf16[128,2048]{1,0:T(8,128)(2,1)}, bf16[128,2048]{1,0:T(8,128)(2,1)}, u32[]{:S(2)}, u32[]{:S(2)}) collective-permute-start(bf16[128,2048]{1,0:T(8,128)(2,1)} %c), channel_id=1, source_target_pairs={{0,8},{4,12},{8,0},{12,4},{1,9},{5,13},{9,1},{13,5},{2,10},{6,14},... | collective-permute-start | bytes 1572872 | tf_op jit(solution)/shard_map/c2/ppermute | solution.py:21
  6.3 1.5 %collective-permute-start.2 = (bf16[128,2048]{1,0:T(8,128)(2,1)}, bf16[128,2048]{1,0:T(8,128)(2,1)S(1)}, u32[]{:S(2)}, u32[]{:S(2)}) collective-permute-start(bf16[128,2048]{1,0:T(8,128)(2,1)} %c), channel_id=1, source_target_pairs={{0,2},{2,0},{1,3},{3,1},{4,6},{6,4},{5,7},{7,5},{8,10},{10,8},{9,1... | collective-permute-start | bytes 1572872 | tf_op jit(solution)/shard_map/x0/ppermute | solution.py:21
  7.8 3.2 %constant_dynamic-slice_fusion = (bf16[128,1376]{1,0:T(8,128)(2,1)}, bf16[128,1376]{1,0:T(8,128)(2,1)}, bf16[128,1376]{1,0:T(8,128)(2,1)S(1)}, bf16[128,1376]{1,0:T(8,128)(2,1)}) fusion(bf16[128,5504]{1,0:T(8,128)(2,1)} %param.6, s32[]{:T(128)S(6)} %select_n.32, s32[]{:T(128)S(6)} %select_n.29, s32[]{:T(128)S(6)} %select_n.28, s32[]{:T(128)S(6)} %select_n.31), kind=kLoop, calls=%fused_computation.10 | loop fusion | bytes 2818064 | tf_op jit(solution)/shard_map/dynamic_slice | solution.py:275
  11.1 0.8 constant_dynamic-slice_fusion.2
  11.9 0.5 collective-permute-start.3
  12.4 0.1 pad_add_fusion.at
  12.5 4.2 %copy-done = bf16[1376,4096]{1,0:T(8,128)(2,1)S(1)} copy-done((bf16[1376,4096]{1,0:T(8,128)(2,1)S(1)}, bf16[1376,4096]{1,0:T(8,128)(2,1)}, u32[]{:S(2)}) %copy-start) | copy-done | bytes 11272216
  16.7 2.4 %forward.4 = (bf16[128,2048]{1,0:T(8,128)(2,1)}, f32[128,2048]{1,0:T(8,128)S(1)}) custom-call(s32[2]{0:T(128)S(1)} %pad_add_fusion.at, bf16[128,1376]{1,0:T(8,128)(2,1)S(1)} %get-tuple-element.114.h.refs_0_, bf16[1376,4096]{1,0:T(8,128)(2,1)S(1)} %copy-done), custom_call_target="tpu_custom_call" | custom-call | flops 1 | bytes 1 | tf_op jit(solution)/shard_map/forward/pallas_call | solution.py:134
  19.1 8.0 %collective-permute-done.1.c = bf16[128,2048]{1,0:T(8,128)(2,1)} collective-permute-done((bf16[128,2048]{1,0:T(8,128)(2,1)}, bf16[128,2048]{1,0:T(8,128)(2,1)}, u32[]{:S(2)}, u32[]{:S(2)}) %collective-permute-start.1) | collective-permute-done | bytes 524320 | tf_op jit(solution)/shard_map/c1/ppermute | solution.py:21
  27.1 2.5 %collective-permute-done.c = bf16[128,2048]{1,0:T(8,128)(2,1)} collective-permute-done((bf16[128,2048]{1,0:T(8,128)(2,1)}, bf16[128,2048]{1,0:T(8,128)(2,1)}, u32[]{:S(2)}, u32[]{:S(2)}) %collective-permute-start) | collective-permute-done | bytes 524320 | tf_op jit(solution)/shard_map/c2/ppermute | solution.py:21
  29.6 1.2 collective-permute-done.3.got
  30.9 0.0 collective-permute-start.4
  30.9 1.5 %collective-permute-start.5 = (bf16[128,2048]{1,0:T(8,128)(2,1)}, bf16[128,2048]{1,0:T(8,128)(2,1)S(1)}, u32[]{:S(2)}, u32[]{:S(2)}) collective-permute-start(bf16[128,2048]{1,0:T(8,128)(2,1)} %collective-permute-done.c), channel_id=1, source_target_pairs={{0,2},{2,0},{1,3},{3,1},{4,6},{6,4},{5,7},{7,5},{8,10},{10,8},{9,1... | collective-permute-start | bytes 1572872 | tf_op jit(solution)/shard_map/x2/ppermute | solution.py:21
  32.4 1.3 collective-permute-start.6
  33.7 0.6 collective-permute-start.10
  34.3 3.9 %backward.4 = (bf16[1376,128]{1,0:T(8,128)(2,1)S(1)}, bf16[128,256]{1,0:T(8,128)(2,1)S(1)}) custom-call(s32[2]{0:T(128)S(1)} %pad_add_fusion.at, bf16[128,2048]{1,0:T(8,128)(2,1)S(1)} %copy-done.10, bf16[128,2048]{1,0:T(8,128)(2,1)S(1)} %collective-permute-done.2.x, bf16[1376,4096]{1,0:T(8,128)(2,1)S(1)} %copy-done, bf16[2048,256]{1,0:T(8,128)(2,1)S(1)} %copy-done.1, ...), custom_call_target="tpu_custom_call" | custom-call | flops 1 | bytes 1 | tf_op jit(solution)/shard_map/backward/pallas_call | solution.py:134
  38.2 0.6 copy-done.13
  38.8 6.9 %collective-permute-done.5.x = bf16[128,2048]{1,0:T(8,128)(2,1)S(1)} collective-permute-done((bf16[128,2048]{1,0:T(8,128)(2,1)}, bf16[128,2048]{1,0:T(8,128)(2,1)S(1)}, u32[]{:S(2)}, u32[]{:S(2)}) %collective-permute-start.5) | collective-permute-done | bytes 524320 | tf_op jit(solution)/shard_map/x2/ppermute | solution.py:21
  45.8 4.6 %backward.5 = (bf16[1376,128]{1,0:T(8,128)(2,1)S(1)}, bf16[128,256]{1,0:T(8,128)(2,1)S(1)}) custom-call(s32[2]{0:T(128)S(1)} %pad_add_fusion.at, bf16[128,2048]{1,0:T(8,128)(2,1)} %collective-permute-done.c, bf16[128,2048]{1,0:T(8,128)(2,1)S(1)} %collective-permute-done.5.x, bf16[1376,4096]{1,0:T(8,128)(2,1)S(1)} %copy-done, ...), custom_call_target="tpu_custom_call" | custom-call | flops 1 | bytes 1 | tf_op jit(solution)/shard_map/backward/pallas_call | solution.py:134
  50.4 0.6 collective-permute-start.8
  51.0 1.4 collective-permute-start.7
  52.4 2.4 %forward.5 = (bf16[128,2048]{1,0:T(8,128)(2,1)S(1)}, f32[128,2048]{1,0:T(8,128)S(1)}) custom-call(s32[2]{0:T(128)S(1)} %pad_add_fusion.at, bf16[128,1376]{1,0:T(8,128)(2,1)S(1)} %collective-permute-done.6.h.refs_3_, bf16[1376,4096]{1,0:T(8,128)(2,1)S(1)} %bitcast.17), custom_call_target="tpu_custom_call" | custom-call | flops 1 | bytes 1 | tf_op jit(solution)/shard_map/forward/pallas_call | solution.py:134
  54.7 4.1 %collective-permute-done.9.c = bf16[128,2048]{1,0:T(8,128)(2,1)S(1)} collective-permute-done((bf16[128,2048]{1,0:T(8,128)(2,1)}, bf16[128,2048]{1,0:T(8,128)(2,1)S(1)}, u32[]{:S(2)}, u32[]{:S(2)}) %collective-permute-start.9) | collective-permute-done | bytes 524320 | tf_op jit(solution)/shard_map/c3/ppermute | solution.py:21
  58.8 4.4 %backward.6 = (bf16[1376,128]{1,0:T(8,128)(2,1)S(1)}, bf16[128,256]{1,0:T(8,128)(2,1)S(1)}) custom-call(s32[2]{0:T(128)S(1)} %pad_add_fusion.at, bf16[128,2048]{1,0:T(8,128)(2,1)} %collective-permute-done.1.c, bf16[128,2048]{1,0:T(8,128)(2,1)S(1)} %collective-permute-done.10.x, bf16[1376,4096]{1,0:T(8,128)(2,1)S(1)} %bitcast.17, ...), custom_call_target="tpu_custom_call" | custom-call | flops 1 | bytes 1 | tf_op jit(solution)/shard_map/backward/pallas_call | solution.py:134
  63.3 5.7 %collective-permute-done.8.h.refs_2_ = bf16[128,1376]{1,0:T(8,128)(2,1)S(1)} collective-permute-done((bf16[128,1376]{1,0:T(8,128)(2,1)S(1)}, bf16[128,1376]{1,0:T(8,128)(2,1)S(1)}, u32[]{:S(2)}, u32[]{:S(2)}) %collective-permute-start.8) | collective-permute-done | bytes 352288 | tf_op jit(solution)/shard_map/h2/ppermute | solution.py:21
  68.9 1.5 %collective-permute-start.12 = (bf16[128,2048]{1,0:T(8,128)(2,1)S(1)}, bf16[128,2048]{1,0:T(8,128)(2,1)S(1)}, u32[]{:S(2)}, u32[]{:S(2)}) collective-permute-start(bf16[128,2048]{1,0:T(8,128)(2,1)S(1)} %get-tuple-element.80), channel_id=1, source_target_pairs={{0,2},{2,0},{1,3},{3,1},{4,6},{6,4},{5,7},{7,5},{8,10},{10,8},{9,1... | collective-permute-start | bytes 1572872 | tf_op jit(solution)/shard_map/y3/ppermute | solution.py:21
  70.4 0.0 collective-permute-start.13
  70.4 2.5 %forward.6 = (bf16[128,2048]{1,0:T(8,128)(2,1)}, f32[128,2048]{1,0:T(8,128)S(1)}) custom-call(s32[2]{0:T(128)S(1)} %pad_add_fusion.at, bf16[128,1376]{1,0:T(8,128)(2,1)S(1)} %collective-permute-done.8.h.refs_2_, bf16[1376,4096]{1,0:T(8,128)(2,1)S(1)} %bitcast.17), custom_call_target="tpu_custom_call" | custom-call | flops 1 | bytes 1 | tf_op jit(solution)/shard_map/forward/pallas_call | solution.py:134
  73.0 0.0 copy-start.6
  73.0 1.0 copy-done.6
  73.9 1.7 %collective-permute-start.14 = (bf16[1376,128]{1,0:T(8,128)(2,1)S(1)}, bf16[1376,128]{1,0:T(8,128)(2,1)S(1)}, u32[]{:S(2)}, u32[]{:S(2)}) collective-permute-start(bf16[1376,128]{1,0:T(8,128)(2,1)S(1)} %get-tuple-element.82), channel_id=1, source_target_pairs={{0,4},{4,0},{8,12},{12,8},{1,5},{5,1},{9,13},{13,9},{2,6},{6,2},{1... | collective-permute-start | bytes 1056776 | tf_op jit(solution)/shard_map/a1/ppermute | solution.py:21
  75.6 2.4 %forward.7 = (bf16[128,2048]{1,0:T(8,128)(2,1)}, f32[128,2048]{1,0:T(8,128)S(1)}) custom-call(s32[2]{0:T(128)S(1)} %pad_add_fusion.at, bf16[128,1376]{1,0:T(8,128)(2,1)S(1)} %collective-permute-done.7.h.refs_1_, bf16[1376,4096]{1,0:T(8,128)(2,1)S(1)} %bitcast.17), custom_call_target="tpu_custom_call" | custom-call | flops 1 | bytes 1 | tf_op jit(solution)/shard_map/forward/pallas_call | solution.py:134
  78.0 0.0 copy-start.8
  78.0 1.0 copy-done.8
  79.0 0.5 collective-permute-start.17
  79.5 3.9 %backward.7 = (bf16[1376,128]{1,0:T(8,128)(2,1)S(1)}, bf16[128,256]{1,0:T(8,128)(2,1)S(1)}) custom-call(s32[2]{0:T(128)S(1)} %pad_add_fusion.at, bf16[128,2048]{1,0:T(8,128)(2,1)S(1)} %collective-permute-done.9.c, bf16[128,2048]{1,0:T(8,128)(2,1)S(1)} %collective-permute-done.11.x, bf16[1376,4096]{1,0:T(8,128)(2,1)S(1)} %bitcast.17, ...), custom_call_target="tpu_custom_call" | custom-call | flops 1 | bytes 1 | tf_op jit(solution)/shard_map/backward/pallas_call | solution.py:134
  83.5 3.2 %collective-permute-done.13 = bf16[1376,128]{1,0:T(8,128)(2,1)S(1)} collective-permute-done((bf16[1376,128]{1,0:T(8,128)(2,1)S(1)}, bf16[1376,128]{1,0:T(8,128)(2,1)S(1)}, u32[]{:S(2)}, u32[]{:S(2)}) %collective-permute-start.13) | collective-permute-done | bytes 352288 | tf_op jit(solution)/shard_map/a2/ppermute | solution.py:21
  86.7 3.3 %collective-permute-done.14 = bf16[1376,128]{1,0:T(8,128)(2,1)S(1)} collective-permute-done((bf16[1376,128]{1,0:T(8,128)(2,1)S(1)}, bf16[1376,128]{1,0:T(8,128)(2,1)S(1)}, u32[]{:S(2)}, u32[]{:S(2)}) %collective-permute-start.14) | collective-permute-done | bytes 352288 | tf_op jit(solution)/shard_map/a1/ppermute | solution.py:21
  90.0 0.3 collective-permute-start.16
  90.2 0.9 add_convert_fusion.3
  91.2 0.1 collective-permute-start.18
  91.3 0.0 copy-start.9
  91.3 2.3 %collective-permute-start.19 = (bf16[1376,128]{1,0:T(8,128)(2,1)}, bf16[1376,128]{1,0:T(8,128)(2,1)S(1)}, u32[]{:S(2)}, u32[]{:S(2)}) collective-permute-start(bf16[1376,128]{1,0:T(8,128)(2,1)} %copy-done.21), channel_id=1, source_target_pairs={{0,12},{4,8},{8,4},{12,0},{1,13},{5,9},{9,5},{13,1},{2,14},{6,10},... | collective-permute-start | bytes 1056776 | tf_op jit(solution)/shard_map/a3/ppermute | solution.py:21
  93.6 0.8 copy-done.14
  94.4 0.8 copy-done.16
  95.3 0.8 copy-done.18
  96.1 0.8 copy-done.20
  97.0 2.4 %project.1 = (f32[688,256]{1,0:T(8,128)}, f32[688,256]{1,0:T(8,128)}) custom-call(s32[2]{0:T(128)S(1)} %pad_add_fusion.at, bf16[128,1376]{1,0:T(8,128)(2,1)S(1)} %get-tuple-element.114.h.refs_0_, bf16[128,1376]{1,0:T(8,128)(2,1)S(1)} %collective-permute-done.7.h.refs_1_, bf16[128,1376]{1,0:T(8,128)(2,1)S(1)} %collective-permute-done.8.h.refs_2_, ...), custom_call_target="tpu_custom_call" | custom-call | flops 1 | bytes 1 | tf_op jit(solution)/shard_map/project/pallas_call | solution.py:134
  99.4 0.5 collective-permute-start.15
  99.9 5.1 %collective-permute-done.16 = bf16[128,2048]{1,0:T(8,128)(2,1)} collective-permute-done((bf16[128,2048]{1,0:T(8,128)(2,1)}, bf16[128,2048]{1,0:T(8,128)(2,1)}, u32[]{:S(2)}, u32[]{:S(2)}) %collective-permute-start.16) | collective-permute-done | bytes 524320 | tf_op jit(solution)/shard_map/y1/ppermute | solution.py:21
  105.0 2.0 %add_convert_fusion.2 = bf16[128,2048]{1,0:T(8,128)(2,1)} fusion(f32[128,2048]{1,0:T(8,128)S(1)} %copy-done.9, bf16[128,2048]{1,0:T(8,128)(2,1)} %collective-permute-done.16), kind=kLoop, calls=%fused_computation.4 | loop fusion | flops 786432 | bytes 2097152 | tf_op jit(solution)/shard_map/convert_element_type | solution.py:322
  107.0 2.3 %add_convert_fusion.1 = bf16[128,2048]{1,0:T(8,128)(2,1)} fusion(bf16[128,2048]{1,0:T(8,128)(2,1)} %collective-permute-done.18, f32[128,2048]{1,0:T(8,128)S(1)} %copy-done.7, bf16[128,2048]{1,0:T(8,128)(2,1)} %collective-permute-done.17), kind=kLoop, calls=%fused_computation.3 | loop fusion | flops 1310720 | bytes 2621440 | tf_op jit(solution)/shard_map/convert_element_type | solution.py:325
  109.3 3.2 %collective-permute-start.23 = (bf16[128,2048]{1,0:T(8,128)(2,1)}, bf16[128,2048]{1,0:T(8,128)(2,1)}, u32[]{:S(2)}, u32[]{:S(2)}) collective-permute-start(bf16[128,2048]{1,0:T(8,128)(2,1)} %add_convert_fusion.1), channel_id=1, source_target_pairs={{0,8},{4,12},{8,0},{12,4},{1,9},{5,13},{9,1},{13,5},{2,10},{6,14},... | collective-permute-start | bytes 1572872 | tf_op jit(solution)/shard_map/r2/ppermute | solution.py:21
  112.5 2.9 %collective-permute-start.21 = (bf16[128,2048]{1,0:T(8,128)(2,1)}, bf16[128,2048]{1,0:T(8,128)(2,1)}, u32[]{:S(2)}, u32[]{:S(2)}) collective-permute-start(bf16[128,2048]{1,0:T(8,128)(2,1)} %get-tuple-element.100), channel_id=1, source_target_pairs={{0,2},{2,0},{1,3},{3,1},{4,6},{6,4},{5,7},{7,5},{8,10},{10,8},{9,1... | collective-permute-start | bytes 1572872 | tf_op jit(solution)/shard_map/y0/ppermute | solution.py:21
  115.5 0.2 pad_maximum_fusion
  115.7 0.1 dynamic-slice_bitcast_fusion.3
  115.8 1.2 maximum_bitcast_fusion
  117.0 2.6 %copy.11 = bf16[128,5504]{1,0:T(8,128)(2,1)} copy(bf16[128,5504]{0,1:T(8,128)(2,1)} %maximum_bitcast_fusion) | data formatting | bytes 2818048
  119.6 0.0 copy-start.3
  119.6 1.3 copy-done.3
  120.9 11.0 %adam_step.1 = (f32[1376,4096]{1,0:T(8,128)}, f32[1376,256]{1,0:T(8,128)}, f32[1376,256]{1,0:T(8,128)}) custom-call(s32[2]{0:T(128)S(1)} %pad_add_fusion.at, f32[688,256]{1,0:T(8,128)} %get-tuple-element.88.h_up, f32[688,256]{1,0:T(8,128)} %get-tuple-element.89.h_low, f32[688,256]{1,0:T(8,128)} %collective-permute-done.15.t_up, ...), custom_call_target="tpu_custom_call" | custom-call | flops 1 | bytes 1 | tf_op jit(solution)/shard_map/adam_step/pallas_call | solution.py:241
  131.9 3.1 %collective-permute-done.23 = bf16[128,2048]{1,0:T(8,128)(2,1)} collective-permute-done((bf16[128,2048]{1,0:T(8,128)(2,1)}, bf16[128,2048]{1,0:T(8,128)(2,1)}, u32[]{:S(2)}, u32[]{:S(2)}) %collective-permute-start.23) | collective-permute-done | bytes 524320 | tf_op jit(solution)/shard_map/r2/ppermute | solution.py:21
  135.0 2.5 %add_convert_fusion = bf16[128,2048]{1,0:T(8,128)(2,1)} fusion(bf16[128,2048]{1,0:T(8,128)(2,1)} %collective-permute-done.23, bf16[128,2048]{1,0:T(8,128)(2,1)} %collective-permute-done.22, f32[128,2048]{1,0:T(8,128)S(1)} %copy-done.5, bf16[128,2048]{1,0:T(8,128)(2,1)} %collective-permute-done.21), kind=kLoop, calls=%fused_computation.2 | loop fusion | flops 1835008 | bytes 3145728 | tf_op jit(solution)/shard_map/convert_element_type | solution.py:340
  (70 shorter events, 0.1 us)
Async XLA Ops:
  0.6 26.4 %collective-permute-start.1 = (bf16[128,2048]{1,0:T(8,128)(2,1)}, bf16[128,2048]{1,0:T(8,128)(2,1)}, u32[]{:S(2)}, u32[]{:S(2)}) collective-permute-start(bf16[128,2048]{1,0:T(8,128)(2,1)} %c), channel_id=1, source_target_pairs={{0,4},{4,0},{8,12},{12,8},{1,5},{5,1},{9,13},{13,9},{2,6},{6,2},{1... | collective-permute-start | bytes 1572872 | tf_op jit(solution)/shard_map/c1/ppermute | solution.py:21
  3.7 25.9 %collective-permute-start = (bf16[128,2048]{1,0:T(8,128)(2,1)}, bf16[128,2048]{1,0:T(8,128)(2,1)}, u32[]{:S(2)}, u32[]{:S(2)}) collective-permute-start(bf16[128,2048]{1,0:T(8,128)(2,1)} %c), channel_id=1, source_target_pairs={{0,8},{4,12},{8,0},{12,4},{1,9},{5,13},{9,1},{13,5},{2,10},{6,14},... | collective-permute-start | bytes 1572872 | tf_op jit(solution)/shard_map/c2/ppermute | solution.py:21
  6.3 23.3 %collective-permute-start.2 = (bf16[128,2048]{1,0:T(8,128)(2,1)}, bf16[128,2048]{1,0:T(8,128)(2,1)S(1)}, u32[]{:S(2)}, u32[]{:S(2)}) collective-permute-start(bf16[128,2048]{1,0:T(8,128)(2,1)} %c), channel_id=1, source_target_pairs={{0,2},{2,0},{1,3},{3,1},{4,6},{6,4},{5,7},{7,5},{8,10},{10,8},{9,1... | collective-permute-start | bytes 1572872 | tf_op jit(solution)/shard_map/x0/ppermute | solution.py:21
  7.8 3.2 %copy-start.1 = (bf16[2048,256]{1,0:T(8,128)(2,1)S(1)}, bf16[2048,256]{1,0:T(8,128)(2,1)}, u32[]{:S(2)}) copy-start(bf16[2048,256]{1,0:T(8,128)(2,1)} %basis.9) | copy-start | bytes 3145732
  11.9 19.0 %collective-permute-start.3 = (bf16[1024,256]{1,0:T(8,128)(2,1)}, bf16[1024,256]{1,0:T(8,128)(2,1)S(1)}, u32[]{:S(2)}, u32[]{:S(2)}) collective-permute-start(bf16[1024,256]{1,0:T(8,128)(2,1)} %constant_dynamic-slice_fusion.2), channel_id=1, source_target_pairs={{0,2},{2,0},{1,3},{3,1},{4,6},{6,4},{5,7},{7,5},{8,10},{10,8},{9,1... | collective-permute-start | bytes 1572872 | tf_op jit(solution)/shard_map/half/ppermute | solution.py:21
  12.5 4.2 %copy-start = (bf16[1376,4096]{1,0:T(8,128)(2,1)S(1)}, bf16[1376,4096]{1,0:T(8,128)(2,1)}, u32[]{:S(2)}) copy-start(bf16[1376,4096]{1,0:T(8,128)(2,1)} %w.15) | copy-start | bytes 33816580
  16.7 15.7 %copy-start.24 = (bf16[128,1376]{1,0:T(8,128)(2,1)S(1)}, bf16[128,1376]{1,0:T(8,128)(2,1)}, u32[]{:S(2)}) copy-start(bf16[128,1376]{1,0:T(8,128)(2,1)} %get-tuple-element.63) | copy-start | bytes 1056772
  16.7 17.6 %copy-start.10 = (bf16[128,2048]{1,0:T(8,128)(2,1)S(1)}, bf16[128,2048]{1,0:T(8,128)(2,1)}, u32[]{:S(2)}) copy-start(bf16[128,2048]{1,0:T(8,128)(2,1)} %c) | copy-start | bytes 1572868
  19.1 19.1 %copy-start.4 = (f32[128,2048]{1,0:T(8,128)}, f32[128,2048]{1,0:T(8,128)S(1)}, u32[]{:S(2)}) copy-start(f32[128,2048]{1,0:T(8,128)S(1)} %get-tuple-element.99) | copy-start | bytes 3145732
  30.9 2.8 %collective-permute-start.4 = (bf16[1024,256]{1,0:T(8,128)(2,1)S(1)}, bf16[1024,256]{1,0:T(8,128)(2,1)S(1)}, u32[]{:S(2)}, u32[]{:S(2)}) collective-permute-start(bf16[1024,256]{1,0:T(8,128)(2,1)S(1)} %collective-permute-done.3.got), channel_id=1, source_target_pairs={{0,1},{1,0},{2,3},{3,2},{4,5},{5,4},{6,7},{7,6},{8,9},{9,8},{10,11... | collective-permute-start | bytes 1572872 | tf_op jit(solution)/shard_map/basis/ppermute | solution.py:21
  30.9 14.9 %collective-permute-start.5 = (bf16[128,2048]{1,0:T(8,128)(2,1)}, bf16[128,2048]{1,0:T(8,128)(2,1)S(1)}, u32[]{:S(2)}, u32[]{:S(2)}) collective-permute-start(bf16[128,2048]{1,0:T(8,128)(2,1)} %collective-permute-done.c), channel_id=1, source_target_pairs={{0,2},{2,0},{1,3},{3,1},{4,6},{6,4},{5,7},{7,5},{8,10},{10,8},{9,1... | collective-permute-start | bytes 1572872 | tf_op jit(solution)/shard_map/x2/ppermute | solution.py:21
  32.4 18.0 %collective-permute-start.6 = (bf16[128,1376]{1,0:T(8,128)(2,1)S(1)}, bf16[128,1376]{1,0:T(8,128)(2,1)S(1)}, u32[]{:S(2)}, u32[]{:S(2)}) collective-permute-start(bf16[128,1376]{1,0:T(8,128)(2,1)S(1)} %copy-done.24), channel_id=1, source_target_pairs={{0,12},{4,8},{8,4},{12,0},{1,13},{5,9},{9,5},{13,1},{2,14},{6,10},... | collective-permute-start | bytes 1056776 | tf_op jit(solution)/shard_map/h3/ppermute | solution.py:21
  33.6 25.2 %collective-permute-start.9 = (bf16[128,2048]{1,0:T(8,128)(2,1)}, bf16[128,2048]{1,0:T(8,128)(2,1)S(1)}, u32[]{:S(2)}, u32[]{:S(2)}) collective-permute-start(bf16[128,2048]{1,0:T(8,128)(2,1)} %collective-permute-done.c), channel_id=1, source_target_pairs={{0,4},{4,0},{8,12},{12,8},{1,5},{5,1},{9,13},{13,9},{2,6},{6,2},{1... | collective-permute-start | bytes 1572872 | tf_op jit(solution)/shard_map/c3/ppermute | solution.py:21
  33.7 25.2 %collective-permute-start.10 = (bf16[128,2048]{1,0:T(8,128)(2,1)}, bf16[128,2048]{1,0:T(8,128)(2,1)S(1)}, u32[]{:S(2)}, u32[]{:S(2)}) collective-permute-start(bf16[128,2048]{1,0:T(8,128)(2,1)} %collective-permute-done.1.c), channel_id=1, source_target_pairs={{0,2},{2,0},{1,3},{3,1},{4,6},{6,4},{5,7},{7,5},{8,10},{10,8},{9,1... | collective-permute-start | bytes 1572872 | tf_op jit(solution)/shard_map/x1/ppermute | solution.py:21
  34.3 18.1 %slice-start = ((s8[11272192]{0:T(1024)(128)(4,1)}), s8[4194304]{0:T(1024)(128)(4,1)S(1)}, s32[]{:S(2)}) async-start(s8[11272192]{0:T(1024)(128)(4,1)} %bitcast.16), calls=%async_computation | async-start | bytes 8388608
  34.3 18.1 %slice-start.1 = ((s8[11272192]{0:T(1024)(128)(4,1)}), s8[4194304]{0:T(1024)(128)(4,1)S(1)}, s32[]{:S(2)}) async-start(s8[11272192]{0:T(1024)(128)(4,1)} %bitcast.16), calls=%async_computation.1 | async-start | bytes 8388608
  38.2 0.6 copy-start.13
  38.8 11.5 %copy-start.11 = (bf16[1376,128]{1,0:T(8,128)(2,1)}, bf16[1376,128]{1,0:T(8,128)(2,1)S(1)}, u32[]{:S(2)}) copy-start(bf16[1376,128]{1,0:T(8,128)(2,1)S(1)} %get-tuple-element.96) | copy-start | bytes 1056772
  45.8 4.6 %copy-start.23 = (bf16[128,1376]{1,0:T(8,128)(2,1)S(1)}, bf16[128,1376]{1,0:T(8,128)(2,1)}, u32[]{:S(2)}) copy-start(bf16[128,1376]{1,0:T(8,128)(2,1)} %get-tuple-element.65) | copy-start | bytes 1056772
  45.8 5.2 %copy-start.22 = (bf16[128,1376]{1,0:T(8,128)(2,1)S(1)}, bf16[128,1376]{1,0:T(8,128)(2,1)}, u32[]{:S(2)}) copy-start(bf16[128,1376]{1,0:T(8,128)(2,1)} %get-tuple-element.64) | copy-start | bytes 1056772
  45.8 6.5 %slice-start.2 = ((s8[11272192]{0:T(1024)(128)(4,1)}), s8[2883584]{0:T(1024)(128)(4,1)S(1)}, s32[]{:S(2)}) async-start(s8[11272192]{0:T(1024)(128)(4,1)} %bitcast.16), calls=%async_computation.2 | async-start | bytes 5767168
  50.4 4.3 %copy-start.15 = (bf16[128,256]{1,0:T(8,128)(2,1)}, bf16[128,256]{1,0:T(8,128)(2,1)S(1)}, u32[]{:S(2)}) copy-start(bf16[128,256]{1,0:T(8,128)(2,1)S(1)} %get-tuple-element.86.refs_6_) | copy-start | bytes 196612
  50.4 18.5 %collective-permute-start.8 = (bf16[128,1376]{1,0:T(8,128)(2,1)S(1)}, bf16[128,1376]{1,0:T(8,128)(2,1)S(1)}, u32[]{:S(2)}, u32[]{:S(2)}) collective-permute-start(bf16[128,1376]{1,0:T(8,128)(2,1)S(1)} %copy-done.23), channel_id=1, source_target_pairs={{0,8},{4,12},{8,0},{12,4},{1,9},{5,13},{9,1},{13,5},{2,10},{6,14},... | collective-permute-start | bytes 1056776 | tf_op jit(solution)/shard_map/h2/ppermute | solution.py:21
  51.0 23.0 %collective-permute-start.7 = (bf16[128,1376]{1,0:T(8,128)(2,1)S(1)}, bf16[128,1376]{1,0:T(8,128)(2,1)S(1)}, u32[]{:S(2)}, u32[]{:S(2)}) collective-permute-start(bf16[128,1376]{1,0:T(8,128)(2,1)S(1)} %copy-done.22), channel_id=1, source_target_pairs={{0,4},{4,0},{8,12},{12,8},{1,5},{5,1},{9,13},{13,9},{2,6},{6,2},{1... | collective-permute-start | bytes 1056776 | tf_op jit(solution)/shard_map/h1/ppermute | solution.py:21
  58.8 20.2 %collective-permute-start.11 = (bf16[128,2048]{1,0:T(8,128)(2,1)S(1)}, bf16[128,2048]{1,0:T(8,128)(2,1)S(1)}, u32[]{:S(2)}, u32[]{:S(2)}) collective-permute-start(bf16[128,2048]{1,0:T(8,128)(2,1)S(1)} %collective-permute-done.9.c), channel_id=1, source_target_pairs={{0,2},{2,0},{1,3},{3,1},{4,6},{6,4},{5,7},{7,5},{8,10},{10,8},{9,1... | collective-permute-start | bytes 1572872 | tf_op jit(solution)/shard_map/x3/ppermute | solution.py:21
  63.2 9.7 %copy-start.17 = (bf16[128,256]{1,0:T(8,128)(2,1)}, bf16[128,256]{1,0:T(8,128)(2,1)S(1)}, u32[]{:S(2)}) copy-start(bf16[128,256]{1,0:T(8,128)(2,1)S(1)} %get-tuple-element.85.refs_5_) | copy-start | bytes 196612
  68.9 21.1 %collective-permute-start.12 = (bf16[128,2048]{1,0:T(8,128)(2,1)S(1)}, bf16[128,2048]{1,0:T(8,128)(2,1)S(1)}, u32[]{:S(2)}, u32[]{:S(2)}) collective-permute-start(bf16[128,2048]{1,0:T(8,128)(2,1)S(1)} %get-tuple-element.80), channel_id=1, source_target_pairs={{0,2},{2,0},{1,3},{3,1},{4,6},{6,4},{5,7},{7,5},{8,10},{10,8},{9,1... | collective-permute-start | bytes 1572872 | tf_op jit(solution)/shard_map/y3/ppermute | solution.py:21
  70.4 16.3 %collective-permute-start.13 = (bf16[1376,128]{1,0:T(8,128)(2,1)S(1)}, bf16[1376,128]{1,0:T(8,128)(2,1)S(1)}, u32[]{:S(2)}, u32[]{:S(2)}) collective-permute-start(bf16[1376,128]{1,0:T(8,128)(2,1)S(1)} %get-tuple-element.81), channel_id=1, source_target_pairs={{0,8},{4,12},{8,0},{12,4},{1,9},{5,13},{9,1},{13,5},{2,10},{6,14},... | collective-permute-start | bytes 1056776 | tf_op jit(solution)/shard_map/a2/ppermute | solution.py:21
  73.0 1.0 copy-start.6
  73.9 16.0 %collective-permute-start.14 = (bf16[1376,128]{1,0:T(8,128)(2,1)S(1)}, bf16[1376,128]{1,0:T(8,128)(2,1)S(1)}, u32[]{:S(2)}, u32[]{:S(2)}) collective-permute-start(bf16[1376,128]{1,0:T(8,128)(2,1)S(1)} %get-tuple-element.82), channel_id=1, source_target_pairs={{0,4},{4,0},{8,12},{12,8},{1,5},{5,1},{9,13},{13,9},{2,6},{6,2},{1... | collective-permute-start | bytes 1056776 | tf_op jit(solution)/shard_map/a1/ppermute | solution.py:21
  78.0 1.0 copy-start.8
  79.0 20.4 %collective-permute-start.17 = (bf16[128,2048]{1,0:T(8,128)(2,1)}, bf16[128,2048]{1,0:T(8,128)(2,1)}, u32[]{:S(2)}, u32[]{:S(2)}) collective-permute-start(bf16[128,2048]{1,0:T(8,128)(2,1)} %get-tuple-element.93), channel_id=1, source_target_pairs={{0,2},{2,0},{1,3},{3,1},{4,6},{6,4},{5,7},{7,5},{8,10},{10,8},{9,1... | collective-permute-start | bytes 1572872 | tf_op jit(solution)/shard_map/y2/ppermute | solution.py:21
  83.4 7.7 %copy-start.19 = (bf16[128,256]{1,0:T(8,128)(2,1)}, bf16[128,256]{1,0:T(8,128)(2,1)S(1)}, u32[]{:S(2)}) copy-start(bf16[128,256]{1,0:T(8,128)(2,1)S(1)} %get-tuple-element.87.refs_7_) | copy-start | bytes 196612
  83.5 7.7 %copy-start.21 = (bf16[1376,128]{1,0:T(8,128)(2,1)}, bf16[1376,128]{1,0:T(8,128)(2,1)S(1)}, u32[]{:S(2)}) copy-start(bf16[1376,128]{1,0:T(8,128)(2,1)S(1)} %get-tuple-element.79) | copy-start | bytes 1056772
  86.7 4.5 %copy-start.25 = (bf16[1376,128]{1,0:T(8,128)(2,1)}, bf16[1376,128]{1,0:T(8,128)(2,1)S(1)}, u32[]{:S(2)}) copy-start(bf16[1376,128]{1,0:T(8,128)(2,1)S(1)} %collective-permute-done.13) | copy-start | bytes 1056772
  90.0 1.2 copy-start.27
  90.0 15.0 %collective-permute-start.16 = (bf16[128,2048]{1,0:T(8,128)(2,1)}, bf16[128,2048]{1,0:T(8,128)(2,1)}, u32[]{:S(2)}, u32[]{:S(2)}) collective-permute-start(bf16[128,2048]{1,0:T(8,128)(2,1)} %get-tuple-element.92), channel_id=1, source_target_pairs={{0,2},{2,0},{1,3},{3,1},{4,6},{6,4},{5,7},{7,5},{8,10},{10,8},{9,1... | collective-permute-start | bytes 1572872 | tf_op jit(solution)/shard_map/y1/ppermute | solution.py:21
  91.2 15.8 %collective-permute-start.18 = (bf16[128,2048]{1,0:T(8,128)(2,1)}, bf16[128,2048]{1,0:T(8,128)(2,1)}, u32[]{:S(2)}, u32[]{:S(2)}) collective-permute-start(bf16[128,2048]{1,0:T(8,128)(2,1)} %add_convert_fusion.3), channel_id=1, source_target_pairs={{0,4},{4,0},{8,12},{12,8},{1,5},{5,1},{9,13},{13,9},{2,6},{6,2},{1... | collective-permute-start | bytes 1572872 | tf_op jit(solution)/shard_map/r3/ppermute | solution.py:21
  91.3 13.7 %copy-start.9 = (f32[128,2048]{1,0:T(8,128)S(1)}, f32[128,2048]{1,0:T(8,128)}, u32[]{:S(2)}) copy-start(f32[128,2048]{1,0:T(8,128)} %copy-done.8) | copy-start | bytes 3145732
  91.3 21.3 %collective-permute-start.19 = (bf16[1376,128]{1,0:T(8,128)(2,1)}, bf16[1376,128]{1,0:T(8,128)(2,1)S(1)}, u32[]{:S(2)}, u32[]{:S(2)}) collective-permute-start(bf16[1376,128]{1,0:T(8,128)(2,1)} %copy-done.21), channel_id=1, source_target_pairs={{0,12},{4,8},{8,4},{12,0},{1,13},{5,9},{9,5},{13,1},{2,14},{6,10},... | collective-permute-start | bytes 1056776 | tf_op jit(solution)/shard_map/a3/ppermute | solution.py:21
  93.6 0.8 copy-start.14
  94.4 0.8 copy-start.16
  95.3 0.8 copy-start.18
  96.1 0.8 copy-start.20
  99.3 7.6 %copy-start.7 = (f32[128,2048]{1,0:T(8,128)S(1)}, f32[128,2048]{1,0:T(8,128)}, u32[]{:S(2)}) copy-start(f32[128,2048]{1,0:T(8,128)} %copy-done.6) | copy-start | bytes 3145732
  99.3 20.2 %collective-permute-start.20 = (f32[688,256]{1,0:T(8,128)}, f32[688,256]{1,0:T(8,128)}, u32[]{:S(2)}, u32[]{:S(2)}) collective-permute-start(f32[688,256]{1,0:T(8,128)} %get-tuple-element.89.h_low), channel_id=1, source_target_pairs={{0,1},{1,0},{2,3},{3,2},{4,5},{5,4},{6,7},{7,6},{8,9},{9,8},{10,11... | collective-permute-start | bytes 2113544 | tf_op jit(solution)/shard_map/rows/ppermute | solution.py:21
  99.4 20.2 %collective-permute-start.15 = (f32[688,256]{1,0:T(8,128)}, f32[688,256]{1,0:T(8,128)}, u32[]{:S(2)}, u32[]{:S(2)}) collective-permute-start(f32[688,256]{1,0:T(8,128)} %get-tuple-element.88.h_up), channel_id=1, source_target_pairs={{0,1},{1,0},{2,3},{3,2},{4,5},{5,4},{6,7},{7,6},{8,9},{9,8},{10,11... | collective-permute-start | bytes 2113544 | tf_op jit(solution)/shard_map/rows/ppermute | solution.py:21
  107.0 8.5 %copy-start.12 = (bf16[1376,128]{1,0:T(8,128)(2,1)S(1)}, bf16[1376,128]{1,0:T(8,128)(2,1)}, u32[]{:S(2)}) copy-start(bf16[1376,128]{1,0:T(8,128)(2,1)} %copy-done.11) | copy-start | bytes 1056772
  107.0 8.5 %copy-start.26 = (bf16[1376,128]{1,0:T(8,128)(2,1)S(1)}, bf16[1376,128]{1,0:T(8,128)(2,1)}, u32[]{:S(2)}) copy-start(bf16[1376,128]{1,0:T(8,128)(2,1)} %copy-done.25) | copy-start | bytes 1056772
  107.0 8.5 %copy-start.28 = (bf16[1376,128]{1,0:T(8,128)(2,1)S(1)}, bf16[1376,128]{1,0:T(8,128)(2,1)}, u32[]{:S(2)}) copy-start(bf16[1376,128]{1,0:T(8,128)(2,1)} %copy-done.27) | copy-start | bytes 1056772
  107.0 28.0 %collective-permute-start.22 = (bf16[128,2048]{1,0:T(8,128)(2,1)}, bf16[128,2048]{1,0:T(8,128)(2,1)}, u32[]{:S(2)}, u32[]{:S(2)}) collective-permute-start(bf16[128,2048]{1,0:T(8,128)(2,1)} %add_convert_fusion.2), channel_id=1, source_target_pairs={{0,4},{4,0},{8,12},{12,8},{1,5},{5,1},{9,13},{13,9},{2,6},{6,2},{1... | collective-permute-start | bytes 1572872 | tf_op jit(solution)/shard_map/r1/ppermute | solution.py:21
  109.3 25.7 %collective-permute-start.23 = (bf16[128,2048]{1,0:T(8,128)(2,1)}, bf16[128,2048]{1,0:T(8,128)(2,1)}, u32[]{:S(2)}, u32[]{:S(2)}) collective-permute-start(bf16[128,2048]{1,0:T(8,128)(2,1)} %add_convert_fusion.1), channel_id=1, source_target_pairs={{0,8},{4,12},{8,0},{12,4},{1,9},{5,13},{9,1},{13,5},{2,10},{6,14},... | collective-permute-start | bytes 1572872 | tf_op jit(solution)/shard_map/r2/ppermute | solution.py:21
  112.5 22.4 %collective-permute-start.21 = (bf16[128,2048]{1,0:T(8,128)(2,1)}, bf16[128,2048]{1,0:T(8,128)(2,1)}, u32[]{:S(2)}, u32[]{:S(2)}) collective-permute-start(bf16[128,2048]{1,0:T(8,128)(2,1)} %get-tuple-element.100), channel_id=1, source_target_pairs={{0,2},{2,0},{1,3},{3,1},{4,6},{6,4},{5,7},{7,5},{8,10},{10,8},{9,1... | collective-permute-start | bytes 1572872 | tf_op jit(solution)/shard_map/y0/ppermute | solution.py:21
  116.9 2.6 %copy-start.2 = (f32[1376,256]{1,0:T(8,128)S(1)}, f32[1376,256]{1,0:T(8,128)}, u32[]{:S(2)}) copy-start(f32[1376,256]{1,0:T(8,128)} %first.1) | copy-start | bytes 4227076
  119.6 1.4 copy-start.3
  120.9 14.0 %copy-start.5 = (f32[128,2048]{1,0:T(8,128)S(1)}, f32[128,2048]{1,0:T(8,128)}, u32[]{:S(2)}) copy-start(f32[128,2048]{1,0:T(8,128)} %copy-done.4) | copy-start | bytes 3145732

commit v3 on v2

--- a/solution.py
+++ b/solution.py
@@ -276,13 +276,13 @@
 
     c0 = cotangent
     c2 = swap(c0, "fsdp", 2, "c2")
-    c1 = swap(c0, "fsdp", 1, "c1")
     x0 = swap(c0, "tp", 1, "x0")
     h0, h1, h2, h3 = (own_units(k) for k in range(4))
     seen(h0)
+    c1 = swap(go(c0), "fsdp", 1, "c1")
     half = swap(halves(go(projector), 0, c)[0], "tp", 1, "half")
     p0, m0 = forward(at, h0, w_down)
-    seen(p0, c2, half, c1, x0)
+    seen(p0, c2, half, x0)
     x2 = swap(go(c2), "tp", 1, "x2")
     h3 = swap(go(h3), "fsdp", 3, "h3")
     c3 = swap(go(c2), "fsdp", 1, "c3")
@@ -335,9 +335,9 @@
         at, local, (go(other[0]), other[1]), tokens, first_moment, second_moment, projector, half, basis
     )
     seen(weight_step)
-    block_out = (
-        go(m0) + y0.astype(f32) + r1.astype(f32) + r2.astype(f32)
-    ).astype(bf16)
+    o0 = go(m0) + y0.astype(f32) + r1.astype(f32)
+    seen(o0)
+    block_out = (o0 + go(r2).astype(f32)).astype(bf16)
     return (block_out, acts_grad, weight_step, new_first, new_second)
 
 

time: 138 us -> 137 us (level)
  waiting for transfers between devices: 43.2 us -> 39.4 us
    ppermute x24, waiting for transfers between devices: 43.2 us -> 39.4 us  [swap(): return lax.ppermute(x, axis, [(i, i ^ bit) for i in range(n)])]
    add x0 -> x1, other arithmetic: none -> 1.4 us  [shards_line(): o0 = go(m0) + y0.astype(f32) + r1.astype(f32)]
  transfers between devices with their start and end apart: 24 -> 24, of which waited for: 10 -> 12; matrix products, arithmetic and copies ran while one was open for 10% -> 11% of each run, Pallas kernels for 29% -> 30%
where the time goes in v3:
time: 137 us; the launch traced here: 136 us
  Pallas kernels  40.3 us (29%)
  waiting for transfers between devices  39.4 us (29%)
  starting transfers between devices  26.3 us (19%)
  local copies, waits for them, and re-layouts  19.6 us (14%)
  other arithmetic  9.89 us (7%)
    ppermute x24, waiting for transfers between devices, swap(): return lax.ppermute(x, axis, [(i, i ^ bit) for i in range(n)])  39.4 us
    pallas_call x9, Pallas kernels, in_vmem(): pl.pallas_call(kernel, in_specs=[pl.BlockSpec(memory_space=pltpu.SMEM)] +...  29.4 us
    ppermute x24, starting transfers between devices, swap(): return lax.ppermute(x, axis, [(i, i ^ bit) for i in range(n)])  26.3 us
    unnamed x65, local copies, waits for them, and re-layouts  15.4 us
    pallas_call x1, Pallas kernels, adam_step(): pl.pallas_call(kernel, grid=(4,), in_specs=[pl.BlockSpec(memory_space=plt...  10.9 us
    dynamic_slice x1, local copies, waits for them, and re-layouts, own_units(): return lax.dynamic_slice_in_dim(hidden_acts, (z ^ k) * width, width, 1)  3.28 us
  transfers between devices with their start and end apart: 24, of which 12 were waited for; matrix products, arithmetic and copies ran while one was open for 11% of the time, Pallas kernels for 30%

profile of v3, /device:TPU:0, one launch (start us, length us, event | category | flops | bytes accessed | tf_op | source)
XLA Modules:
  0.0 136.4 jit_solution(10987659763993638509)
XLA Ops:
  0.6 4.1 %collective-permute-start = (bf16[128,2048]{1,0:T(8,128)(2,1)}, bf16[128,2048]{1,0:T(8,128)(2,1)}, u32[]{:S(2)}, u32[]{:S(2)}) collective-permute-start(bf16[128,2048]{1,0:T(8,128)(2,1)} %c), channel_id=1, source_target_pairs={{0,8},{4,12},{8,0},{12,4},{1,9},{5,13},{9,1},{13,5},{2,10},{6,14},... | collective-permute-start | bytes 1572872 | tf_op jit(solution)/shard_map/c2/ppermute | solution.py:21
  4.7 1.5 %collective-permute-start.2 = (bf16[128,2048]{1,0:T(8,128)(2,1)}, bf16[128,2048]{1,0:T(8,128)(2,1)}, u32[]{:S(2)}, u32[]{:S(2)}) collective-permute-start(bf16[128,2048]{1,0:T(8,128)(2,1)} %c), channel_id=1, source_target_pairs={{0,2},{2,0},{1,3},{3,1},{4,6},{6,4},{5,7},{7,5},{8,10},{10,8},{9,1... | collective-permute-start | bytes 1572872 | tf_op jit(solution)/shard_map/x0/ppermute | solution.py:21
  6.2 3.3 %constant_dynamic-slice_fusion = (bf16[128,1376]{1,0:T(8,128)(2,1)}, bf16[128,1376]{1,0:T(8,128)(2,1)}, bf16[128,1376]{1,0:T(8,128)(2,1)S(1)}, bf16[128,1376]{1,0:T(8,128)(2,1)}) fusion(bf16[128,5504]{1,0:T(8,128)(2,1)} %param.6, s32[]{:T(128)S(6)} %select_n.32, s32[]{:T(128)S(6)} %select_n.29, s32[]{:T(128)S(6)} %select_n.28, s32[]{:T(128)S(6)} %select_n.31), kind=kLoop, calls=%fused_computation.11 | loop fusion | bytes 2818064 | tf_op jit(solution)/shard_map/dynamic_slice | solution.py:275
  9.5 0.8 constant_dynamic-slice_fusion.2
  10.3 0.5 collective-permute-start.3
  10.9 1.6 %collective-permute-start.1 = (bf16[128,2048]{1,0:T(8,128)(2,1)S(1)}, bf16[128,2048]{1,0:T(8,128)(2,1)}, u32[]{:S(2)}, u32[]{:S(2)}) collective-permute-start(bf16[128,2048]{1,0:T(8,128)(2,1)S(1)} %copy-done.10), channel_id=1, source_target_pairs={{0,4},{4,0},{8,12},{12,8},{1,5},{5,1},{9,13},{13,9},{2,6},{6,2},{1... | collective-permute-start | bytes 1572872 | tf_op jit(solution)/shard_map/c1/ppermute | solution.py:21
  12.5 0.1 pad_add_fusion.at
  12.5 4.2 %copy-done = bf16[1376,4096]{1,0:T(8,128)(2,1)S(1)} copy-done((bf16[1376,4096]{1,0:T(8,128)(2,1)S(1)}, bf16[1376,4096]{1,0:T(8,128)(2,1)}, u32[]{:S(2)}) %copy-start) | copy-done | bytes 11272216
  16.7 2.4 %forward.4 = (bf16[128,2048]{1,0:T(8,128)(2,1)}, f32[128,2048]{1,0:T(8,128)S(1)}) custom-call(s32[2]{0:T(128)S(1)} %pad_add_fusion.at, bf16[128,1376]{1,0:T(8,128)(2,1)S(1)} %get-tuple-element.118.h.refs_0_, bf16[1376,4096]{1,0:T(8,128)(2,1)S(1)} %copy-done), custom_call_target="tpu_custom_call" | custom-call | flops 1 | bytes 1 | tf_op jit(solution)/shard_map/forward/pallas_call | solution.py:134
  19.1 9.2 %collective-permute-done.c = bf16[128,2048]{1,0:T(8,128)(2,1)} collective-permute-done((bf16[128,2048]{1,0:T(8,128)(2,1)}, bf16[128,2048]{1,0:T(8,128)(2,1)}, u32[]{:S(2)}, u32[]{:S(2)}) %collective-permute-start) | collective-permute-done | bytes 524320 | tf_op jit(solution)/shard_map/c2/ppermute | solution.py:21
  28.3 1.2 collective-permute-done.3.got
  29.6 1.5 %collective-permute-start.5 = (bf16[128,2048]{1,0:T(8,128)(2,1)}, bf16[128,2048]{1,0:T(8,128)(2,1)S(1)}, u32[]{:S(2)}, u32[]{:S(2)}) collective-permute-start(bf16[128,2048]{1,0:T(8,128)(2,1)} %collective-permute-done.c), channel_id=1, source_target_pairs={{0,2},{2,0},{1,3},{3,1},{4,6},{6,4},{5,7},{7,5},{8,10},{10,8},{9,1... | collective-permute-start | bytes 1572872 | tf_op jit(solution)/shard_map/x2/ppermute | solution.py:21
  31.1 2.4 %collective-permute-start.6 = (bf16[128,1376]{1,0:T(8,128)(2,1)S(1)}, bf16[128,1376]{1,0:T(8,128)(2,1)S(1)}, u32[]{:S(2)}, u32[]{:S(2)}) collective-permute-start(bf16[128,1376]{1,0:T(8,128)(2,1)S(1)} %copy-done.24), channel_id=1, source_target_pairs={{0,12},{4,8},{8,4},{12,0},{1,13},{5,9},{9,5},{13,1},{2,14},{6,10},... | collective-permute-start | bytes 1056776 | tf_op jit(solution)/shard_map/h3/ppermute | solution.py:21
  33.4 0.4 collective-permute-done.1.c
  33.9 1.5 %collective-permute-start.10 = (bf16[128,2048]{1,0:T(8,128)(2,1)}, bf16[128,2048]{1,0:T(8,128)(2,1)S(1)}, u32[]{:S(2)}, u32[]{:S(2)}) collective-permute-start(bf16[128,2048]{1,0:T(8,128)(2,1)} %collective-permute-done.1.c), channel_id=1, source_target_pairs={{0,2},{2,0},{1,3},{3,1},{4,6},{6,4},{5,7},{7,5},{8,10},{10,8},{9,1... | collective-permute-start | bytes 1572872 | tf_op jit(solution)/shard_map/x1/ppermute | solution.py:21
  35.4 4.4 %backward.4 = (bf16[1376,128]{1,0:T(8,128)(2,1)S(1)}, bf16[128,256]{1,0:T(8,128)(2,1)S(1)}) custom-call(s32[2]{0:T(128)S(1)} %pad_add_fusion.at, bf16[128,2048]{1,0:T(8,128)(2,1)S(1)} %copy-done.10, bf16[128,2048]{1,0:T(8,128)(2,1)} %collective-permute-done.2.x, bf16[1376,4096]{1,0:T(8,128)(2,1)S(1)} %copy-done, bf16[2048,256]{1,0:T(8,128)(2,1)S(1)} %copy-done.1, ...), custom_call_target="tpu_custom_call" | custom-call | flops 1 | bytes 1 | tf_op jit(solution)/shard_map/backward/pallas_call | solution.py:134
  39.9 4.6 %collective-permute-done.5.x = bf16[128,2048]{1,0:T(8,128)(2,1)S(1)} collective-permute-done((bf16[128,2048]{1,0:T(8,128)(2,1)}, bf16[128,2048]{1,0:T(8,128)(2,1)S(1)}, u32[]{:S(2)}, u32[]{:S(2)}) %collective-permute-start.5) | collective-permute-done | bytes 524320 | tf_op jit(solution)/shard_map/x2/ppermute | solution.py:21
  44.5 4.5 %backward.5 = (bf16[1376,128]{1,0:T(8,128)(2,1)S(1)}, bf16[128,256]{1,0:T(8,128)(2,1)S(1)}) custom-call(s32[2]{0:T(128)S(1)} %pad_add_fusion.at, bf16[128,2048]{1,0:T(8,128)(2,1)} %collective-permute-done.c, bf16[128,2048]{1,0:T(8,128)(2,1)S(1)} %collective-permute-done.5.x, bf16[1376,4096]{1,0:T(8,128)(2,1)S(1)} %copy-done, ...), custom_call_target="tpu_custom_call" | custom-call | flops 1 | bytes 1 | tf_op jit(solution)/shard_map/backward/pallas_call | solution.py:134
  49.0 0.6 copy-done.15
  49.6 1.0 collective-permute-start.8
  50.6 1.9 %collective-permute-start.7 = (bf16[128,1376]{1,0:T(8,128)(2,1)S(1)}, bf16[128,1376]{1,0:T(8,128)(2,1)S(1)}, u32[]{:S(2)}, u32[]{:S(2)}) collective-permute-start(bf16[128,1376]{1,0:T(8,128)(2,1)S(1)} %copy-done.22), channel_id=1, source_target_pairs={{0,4},{4,0},{8,12},{12,8},{1,5},{5,1},{9,13},{13,9},{2,6},{6,2},{1... | collective-permute-start | bytes 1056776 | tf_op jit(solution)/shard_map/h1/ppermute | solution.py:21
  52.6 2.4 %forward.5 = (bf16[128,2048]{1,0:T(8,128)(2,1)S(1)}, f32[128,2048]{1,0:T(8,128)S(1)}) custom-call(s32[2]{0:T(128)S(1)} %pad_add_fusion.at, bf16[128,1376]{1,0:T(8,128)(2,1)S(1)} %collective-permute-done.6.h.refs_3_, bf16[1376,4096]{1,0:T(8,128)(2,1)S(1)} %copy-done), custom_call_target="tpu_custom_call" | custom-call | flops 1 | bytes 1 | tf_op jit(solution)/shard_map/forward/pallas_call | solution.py:134
  54.9 2.2 %collective-permute-done.9.c = bf16[128,2048]{1,0:T(8,128)(2,1)S(1)} collective-permute-done((bf16[128,2048]{1,0:T(8,128)(2,1)}, bf16[128,2048]{1,0:T(8,128)(2,1)S(1)}, u32[]{:S(2)}, u32[]{:S(2)}) %collective-permute-start.9) | collective-permute-done | bytes 524320 | tf_op jit(solution)/shard_map/c3/ppermute | solution.py:21
  57.2 4.6 %backward.6 = (bf16[1376,128]{1,0:T(8,128)(2,1)S(1)}, bf16[128,256]{1,0:T(8,128)(2,1)S(1)}) custom-call(s32[2]{0:T(128)S(1)} %pad_add_fusion.at, bf16[128,2048]{1,0:T(8,128)(2,1)} %collective-permute-done.1.c, bf16[128,2048]{1,0:T(8,128)(2,1)S(1)} %collective-permute-done.10.x, bf16[1376,4096]{1,0:T(8,128)(2,1)S(1)} %copy-done, ...), custom_call_target="tpu_custom_call" | custom-call | flops 1 | bytes 1 | tf_op jit(solution)/shard_map/backward/pallas_call | solution.py:134
  61.8 0.6 copy-done.17
  62.4 5.7 %collective-permute-done.8.h.refs_2_ = bf16[128,1376]{1,0:T(8,128)(2,1)S(1)} collective-permute-done((bf16[128,1376]{1,0:T(8,128)(2,1)S(1)}, bf16[128,1376]{1,0:T(8,128)(2,1)S(1)}, u32[]{:S(2)}, u32[]{:S(2)}) %collective-permute-start.8) | collective-permute-done | bytes 352288 | tf_op jit(solution)/shard_map/h2/ppermute | solution.py:21
  68.1 1.5 %collective-permute-start.12 = (bf16[128,2048]{1,0:T(8,128)(2,1)S(1)}, bf16[128,2048]{1,0:T(8,128)(2,1)S(1)}, u32[]{:S(2)}, u32[]{:S(2)}) collective-permute-start(bf16[128,2048]{1,0:T(8,128)(2,1)S(1)} %get-tuple-element.83), channel_id=1, source_target_pairs={{0,2},{2,0},{1,3},{3,1},{4,6},{6,4},{5,7},{7,5},{8,10},{10,8},{9,1... | collective-permute-start | bytes 1572872 | tf_op jit(solution)/shard_map/y3/ppermute | solution.py:21
  69.6 2.5 %forward.6 = (bf16[128,2048]{1,0:T(8,128)(2,1)}, f32[128,2048]{1,0:T(8,128)S(1)}) custom-call(s32[2]{0:T(128)S(1)} %pad_add_fusion.at, bf16[128,1376]{1,0:T(8,128)(2,1)S(1)} %collective-permute-done.8.h.refs_2_, bf16[1376,4096]{1,0:T(8,128)(2,1)S(1)} %copy-done), custom_call_target="tpu_custom_call" | custom-call | flops 1 | bytes 1 | tf_op jit(solution)/shard_map/forward/pallas_call | solution.py:134
  72.1 0.0 copy-start.6
  72.1 1.0 copy-done.6
  73.1 2.7 %collective-permute-start.14 = (bf16[1376,128]{1,0:T(8,128)(2,1)S(1)}, bf16[1376,128]{1,0:T(8,128)(2,1)S(1)}, u32[]{:S(2)}, u32[]{:S(2)}) collective-permute-start(bf16[1376,128]{1,0:T(8,128)(2,1)S(1)} %get-tuple-element.85), channel_id=1, source_target_pairs={{0,4},{4,0},{8,12},{12,8},{1,5},{5,1},{9,13},{13,9},{2,6},{6,2},{1... | collective-permute-start | bytes 1056776 | tf_op jit(solution)/shard_map/a1/ppermute | solution.py:21
  75.8 2.4 %forward.7 = (bf16[128,2048]{1,0:T(8,128)(2,1)}, f32[128,2048]{1,0:T(8,128)S(1)}) custom-call(s32[2]{0:T(128)S(1)} %pad_add_fusion.at, bf16[128,1376]{1,0:T(8,128)(2,1)S(1)} %collective-permute-done.7.h.refs_1_, bf16[1376,4096]{1,0:T(8,128)(2,1)S(1)} %bitcast.17), custom_call_target="tpu_custom_call" | custom-call | flops 1 | bytes 1 | tf_op jit(solution)/shard_map/forward/pallas_call | solution.py:134
  78.2 1.0 copy-done.8
  79.2 0.6 collective-permute-start.17
  79.8 3.9 %backward.7 = (bf16[1376,128]{1,0:T(8,128)(2,1)S(1)}, bf16[128,256]{1,0:T(8,128)(2,1)S(1)}) custom-call(s32[2]{0:T(128)S(1)} %pad_add_fusion.at, bf16[128,2048]{1,0:T(8,128)(2,1)S(1)} %collective-permute-done.9.c, bf16[128,2048]{1,0:T(8,128)(2,1)S(1)} %collective-permute-done.11.x, bf16[1376,4096]{1,0:T(8,128)(2,1)S(1)} %bitcast.17, ...), custom_call_target="tpu_custom_call" | custom-call | flops 1 | bytes 1 | tf_op jit(solution)/shard_map/backward/pallas_call | solution.py:134
  83.7 0.6 copy-done.19
  84.3 2.0 %collective-permute-done.13 = bf16[1376,128]{1,0:T(8,128)(2,1)S(1)} collective-permute-done((bf16[1376,128]{1,0:T(8,128)(2,1)S(1)}, bf16[1376,128]{1,0:T(8,128)(2,1)S(1)}, u32[]{:S(2)}, u32[]{:S(2)}) %collective-permute-start.13) | collective-permute-done | bytes 352288 | tf_op jit(solution)/shard_map/a2/ppermute | solution.py:21
  86.3 3.6 %collective-permute-done.14 = bf16[1376,128]{1,0:T(8,128)(2,1)S(1)} collective-permute-done((bf16[1376,128]{1,0:T(8,128)(2,1)S(1)}, bf16[1376,128]{1,0:T(8,128)(2,1)S(1)}, u32[]{:S(2)}, u32[]{:S(2)}) %collective-permute-start.14) | collective-permute-done | bytes 352288 | tf_op jit(solution)/shard_map/a1/ppermute | solution.py:21
  89.9 0.3 collective-permute-start.16
  90.2 0.9 add_convert_fusion.3
  91.2 0.1 collective-permute-start.18
  91.3 1.6 %collective-permute-start.19 = (bf16[1376,128]{1,0:T(8,128)(2,1)}, bf16[1376,128]{1,0:T(8,128)(2,1)S(1)}, u32[]{:S(2)}, u32[]{:S(2)}) collective-permute-start(bf16[1376,128]{1,0:T(8,128)(2,1)} %copy-done.21), channel_id=1, source_target_pairs={{0,12},{4,8},{8,4},{12,0},{1,13},{5,9},{9,5},{13,1},{2,14},{6,10},... | collective-permute-start | bytes 1056776 | tf_op jit(solution)/shard_map/a3/ppermute | solution.py:21
  92.9 0.8 copy-done.14
  93.7 0.8 copy-done.16
  94.5 0.8 copy-done.18
  95.4 0.8 copy-done.20
  96.2 2.4 %project.1 = (f32[688,256]{1,0:T(8,128)}, f32[688,256]{1,0:T(8,128)}) custom-call(s32[2]{0:T(128)S(1)} %pad_add_fusion.at, bf16[128,1376]{1,0:T(8,128)(2,1)S(1)} %get-tuple-element.118.h.refs_0_, bf16[128,1376]{1,0:T(8,128)(2,1)S(1)} %collective-permute-done.7.h.refs_1_, bf16[128,1376]{1,0:T(8,128)(2,1)S(1)} %collective-permute-done.8.h.refs_2_, ...), custom_call_target="tpu_custom_call" | custom-call | flops 1 | bytes 1 | tf_op jit(solution)/shard_map/project/pallas_call | solution.py:134
  98.6 0.5 collective-permute-start.15
  99.1 5.6 %collective-permute-done.16 = bf16[128,2048]{1,0:T(8,128)(2,1)} collective-permute-done((bf16[128,2048]{1,0:T(8,128)(2,1)}, bf16[128,2048]{1,0:T(8,128)(2,1)}, u32[]{:S(2)}, u32[]{:S(2)}) %collective-permute-start.16) | collective-permute-done | bytes 524320 | tf_op jit(solution)/shard_map/y1/ppermute | solution.py:21
  104.7 2.0 %add_convert_fusion.2 = bf16[128,2048]{1,0:T(8,128)(2,1)} fusion(f32[128,2048]{1,0:T(8,128)S(1)} %copy-done.9, bf16[128,2048]{1,0:T(8,128)(2,1)} %collective-permute-done.16), kind=kLoop, calls=%fused_computation.5 | loop fusion | flops 786432 | bytes 2097152 | tf_op jit(solution)/shard_map/convert_element_type | solution.py:322
  106.7 3.1 %collective-permute-done.18 = bf16[128,2048]{1,0:T(8,128)(2,1)} collective-permute-done((bf16[128,2048]{1,0:T(8,128)(2,1)}, bf16[128,2048]{1,0:T(8,128)(2,1)}, u32[]{:S(2)}, u32[]{:S(2)}) %collective-permute-start.18) | collective-permute-done | bytes 524320 | tf_op jit(solution)/shard_map/r3/ppermute | solution.py:21
  109.8 2.2 %add_convert_fusion.1 = bf16[128,2048]{1,0:T(8,128)(2,1)} fusion(bf16[128,2048]{1,0:T(8,128)(2,1)} %collective-permute-done.18, f32[128,2048]{1,0:T(8,128)S(1)} %copy-done.7, bf16[128,2048]{1,0:T(8,128)(2,1)} %collective-permute-done.17), kind=kLoop, calls=%fused_computation.4 | loop fusion | flops 1310720 | bytes 2621440 | tf_op jit(solution)/shard_map/convert_element_type | solution.py:325
  112.0 0.1 collective-permute-done.19
  112.1 3.0 %collective-permute-start.21 = (bf16[128,2048]{1,0:T(8,128)(2,1)}, bf16[128,2048]{1,0:T(8,128)(2,1)}, u32[]{:S(2)}, u32[]{:S(2)}) collective-permute-start(bf16[128,2048]{1,0:T(8,128)(2,1)} %get-tuple-element.103), channel_id=1, source_target_pairs={{0,2},{2,0},{1,3},{3,1},{4,6},{6,4},{5,7},{7,5},{8,10},{10,8},{9,1... | collective-permute-start | bytes 1572872 | tf_op jit(solution)/shard_map/y0/ppermute | solution.py:21
  115.1 0.2 pad_maximum_fusion
  115.3 0.1 dynamic-slice_bitcast_fusion.3
  115.4 1.2 maximum_bitcast_fusion
  116.6 2.6 %copy.11 = bf16[128,5504]{1,0:T(8,128)(2,1)} copy(bf16[128,5504]{0,1:T(8,128)(2,1)} %maximum_bitcast_fusion) | data formatting | bytes 2818048
  119.2 0.0 copy-start.3
  119.2 1.3 copy-done.3
  120.6 10.9 %adam_step.1 = (f32[1376,4096]{1,0:T(8,128)}, f32[1376,256]{1,0:T(8,128)}, f32[1376,256]{1,0:T(8,128)}) custom-call(s32[2]{0:T(128)S(1)} %pad_add_fusion.at, f32[688,256]{1,0:T(8,128)} %get-tuple-element.91.h_up, f32[688,256]{1,0:T(8,128)} %get-tuple-element.92.h_low, f32[688,256]{1,0:T(8,128)} %collective-permute-done.15.t_up, ...), custom_call_target="tpu_custom_call" | custom-call | flops 1 | bytes 1 | tf_op jit(solution)/shard_map/adam_step/pallas_call | solution.py:241
  131.5 1.4 %convert_add_fusion = f32[128,2048]{1,0:T(8,128)S(1)} fusion(bf16[128,2048]{1,0:T(8,128)(2,1)} %collective-permute-done.22, f32[128,2048]{1,0:T(8,128)S(1)} %copy-done.5, bf16[128,2048]{1,0:T(8,128)(2,1)} %collective-permute-done.21), kind=kLoop, calls=%fused_computation.3 | loop fusion | flops 1048576 | bytes 3145728 | tf_op jit(solution)/shard_map/add | solution.py:338
  133.0 1.5 %collective-permute-done.23 = bf16[128,2048]{1,0:T(8,128)(2,1)} collective-permute-done((bf16[128,2048]{1,0:T(8,128)(2,1)}, bf16[128,2048]{1,0:T(8,128)(2,1)}, u32[]{:S(2)}, u32[]{:S(2)}) %collective-permute-start.23) | collective-permute-done | bytes 524320 | tf_op jit(solution)/shard_map/r2/ppermute | solution.py:21
  134.5 1.9 %add_convert_fusion = bf16[128,2048]{1,0:T(8,128)(2,1)} fusion(f32[128,2048]{1,0:T(8,128)S(1)} %convert_add_fusion, bf16[128,2048]{1,0:T(8,128)(2,1)} %collective-permute-done.23), kind=kLoop, calls=%fused_computation.2 | loop fusion | flops 786432 | bytes 2097152 | tf_op jit(solution)/shard_map/convert_element_type | solution.py:340
  (71 shorter events, 0.2 us)
Async XLA Ops:
  0.6 27.7 %collective-permute-start = (bf16[128,2048]{1,0:T(8,128)(2,1)}, bf16[128,2048]{1,0:T(8,128)(2,1)}, u32[]{:S(2)}, u32[]{:S(2)}) collective-permute-start(bf16[128,2048]{1,0:T(8,128)(2,1)} %c), channel_id=1, source_target_pairs={{0,8},{4,12},{8,0},{12,4},{1,9},{5,13},{9,1},{13,5},{2,10},{6,14},... | collective-permute-start | bytes 1572872 | tf_op jit(solution)/shard_map/c2/ppermute | solution.py:21
  4.7 23.6 %collective-permute-start.2 = (bf16[128,2048]{1,0:T(8,128)(2,1)}, bf16[128,2048]{1,0:T(8,128)(2,1)}, u32[]{:S(2)}, u32[]{:S(2)}) collective-permute-start(bf16[128,2048]{1,0:T(8,128)(2,1)} %c), channel_id=1, source_target_pairs={{0,2},{2,0},{1,3},{3,1},{4,6},{6,4},{5,7},{7,5},{8,10},{10,8},{9,1... | collective-permute-start | bytes 1572872 | tf_op jit(solution)/shard_map/x0/ppermute | solution.py:21
  6.2 3.3 %copy-start.1 = (bf16[2048,256]{1,0:T(8,128)(2,1)S(1)}, bf16[2048,256]{1,0:T(8,128)(2,1)}, u32[]{:S(2)}) copy-start(bf16[2048,256]{1,0:T(8,128)(2,1)} %basis.9) | copy-start | bytes 3145732
  6.2 4.6 %copy-start.10 = (bf16[128,2048]{1,0:T(8,128)(2,1)S(1)}, bf16[128,2048]{1,0:T(8,128)(2,1)}, u32[]{:S(2)}) copy-start(bf16[128,2048]{1,0:T(8,128)(2,1)} %c) | copy-start | bytes 1572868
  10.3 19.2 %collective-permute-start.3 = (bf16[1024,256]{1,0:T(8,128)(2,1)}, bf16[1024,256]{1,0:T(8,128)(2,1)S(1)}, u32[]{:S(2)}, u32[]{:S(2)}) collective-permute-start(bf16[1024,256]{1,0:T(8,128)(2,1)} %constant_dynamic-slice_fusion.2), channel_id=1, source_target_pairs={{0,2},{2,0},{1,3},{3,1},{4,6},{6,4},{5,7},{7,5},{8,10},{10,8},{9,1... | collective-permute-start | bytes 1572872 | tf_op jit(solution)/shard_map/half/ppermute | solution.py:21
  10.9 23.0 %collective-permute-start.1 = (bf16[128,2048]{1,0:T(8,128)(2,1)S(1)}, bf16[128,2048]{1,0:T(8,128)(2,1)}, u32[]{:S(2)}, u32[]{:S(2)}) collective-permute-start(bf16[128,2048]{1,0:T(8,128)(2,1)S(1)} %copy-done.10), channel_id=1, source_target_pairs={{0,4},{4,0},{8,12},{12,8},{1,5},{5,1},{9,13},{13,9},{2,6},{6,2},{1... | collective-permute-start | bytes 1572872 | tf_op jit(solution)/shard_map/c1/ppermute | solution.py:21
  12.5 4.2 %copy-start = (bf16[1376,4096]{1,0:T(8,128)(2,1)S(1)}, bf16[1376,4096]{1,0:T(8,128)(2,1)}, u32[]{:S(2)}) copy-start(bf16[1376,4096]{1,0:T(8,128)(2,1)} %w.15) | copy-start | bytes 33816580
  16.7 14.3 %copy-start.24 = (bf16[128,1376]{1,0:T(8,128)(2,1)S(1)}, bf16[128,1376]{1,0:T(8,128)(2,1)}, u32[]{:S(2)}) copy-start(bf16[128,1376]{1,0:T(8,128)(2,1)} %get-tuple-element.66) | copy-start | bytes 1056772
  19.1 20.7 %copy-start.4 = (f32[128,2048]{1,0:T(8,128)}, f32[128,2048]{1,0:T(8,128)S(1)}, u32[]{:S(2)}) copy-start(f32[128,2048]{1,0:T(8,128)S(1)} %get-tuple-element.102) | copy-start | bytes 3145732
  29.6 4.3 %collective-permute-start.4 = (bf16[1024,256]{1,0:T(8,128)(2,1)S(1)}, bf16[1024,256]{1,0:T(8,128)(2,1)S(1)}, u32[]{:S(2)}, u32[]{:S(2)}) collective-permute-start(bf16[1024,256]{1,0:T(8,128)(2,1)S(1)} %collective-permute-done.3.got), channel_id=1, source_target_pairs={{0,1},{1,0},{2,3},{3,2},{4,5},{5,4},{6,7},{7,6},{8,9},{9,8},{10,11... | collective-permute-start | bytes 1572872 | tf_op jit(solution)/shard_map/basis/ppermute | solution.py:21
  29.6 14.9 %collective-permute-start.5 = (bf16[128,2048]{1,0:T(8,128)(2,1)}, bf16[128,2048]{1,0:T(8,128)(2,1)S(1)}, u32[]{:S(2)}, u32[]{:S(2)}) collective-permute-start(bf16[128,2048]{1,0:T(8,128)(2,1)} %collective-permute-done.c), channel_id=1, source_target_pairs={{0,2},{2,0},{1,3},{3,1},{4,6},{6,4},{5,7},{7,5},{8,10},{10,8},{9,1... | collective-permute-start | bytes 1572872 | tf_op jit(solution)/shard_map/x2/ppermute | solution.py:21
  31.1 18.6 %collective-permute-start.6 = (bf16[128,1376]{1,0:T(8,128)(2,1)S(1)}, bf16[128,1376]{1,0:T(8,128)(2,1)S(1)}, u32[]{:S(2)}, u32[]{:S(2)}) collective-permute-start(bf16[128,1376]{1,0:T(8,128)(2,1)S(1)} %copy-done.24), channel_id=1, source_target_pairs={{0,12},{4,8},{8,4},{12,0},{1,13},{5,9},{9,5},{13,1},{2,14},{6,10},... | collective-permute-start | bytes 1056776 | tf_op jit(solution)/shard_map/h3/ppermute | solution.py:21
  33.4 23.7 %collective-permute-start.9 = (bf16[128,2048]{1,0:T(8,128)(2,1)}, bf16[128,2048]{1,0:T(8,128)(2,1)S(1)}, u32[]{:S(2)}, u32[]{:S(2)}) collective-permute-start(bf16[128,2048]{1,0:T(8,128)(2,1)} %collective-permute-done.c), channel_id=1, source_target_pairs={{0,4},{4,0},{8,12},{12,8},{1,5},{5,1},{9,13},{13,9},{2,6},{6,2},{1... | collective-permute-start | bytes 1572872 | tf_op jit(solution)/shard_map/c3/ppermute | solution.py:21
  33.9 23.3 %collective-permute-start.10 = (bf16[128,2048]{1,0:T(8,128)(2,1)}, bf16[128,2048]{1,0:T(8,128)(2,1)S(1)}, u32[]{:S(2)}, u32[]{:S(2)}) collective-permute-start(bf16[128,2048]{1,0:T(8,128)(2,1)} %collective-permute-done.1.c), channel_id=1, source_target_pairs={{0,2},{2,0},{1,3},{3,1},{4,6},{6,4},{5,7},{7,5},{8,10},{10,8},{9,1... | collective-permute-start | bytes 1572872 | tf_op jit(solution)/shard_map/x1/ppermute | solution.py:21
  39.8 9.1 %copy-start.11 = (bf16[1376,128]{1,0:T(8,128)(2,1)}, bf16[1376,128]{1,0:T(8,128)(2,1)S(1)}, u32[]{:S(2)}) copy-start(bf16[1376,128]{1,0:T(8,128)(2,1)S(1)} %get-tuple-element.99) | copy-start | bytes 1056772
  39.9 9.1 %copy-start.13 = (bf16[128,256]{1,0:T(8,128)(2,1)}, bf16[128,256]{1,0:T(8,128)(2,1)S(1)}, u32[]{:S(2)}) copy-start(bf16[128,256]{1,0:T(8,128)(2,1)S(1)} %get-tuple-element.87.refs_4_) | copy-start | bytes 196612
  44.5 5.1 %copy-start.23 = (bf16[128,1376]{1,0:T(8,128)(2,1)S(1)}, bf16[128,1376]{1,0:T(8,128)(2,1)}, u32[]{:S(2)}) copy-start(bf16[128,1376]{1,0:T(8,128)(2,1)} %get-tuple-element.68) | copy-start | bytes 1056772
  44.5 6.1 %copy-start.22 = (bf16[128,1376]{1,0:T(8,128)(2,1)S(1)}, bf16[128,1376]{1,0:T(8,128)(2,1)}, u32[]{:S(2)}) copy-start(bf16[128,1376]{1,0:T(8,128)(2,1)} %get-tuple-element.67) | copy-start | bytes 1056772
  49.0 0.6 copy-start.15
  49.6 18.4 %collective-permute-start.8 = (bf16[128,1376]{1,0:T(8,128)(2,1)S(1)}, bf16[128,1376]{1,0:T(8,128)(2,1)S(1)}, u32[]{:S(2)}, u32[]{:S(2)}) collective-permute-start(bf16[128,1376]{1,0:T(8,128)(2,1)S(1)} %copy-done.23), channel_id=1, source_target_pairs={{0,8},{4,12},{8,0},{12,4},{1,9},{5,13},{9,1},{13,5},{2,10},{6,14},... | collective-permute-start | bytes 1056776 | tf_op jit(solution)/shard_map/h2/ppermute | solution.py:21
  50.6 22.4 %collective-permute-start.7 = (bf16[128,1376]{1,0:T(8,128)(2,1)S(1)}, bf16[128,1376]{1,0:T(8,128)(2,1)S(1)}, u32[]{:S(2)}, u32[]{:S(2)}) collective-permute-start(bf16[128,1376]{1,0:T(8,128)(2,1)S(1)} %copy-done.22), channel_id=1, source_target_pairs={{0,4},{4,0},{8,12},{12,8},{1,5},{5,1},{9,13},{13,9},{2,6},{6,2},{1... | collective-permute-start | bytes 1056776 | tf_op jit(solution)/shard_map/h1/ppermute | solution.py:21
  57.2 22.0 %collective-permute-start.11 = (bf16[128,2048]{1,0:T(8,128)(2,1)S(1)}, bf16[128,2048]{1,0:T(8,128)(2,1)S(1)}, u32[]{:S(2)}, u32[]{:S(2)}) collective-permute-start(bf16[128,2048]{1,0:T(8,128)(2,1)S(1)} %collective-permute-done.9.c), channel_id=1, source_target_pairs={{0,2},{2,0},{1,3},{3,1},{4,6},{6,4},{5,7},{7,5},{8,10},{10,8},{9,1... | collective-permute-start | bytes 1572872 | tf_op jit(solution)/shard_map/x3/ppermute | solution.py:21
  57.2 18.7 %slice-start = ((s8[11272192]{0:T(1024)(128)(4,1)}), s8[4194304]{0:T(1024)(128)(4,1)S(1)}, s32[]{:S(2)}) async-start(s8[11272192]{0:T(1024)(128)(4,1)} %bitcast.16), calls=%async_computation | async-start | bytes 8388608
  57.2 18.7 %slice-start.1 = ((s8[11272192]{0:T(1024)(128)(4,1)}), s8[4194304]{0:T(1024)(128)(4,1)S(1)}, s32[]{:S(2)}) async-start(s8[11272192]{0:T(1024)(128)(4,1)} %bitcast.16), calls=%async_computation.1 | async-start | bytes 8388608
  61.8 0.6 copy-start.17
  68.1 7.8 %slice-start.2 = ((s8[11272192]{0:T(1024)(128)(4,1)}), s8[2883584]{0:T(1024)(128)(4,1)S(1)}, s32[]{:S(2)}) async-start(s8[11272192]{0:T(1024)(128)(4,1)} %bitcast.16), calls=%async_computation.2 | async-start | bytes 5767168
  68.1 21.9 %collective-permute-start.12 = (bf16[128,2048]{1,0:T(8,128)(2,1)S(1)}, bf16[128,2048]{1,0:T(8,128)(2,1)S(1)}, u32[]{:S(2)}, u32[]{:S(2)}) collective-permute-start(bf16[128,2048]{1,0:T(8,128)(2,1)S(1)} %get-tuple-element.83), channel_id=1, source_target_pairs={{0,2},{2,0},{1,3},{3,1},{4,6},{6,4},{5,7},{7,5},{8,10},{10,8},{9,1... | collective-permute-start | bytes 1572872 | tf_op jit(solution)/shard_map/y3/ppermute | solution.py:21
  69.6 16.8 %collective-permute-start.13 = (bf16[1376,128]{1,0:T(8,128)(2,1)S(1)}, bf16[1376,128]{1,0:T(8,128)(2,1)S(1)}, u32[]{:S(2)}, u32[]{:S(2)}) collective-permute-start(bf16[1376,128]{1,0:T(8,128)(2,1)S(1)} %get-tuple-element.84), channel_id=1, source_target_pairs={{0,8},{4,12},{8,0},{12,4},{1,9},{5,13},{9,1},{13,5},{2,10},{6,14},... | collective-permute-start | bytes 1056776 | tf_op jit(solution)/shard_map/a2/ppermute | solution.py:21
  72.1 1.0 copy-start.6
  73.1 16.9 %collective-permute-start.14 = (bf16[1376,128]{1,0:T(8,128)(2,1)S(1)}, bf16[1376,128]{1,0:T(8,128)(2,1)S(1)}, u32[]{:S(2)}, u32[]{:S(2)}) collective-permute-start(bf16[1376,128]{1,0:T(8,128)(2,1)S(1)} %get-tuple-element.85), channel_id=1, source_target_pairs={{0,4},{4,0},{8,12},{12,8},{1,5},{5,1},{9,13},{13,9},{2,6},{6,2},{1... | collective-permute-start | bytes 1056776 | tf_op jit(solution)/shard_map/a1/ppermute | solution.py:21
  78.2 1.0 copy-start.8
  79.2 19.4 %collective-permute-start.17 = (bf16[128,2048]{1,0:T(8,128)(2,1)}, bf16[128,2048]{1,0:T(8,128)(2,1)}, u32[]{:S(2)}, u32[]{:S(2)}) collective-permute-start(bf16[128,2048]{1,0:T(8,128)(2,1)} %get-tuple-element.96), channel_id=1, source_target_pairs={{0,2},{2,0},{1,3},{3,1},{4,6},{6,4},{5,7},{7,5},{8,10},{10,8},{9,1... | collective-permute-start | bytes 1572872 | tf_op jit(solution)/shard_map/y2/ppermute | solution.py:21
  83.7 0.6 copy-start.19
  84.3 6.9 %copy-start.21 = (bf16[1376,128]{1,0:T(8,128)(2,1)}, bf16[1376,128]{1,0:T(8,128)(2,1)S(1)}, u32[]{:S(2)}) copy-start(bf16[1376,128]{1,0:T(8,128)(2,1)S(1)} %get-tuple-element.82) | copy-start | bytes 1056772
  86.3 4.8 %copy-start.25 = (bf16[1376,128]{1,0:T(8,128)(2,1)}, bf16[1376,128]{1,0:T(8,128)(2,1)S(1)}, u32[]{:S(2)}) copy-start(bf16[1376,128]{1,0:T(8,128)(2,1)S(1)} %collective-permute-done.13) | copy-start | bytes 1056772
  89.9 1.2 copy-start.27
  89.9 14.8 %collective-permute-start.16 = (bf16[128,2048]{1,0:T(8,128)(2,1)}, bf16[128,2048]{1,0:T(8,128)(2,1)}, u32[]{:S(2)}, u32[]{:S(2)}) collective-permute-start(bf16[128,2048]{1,0:T(8,128)(2,1)} %get-tuple-element.95), channel_id=1, source_target_pairs={{0,2},{2,0},{1,3},{3,1},{4,6},{6,4},{5,7},{7,5},{8,10},{10,8},{9,1... | collective-permute-start | bytes 1572872 | tf_op jit(solution)/shard_map/y1/ppermute | solution.py:21
  91.2 18.6 %collective-permute-start.18 = (bf16[128,2048]{1,0:T(8,128)(2,1)}, bf16[128,2048]{1,0:T(8,128)(2,1)}, u32[]{:S(2)}, u32[]{:S(2)}) collective-permute-start(bf16[128,2048]{1,0:T(8,128)(2,1)} %add_convert_fusion.3), channel_id=1, source_target_pairs={{0,4},{4,0},{8,12},{12,8},{1,5},{5,1},{9,13},{13,9},{2,6},{6,2},{1... | collective-permute-start | bytes 1572872 | tf_op jit(solution)/shard_map/r3/ppermute | solution.py:21
  91.3 13.5 %copy-start.9 = (f32[128,2048]{1,0:T(8,128)S(1)}, f32[128,2048]{1,0:T(8,128)}, u32[]{:S(2)}) copy-start(f32[128,2048]{1,0:T(8,128)} %copy-done.8) | copy-start | bytes 3145732
  91.3 20.8 %collective-permute-start.19 = (bf16[1376,128]{1,0:T(8,128)(2,1)}, bf16[1376,128]{1,0:T(8,128)(2,1)S(1)}, u32[]{:S(2)}, u32[]{:S(2)}) collective-permute-start(bf16[1376,128]{1,0:T(8,128)(2,1)} %copy-done.21), channel_id=1, source_target_pairs={{0,12},{4,8},{8,4},{12,0},{1,13},{5,9},{9,5},{13,1},{2,14},{6,10},... | collective-permute-start | bytes 1056776 | tf_op jit(solution)/shard_map/a3/ppermute | solution.py:21
  92.9 0.8 copy-start.14
  93.7 0.8 copy-start.16
  94.5 0.8 copy-start.18
  95.4 0.8 copy-start.20
  98.6 11.2 %copy-start.7 = (f32[128,2048]{1,0:T(8,128)S(1)}, f32[128,2048]{1,0:T(8,128)}, u32[]{:S(2)}) copy-start(f32[128,2048]{1,0:T(8,128)} %copy-done.6) | copy-start | bytes 3145732
  98.6 20.6 %collective-permute-start.20 = (f32[688,256]{1,0:T(8,128)}, f32[688,256]{1,0:T(8,128)}, u32[]{:S(2)}, u32[]{:S(2)}) collective-permute-start(f32[688,256]{1,0:T(8,128)} %get-tuple-element.92.h_low), channel_id=1, source_target_pairs={{0,1},{1,0},{2,3},{3,2},{4,5},{5,4},{6,7},{7,6},{8,9},{9,8},{10,11... | collective-permute-start | bytes 2113544 | tf_op jit(solution)/shard_map/rows/ppermute | solution.py:21
  98.6 20.6 %collective-permute-start.15 = (f32[688,256]{1,0:T(8,128)}, f32[688,256]{1,0:T(8,128)}, u32[]{:S(2)}, u32[]{:S(2)}) collective-permute-start(f32[688,256]{1,0:T(8,128)} %get-tuple-element.91.h_up), channel_id=1, source_target_pairs={{0,1},{1,0},{2,3},{3,2},{4,5},{5,4},{6,7},{7,6},{8,9},{9,8},{10,11... | collective-permute-start | bytes 2113544 | tf_op jit(solution)/shard_map/rows/ppermute | solution.py:21
  106.7 8.4 %copy-start.12 = (bf16[1376,128]{1,0:T(8,128)(2,1)S(1)}, bf16[1376,128]{1,0:T(8,128)(2,1)}, u32[]{:S(2)}) copy-start(bf16[1376,128]{1,0:T(8,128)(2,1)} %copy-done.11) | copy-start | bytes 1056772
  106.7 8.4 %copy-start.26 = (bf16[1376,128]{1,0:T(8,128)(2,1)S(1)}, bf16[1376,128]{1,0:T(8,128)(2,1)}, u32[]{:S(2)}) copy-start(bf16[1376,128]{1,0:T(8,128)(2,1)} %copy-done.25) | copy-start | bytes 1056772
  106.7 8.4 %copy-start.28 = (bf16[1376,128]{1,0:T(8,128)(2,1)S(1)}, bf16[1376,128]{1,0:T(8,128)(2,1)}, u32[]{:S(2)}) copy-start(bf16[1376,128]{1,0:T(8,128)(2,1)} %copy-done.27) | copy-start | bytes 1056772
  106.7 24.8 %collective-permute-start.22 = (bf16[128,2048]{1,0:T(8,128)(2,1)}, bf16[128,2048]{1,0:T(8,128)(2,1)}, u32[]{:S(2)}, u32[]{:S(2)}) collective-permute-start(bf16[128,2048]{1,0:T(8,128)(2,1)} %add_convert_fusion.2), channel_id=1, source_target_pairs={{0,4},{4,0},{8,12},{12,8},{1,5},{5,1},{9,13},{13,9},{2,6},{6,2},{1... | collective-permute-start | bytes 1572872 | tf_op jit(solution)/shard_map/r1/ppermute | solution.py:21
  112.0 22.5 %collective-permute-start.23 = (bf16[128,2048]{1,0:T(8,128)(2,1)}, bf16[128,2048]{1,0:T(8,128)(2,1)}, u32[]{:S(2)}, u32[]{:S(2)}) collective-permute-start(bf16[128,2048]{1,0:T(8,128)(2,1)} %add_convert_fusion.1), channel_id=1, source_target_pairs={{0,8},{4,12},{8,0},{12,4},{1,9},{5,13},{9,1},{13,5},{2,10},{6,14},... | collective-permute-start | bytes 1572872 | tf_op jit(solution)/shard_map/r2/ppermute | solution.py:21
  112.1 19.4 %collective-permute-start.21 = (bf16[128,2048]{1,0:T(8,128)(2,1)}, bf16[128,2048]{1,0:T(8,128)(2,1)}, u32[]{:S(2)}, u32[]{:S(2)}) collective-permute-start(bf16[128,2048]{1,0:T(8,128)(2,1)} %get-tuple-element.103), channel_id=1, source_target_pairs={{0,2},{2,0},{1,3},{3,1},{4,6},{6,4},{5,7},{7,5},{8,10},{10,8},{9,1... | collective-permute-start | bytes 1572872 | tf_op jit(solution)/shard_map/y0/ppermute | solution.py:21
  116.6 2.6 %copy-start.2 = (f32[1376,256]{1,0:T(8,128)S(1)}, f32[1376,256]{1,0:T(8,128)}, u32[]{:S(2)}) copy-start(f32[1376,256]{1,0:T(8,128)} %first.1) | copy-start | bytes 4227076
  119.2 1.4 copy-start.3
  120.6 11.0 %copy-start.5 = (f32[128,2048]{1,0:T(8,128)S(1)}, f32[128,2048]{1,0:T(8,128)}, u32[]{:S(2)}) copy-start(f32[128,2048]{1,0:T(8,128)} %copy-done.4) | copy-start | bytes 3145732

commit v4 on v3

--- a/solution.py
+++ b/solution.py
@@ -282,10 +282,11 @@
     c1 = swap(go(c0), "fsdp", 1, "c1")
     half = swap(halves(go(projector), 0, c)[0], "tp", 1, "half")
     p0, m0 = forward(at, h0, w_down)
+    seen(p0, c2)
+    h3 = swap(go(h3), "fsdp", 3, "h3")
+    x2 = swap(go(c2), "tp", 1, "x2")
+    c3 = swap(go(c2), "fsdp", 1, "c3")
     seen(p0, c2, half, x0)
-    x2 = swap(go(c2), "tp", 1, "x2")
-    h3 = swap(go(h3), "fsdp", 3, "h3")
-    c3 = swap(go(c2), "fsdp", 1, "c3")
     basis = swap(go(half), "sub", 1, "basis")
     seen(p0, c1, x0, basis)
     x1 = swap(go(c1), "tp", 1, "x1")

time: 137 us -> 137 us (level)
  no operation moved by 1% of the time
where the time goes in v4:
time: 137 us; the launch traced here: 136 us
  Pallas kernels  40.3 us (29%)
  waiting for transfers between devices  39.4 us (29%)
  starting transfers between devices  26.3 us (19%)
  local copies, waits for them, and re-layouts  19.6 us (14%)
  other arithmetic  9.89 us (7%)
    ppermute x24, waiting for transfers between devices, swap(): return lax.ppermute(x, axis, [(i, i ^ bit) for i in range(n)])  39.4 us
    pallas_call x9, Pallas kernels, in_vmem(): pl.pallas_call(kernel, in_specs=[pl.BlockSpec(memory_space=pltpu.SMEM)] +...  29.4 us
    ppermute x24, starting transfers between devices, swap(): return lax.ppermute(x, axis, [(i, i ^ bit) for i in range(n)])  26.3 us
    unnamed x65, local copies, waits for them, and re-layouts  15.4 us
    pallas_call x1, Pallas kernels, adam_step(): pl.pallas_call(kernel, grid=(4,), in_specs=[pl.BlockSpec(memory_space=plt...  10.9 us
    dynamic_slice x1, local copies, waits for them, and re-layouts, own_units(): return lax.dynamic_slice_in_dim(hidden_acts, (z ^ k) * width, width, 1)  3.28 us
  transfers between devices with their start and end apart: 24, of which 12 were waited for; matrix products, arithmetic and copies ran while one was open for 11% of the time, Pallas kernels for 30%

profile of v4, /device:TPU:0, one launch (start us, length us, event | category | flops | bytes accessed | tf_op | source)
XLA Modules:
  0.0 136.4 jit_solution(10987659763993638509)
XLA Ops:
  0.6 4.1 %collective-permute-start = (bf16[128,2048]{1,0:T(8,128)(2,1)}, bf16[128,2048]{1,0:T(8,128)(2,1)}, u32[]{:S(2)}, u32[]{:S(2)}) collective-permute-start(bf16[128,2048]{1,0:T(8,128)(2,1)} %c), channel_id=1, source_target_pairs={{0,8},{4,12},{8,0},{12,4},{1,9},{5,13},{9,1},{13,5},{2,10},{6,14},... | collective-permute-start | bytes 1572872 | tf_op jit(solution)/shard_map/c2/ppermute | solution.py:21
  4.7 1.5 %collective-permute-start.2 = (bf16[128,2048]{1,0:T(8,128)(2,1)}, bf16[128,2048]{1,0:T(8,128)(2,1)}, u32[]{:S(2)}, u32[]{:S(2)}) collective-permute-start(bf16[128,2048]{1,0:T(8,128)(2,1)} %c), channel_id=1, source_target_pairs={{0,2},{2,0},{1,3},{3,1},{4,6},{6,4},{5,7},{7,5},{8,10},{10,8},{9,1... | collective-permute-start | bytes 1572872 | tf_op jit(solution)/shard_map/x0/ppermute | solution.py:21
  6.2 3.3 %constant_dynamic-slice_fusion = (bf16[128,1376]{1,0:T(8,128)(2,1)}, bf16[128,1376]{1,0:T(8,128)(2,1)}, bf16[128,1376]{1,0:T(8,128)(2,1)S(1)}, bf16[128,1376]{1,0:T(8,128)(2,1)}) fusion(bf16[128,5504]{1,0:T(8,128)(2,1)} %param.6, s32[]{:T(128)S(6)} %select_n.32, s32[]{:T(128)S(6)} %select_n.29, s32[]{:T(128)S(6)} %select_n.28, s32[]{:T(128)S(6)} %select_n.31), kind=kLoop, calls=%fused_computation.11 | loop fusion | bytes 2818064 | tf_op jit(solution)/shard_map/dynamic_slice | solution.py:275
  9.5 0.8 constant_dynamic-slice_fusion.2
  10.3 0.5 collective-permute-start.3
  10.9 1.6 %collective-permute-start.1 = (bf16[128,2048]{1,0:T(8,128)(2,1)S(1)}, bf16[128,2048]{1,0:T(8,128)(2,1)}, u32[]{:S(2)}, u32[]{:S(2)}) collective-permute-start(bf16[128,2048]{1,0:T(8,128)(2,1)S(1)} %copy-done.10), channel_id=1, source_target_pairs={{0,4},{4,0},{8,12},{12,8},{1,5},{5,1},{9,13},{13,9},{2,6},{6,2},{1... | collective-permute-start | bytes 1572872 | tf_op jit(solution)/shard_map/c1/ppermute | solution.py:21
  12.5 0.1 pad_add_fusion.at
  12.5 4.2 %copy-done = bf16[1376,4096]{1,0:T(8,128)(2,1)S(1)} copy-done((bf16[1376,4096]{1,0:T(8,128)(2,1)S(1)}, bf16[1376,4096]{1,0:T(8,128)(2,1)}, u32[]{:S(2)}) %copy-start) | copy-done | bytes 11272216
  16.7 2.4 %forward.4 = (bf16[128,2048]{1,0:T(8,128)(2,1)}, f32[128,2048]{1,0:T(8,128)S(1)}) custom-call(s32[2]{0:T(128)S(1)} %pad_add_fusion.at, bf16[128,1376]{1,0:T(8,128)(2,1)S(1)} %get-tuple-element.118.h.refs_0_, bf16[1376,4096]{1,0:T(8,128)(2,1)S(1)} %copy-done), custom_call_target="tpu_custom_call" | custom-call | flops 1 | bytes 1 | tf_op jit(solution)/shard_map/forward/pallas_call | solution.py:134
  19.1 9.2 %collective-permute-done.c = bf16[128,2048]{1,0:T(8,128)(2,1)} collective-permute-done((bf16[128,2048]{1,0:T(8,128)(2,1)}, bf16[128,2048]{1,0:T(8,128)(2,1)}, u32[]{:S(2)}, u32[]{:S(2)}) %collective-permute-start) | collective-permute-done | bytes 524320 | tf_op jit(solution)/shard_map/c2/ppermute | solution.py:21
  28.3 1.2 collective-permute-done.3.got
  29.6 1.5 %collective-permute-start.5 = (bf16[128,2048]{1,0:T(8,128)(2,1)}, bf16[128,2048]{1,0:T(8,128)(2,1)S(1)}, u32[]{:S(2)}, u32[]{:S(2)}) collective-permute-start(bf16[128,2048]{1,0:T(8,128)(2,1)} %collective-permute-done.c), channel_id=1, source_target_pairs={{0,2},{2,0},{1,3},{3,1},{4,6},{6,4},{5,7},{7,5},{8,10},{10,8},{9,1... | collective-permute-start | bytes 1572872 | tf_op jit(solution)/shard_map/x2/ppermute | solution.py:21
  31.1 2.4 %collective-permute-start.6 = (bf16[128,1376]{1,0:T(8,128)(2,1)S(1)}, bf16[128,1376]{1,0:T(8,128)(2,1)S(1)}, u32[]{:S(2)}, u32[]{:S(2)}) collective-permute-start(bf16[128,1376]{1,0:T(8,128)(2,1)S(1)} %copy-done.24), channel_id=1, source_target_pairs={{0,12},{4,8},{8,4},{12,0},{1,13},{5,9},{9,5},{13,1},{2,14},{6,10},... | collective-permute-start | bytes 1056776 | tf_op jit(solution)/shard_map/h3/ppermute | solution.py:21
  33.4 0.4 collective-permute-done.1.c
  33.9 1.5 %collective-permute-start.10 = (bf16[128,2048]{1,0:T(8,128)(2,1)}, bf16[128,2048]{1,0:T(8,128)(2,1)S(1)}, u32[]{:S(2)}, u32[]{:S(2)}) collective-permute-start(bf16[128,2048]{1,0:T(8,128)(2,1)} %collective-permute-done.1.c), channel_id=1, source_target_pairs={{0,2},{2,0},{1,3},{3,1},{4,6},{6,4},{5,7},{7,5},{8,10},{10,8},{9,1... | collective-permute-start | bytes 1572872 | tf_op jit(solution)/shard_map/x1/ppermute | solution.py:21
  35.4 4.4 %backward.4 = (bf16[1376,128]{1,0:T(8,128)(2,1)S(1)}, bf16[128,256]{1,0:T(8,128)(2,1)S(1)}) custom-call(s32[2]{0:T(128)S(1)} %pad_add_fusion.at, bf16[128,2048]{1,0:T(8,128)(2,1)S(1)} %copy-done.10, bf16[128,2048]{1,0:T(8,128)(2,1)} %collective-permute-done.2.x, bf16[1376,4096]{1,0:T(8,128)(2,1)S(1)} %copy-done, bf16[2048,256]{1,0:T(8,128)(2,1)S(1)} %copy-done.1, ...), custom_call_target="tpu_custom_call" | custom-call | flops 1 | bytes 1 | tf_op jit(solution)/shard_map/backward/pallas_call | solution.py:134
  39.9 4.6 %collective-permute-done.5.x = bf16[128,2048]{1,0:T(8,128)(2,1)S(1)} collective-permute-done((bf16[128,2048]{1,0:T(8,128)(2,1)}, bf16[128,2048]{1,0:T(8,128)(2,1)S(1)}, u32[]{:S(2)}, u32[]{:S(2)}) %collective-permute-start.5) | collective-permute-done | bytes 524320 | tf_op jit(solution)/shard_map/x2/ppermute | solution.py:21
  44.5 4.5 %backward.5 = (bf16[1376,128]{1,0:T(8,128)(2,1)S(1)}, bf16[128,256]{1,0:T(8,128)(2,1)S(1)}) custom-call(s32[2]{0:T(128)S(1)} %pad_add_fusion.at, bf16[128,2048]{1,0:T(8,128)(2,1)} %collective-permute-done.c, bf16[128,2048]{1,0:T(8,128)(2,1)S(1)} %collective-permute-done.5.x, bf16[1376,4096]{1,0:T(8,128)(2,1)S(1)} %copy-done, ...), custom_call_target="tpu_custom_call" | custom-call | flops 1 | bytes 1 | tf_op jit(solution)/shard_map/backward/pallas_call | solution.py:134
  49.0 0.6 copy-done.15
  49.6 1.0 collective-permute-start.8
  50.6 1.9 %collective-permute-start.7 = (bf16[128,1376]{1,0:T(8,128)(2,1)S(1)}, bf16[128,1376]{1,0:T(8,128)(2,1)S(1)}, u32[]{:S(2)}, u32[]{:S(2)}) collective-permute-start(bf16[128,1376]{1,0:T(8,128)(2,1)S(1)} %copy-done.22), channel_id=1, source_target_pairs={{0,4},{4,0},{8,12},{12,8},{1,5},{5,1},{9,13},{13,9},{2,6},{6,2},{1... | collective-permute-start | bytes 1056776 | tf_op jit(solution)/shard_map/h1/ppermute | solution.py:21
  52.6 2.4 %forward.5 = (bf16[128,2048]{1,0:T(8,128)(2,1)S(1)}, f32[128,2048]{1,0:T(8,128)S(1)}) custom-call(s32[2]{0:T(128)S(1)} %pad_add_fusion.at, bf16[128,1376]{1,0:T(8,128)(2,1)S(1)} %collective-permute-done.6.h.refs_3_, bf16[1376,4096]{1,0:T(8,128)(2,1)S(1)} %copy-done), custom_call_target="tpu_custom_call" | custom-call | flops 1 | bytes 1 | tf_op jit(solution)/shard_map/forward/pallas_call | solution.py:134
  54.9 2.2 %collective-permute-done.9.c = bf16[128,2048]{1,0:T(8,128)(2,1)S(1)} collective-permute-done((bf16[128,2048]{1,0:T(8,128)(2,1)}, bf16[128,2048]{1,0:T(8,128)(2,1)S(1)}, u32[]{:S(2)}, u32[]{:S(2)}) %collective-permute-start.9) | collective-permute-done | bytes 524320 | tf_op jit(solution)/shard_map/c3/ppermute | solution.py:21
  57.2 4.6 %backward.6 = (bf16[1376,128]{1,0:T(8,128)(2,1)S(1)}, bf16[128,256]{1,0:T(8,128)(2,1)S(1)}) custom-call(s32[2]{0:T(128)S(1)} %pad_add_fusion.at, bf16[128,2048]{1,0:T(8,128)(2,1)} %collective-permute-done.1.c, bf16[128,2048]{1,0:T(8,128)(2,1)S(1)} %collective-permute-done.10.x, bf16[1376,4096]{1,0:T(8,128)(2,1)S(1)} %copy-done, ...), custom_call_target="tpu_custom_call" | custom-call | flops 1 | bytes 1 | tf_op jit(solution)/shard_map/backward/pallas_call | solution.py:134
  61.8 0.6 copy-done.17
  62.4 5.7 %collective-permute-done.8.h.refs_2_ = bf16[128,1376]{1,0:T(8,128)(2,1)S(1)} collective-permute-done((bf16[128,1376]{1,0:T(8,128)(2,1)S(1)}, bf16[128,1376]{1,0:T(8,128)(2,1)S(1)}, u32[]{:S(2)}, u32[]{:S(2)}) %collective-permute-start.8) | collective-permute-done | bytes 352288 | tf_op jit(solution)/shard_map/h2/ppermute | solution.py:21
  68.1 1.5 %collective-permute-start.12 = (bf16[128,2048]{1,0:T(8,128)(2,1)S(1)}, bf16[128,2048]{1,0:T(8,128)(2,1)S(1)}, u32[]{:S(2)}, u32[]{:S(2)}) collective-permute-start(bf16[128,2048]{1,0:T(8,128)(2,1)S(1)} %get-tuple-element.83), channel_id=1, source_target_pairs={{0,2},{2,0},{1,3},{3,1},{4,6},{6,4},{5,7},{7,5},{8,10},{10,8},{9,1... | collective-permute-start | bytes 1572872 | tf_op jit(solution)/shard_map/y3/ppermute | solution.py:21
  69.6 2.5 %forward.6 = (bf16[128,2048]{1,0:T(8,128)(2,1)}, f32[128,2048]{1,0:T(8,128)S(1)}) custom-call(s32[2]{0:T(128)S(1)} %pad_add_fusion.at, bf16[128,1376]{1,0:T(8,128)(2,1)S(1)} %collective-permute-done.8.h.refs_2_, bf16[1376,4096]{1,0:T(8,128)(2,1)S(1)} %copy-done), custom_call_target="tpu_custom_call" | custom-call | flops 1 | bytes 1 | tf_op jit(solution)/shard_map/forward/pallas_call | solution.py:134
  72.1 0.0 copy-start.6
  72.1 1.0 copy-done.6
  73.1 2.7 %collective-permute-start.14 = (bf16[1376,128]{1,0:T(8,128)(2,1)S(1)}, bf16[1376,128]{1,0:T(8,128)(2,1)S(1)}, u32[]{:S(2)}, u32[]{:S(2)}) collective-permute-start(bf16[1376,128]{1,0:T(8,128)(2,1)S(1)} %get-tuple-element.85), channel_id=1, source_target_pairs={{0,4},{4,0},{8,12},{12,8},{1,5},{5,1},{9,13},{13,9},{2,6},{6,2},{1... | collective-permute-start | bytes 1056776 | tf_op jit(solution)/shard_map/a1/ppermute | solution.py:21
  75.8 2.4 %forward.7 = (bf16[128,2048]{1,0:T(8,128)(2,1)}, f32[128,2048]{1,0:T(8,128)S(1)}) custom-call(s32[2]{0:T(128)S(1)} %pad_add_fusion.at, bf16[128,1376]{1,0:T(8,128)(2,1)S(1)} %collective-permute-done.7.h.refs_1_, bf16[1376,4096]{1,0:T(8,128)(2,1)S(1)} %bitcast.17), custom_call_target="tpu_custom_call" | custom-call | flops 1 | bytes 1 | tf_op jit(solution)/shard_map/forward/pallas_call | solution.py:134
  78.2 1.0 copy-done.8
  79.2 0.6 collective-permute-start.17
  79.8 3.9 %backward.7 = (bf16[1376,128]{1,0:T(8,128)(2,1)S(1)}, bf16[128,256]{1,0:T(8,128)(2,1)S(1)}) custom-call(s32[2]{0:T(128)S(1)} %pad_add_fusion.at, bf16[128,2048]{1,0:T(8,128)(2,1)S(1)} %collective-permute-done.9.c, bf16[128,2048]{1,0:T(8,128)(2,1)S(1)} %collective-permute-done.11.x, bf16[1376,4096]{1,0:T(8,128)(2,1)S(1)} %bitcast.17, ...), custom_call_target="tpu_custom_call" | custom-call | flops 1 | bytes 1 | tf_op jit(solution)/shard_map/backward/pallas_call | solution.py:134
  83.7 0.6 copy-done.19
  84.3 2.0 %collective-permute-done.13 = bf16[1376,128]{1,0:T(8,128)(2,1)S(1)} collective-permute-done((bf16[1376,128]{1,0:T(8,128)(2,1)S(1)}, bf16[1376,128]{1,0:T(8,128)(2,1)S(1)}, u32[]{:S(2)}, u32[]{:S(2)}) %collective-permute-start.13) | collective-permute-done | bytes 352288 | tf_op jit(solution)/shard_map/a2/ppermute | solution.py:21
  86.3 3.6 %collective-permute-done.14 = bf16[1376,128]{1,0:T(8,128)(2,1)S(1)} collective-permute-done((bf16[1376,128]{1,0:T(8,128)(2,1)S(1)}, bf16[1376,128]{1,0:T(8,128)(2,1)S(1)}, u32[]{:S(2)}, u32[]{:S(2)}) %collective-permute-start.14) | collective-permute-done | bytes 352288 | tf_op jit(solution)/shard_map/a1/ppermute | solution.py:21
  89.9 0.3 collective-permute-start.16
  90.2 0.9 add_convert_fusion.3
  91.2 0.1 collective-permute-start.18
  91.3 1.6 %collective-permute-start.19 = (bf16[1376,128]{1,0:T(8,128)(2,1)}, bf16[1376,128]{1,0:T(8,128)(2,1)S(1)}, u32[]{:S(2)}, u32[]{:S(2)}) collective-permute-start(bf16[1376,128]{1,0:T(8,128)(2,1)} %copy-done.21), channel_id=1, source_target_pairs={{0,12},{4,8},{8,4},{12,0},{1,13},{5,9},{9,5},{13,1},{2,14},{6,10},... | collective-permute-start | bytes 1056776 | tf_op jit(solution)/shard_map/a3/ppermute | solution.py:21
  92.9 0.8 copy-done.14
  93.7 0.8 copy-done.16
  94.5 0.8 copy-done.18
  95.4 0.8 copy-done.20
  96.2 2.4 %project.1 = (f32[688,256]{1,0:T(8,128)}, f32[688,256]{1,0:T(8,128)}) custom-call(s32[2]{0:T(128)S(1)} %pad_add_fusion.at, bf16[128,1376]{1,0:T(8,128)(2,1)S(1)} %get-tuple-element.118.h.refs_0_, bf16[128,1376]{1,0:T(8,128)(2,1)S(1)} %collective-permute-done.7.h.refs_1_, bf16[128,1376]{1,0:T(8,128)(2,1)S(1)} %collective-permute-done.8.h.refs_2_, ...), custom_call_target="tpu_custom_call" | custom-call | flops 1 | bytes 1 | tf_op jit(solution)/shard_map/project/pallas_call | solution.py:134
  98.6 0.5 collective-permute-start.15
  99.1 5.6 %collective-permute-done.16 = bf16[128,2048]{1,0:T(8,128)(2,1)} collective-permute-done((bf16[128,2048]{1,0:T(8,128)(2,1)}, bf16[128,2048]{1,0:T(8,128)(2,1)}, u32[]{:S(2)}, u32[]{:S(2)}) %collective-permute-start.16) | collective-permute-done | bytes 524320 | tf_op jit(solution)/shard_map/y1/ppermute | solution.py:21
  104.7 2.0 %add_convert_fusion.2 = bf16[128,2048]{1,0:T(8,128)(2,1)} fusion(f32[128,2048]{1,0:T(8,128)S(1)} %copy-done.9, bf16[128,2048]{1,0:T(8,128)(2,1)} %collective-permute-done.16), kind=kLoop, calls=%fused_computation.5 | loop fusion | flops 786432 | bytes 2097152 | tf_op jit(solution)/shard_map/convert_element_type | solution.py:323
  106.7 3.1 %collective-permute-done.18 = bf16[128,2048]{1,0:T(8,128)(2,1)} collective-permute-done((bf16[128,2048]{1,0:T(8,128)(2,1)}, bf16[128,2048]{1,0:T(8,128)(2,1)}, u32[]{:S(2)}, u32[]{:S(2)}) %collective-permute-start.18) | collective-permute-done | bytes 524320 | tf_op jit(solution)/shard_map/r3/ppermute | solution.py:21
  109.8 2.2 %add_convert_fusion.1 = bf16[128,2048]{1,0:T(8,128)(2,1)} fusion(bf16[128,2048]{1,0:T(8,128)(2,1)} %collective-permute-done.18, f32[128,2048]{1,0:T(8,128)S(1)} %copy-done.7, bf16[128,2048]{1,0:T(8,128)(2,1)} %collective-permute-done.17), kind=kLoop, calls=%fused_computation.4 | loop fusion | flops 1310720 | bytes 2621440 | tf_op jit(solution)/shard_map/convert_element_type | solution.py:326
  112.0 0.1 collective-permute-done.19
  112.1 3.0 %collective-permute-start.21 = (bf16[128,2048]{1,0:T(8,128)(2,1)}, bf16[128,2048]{1,0:T(8,128)(2,1)}, u32[]{:S(2)}, u32[]{:S(2)}) collective-permute-start(bf16[128,2048]{1,0:T(8,128)(2,1)} %get-tuple-element.103), channel_id=1, source_target_pairs={{0,2},{2,0},{1,3},{3,1},{4,6},{6,4},{5,7},{7,5},{8,10},{10,8},{9,1... | collective-permute-start | bytes 1572872 | tf_op jit(solution)/shard_map/y0/ppermute | solution.py:21
  115.1 0.2 pad_maximum_fusion
  115.3 0.1 dynamic-slice_bitcast_fusion.3
  115.4 1.2 maximum_bitcast_fusion
  116.6 2.6 %copy.11 = bf16[128,5504]{1,0:T(8,128)(2,1)} copy(bf16[128,5504]{0,1:T(8,128)(2,1)} %maximum_bitcast_fusion) | data formatting | bytes 2818048
  119.2 0.0 copy-start.3
  119.2 1.3 copy-done.3
  120.6 10.9 %adam_step.1 = (f32[1376,4096]{1,0:T(8,128)}, f32[1376,256]{1,0:T(8,128)}, f32[1376,256]{1,0:T(8,128)}) custom-call(s32[2]{0:T(128)S(1)} %pad_add_fusion.at, f32[688,256]{1,0:T(8,128)} %get-tuple-element.91.h_up, f32[688,256]{1,0:T(8,128)} %get-tuple-element.92.h_low, f32[688,256]{1,0:T(8,128)} %collective-permute-done.15.t_up, ...), custom_call_target="tpu_custom_call" | custom-call | flops 1 | bytes 1 | tf_op jit(solution)/shard_map/adam_step/pallas_call | solution.py:241
  131.5 1.4 %convert_add_fusion = f32[128,2048]{1,0:T(8,128)S(1)} fusion(bf16[128,2048]{1,0:T(8,128)(2,1)} %collective-permute-done.22, f32[128,2048]{1,0:T(8,128)S(1)} %copy-done.5, bf16[128,2048]{1,0:T(8,128)(2,1)} %collective-permute-done.21), kind=kLoop, calls=%fused_computation.3 | loop fusion | flops 1048576 | bytes 3145728 | tf_op jit(solution)/shard_map/add | solution.py:339
  133.0 1.5 %collective-permute-done.23 = bf16[128,2048]{1,0:T(8,128)(2,1)} collective-permute-done((bf16[128,2048]{1,0:T(8,128)(2,1)}, bf16[128,2048]{1,0:T(8,128)(2,1)}, u32[]{:S(2)}, u32[]{:S(2)}) %collective-permute-start.23) | collective-permute-done | bytes 524320 | tf_op jit(solution)/shard_map/r2/ppermute | solution.py:21
  134.5 1.9 %add_convert_fusion = bf16[128,2048]{1,0:T(8,128)(2,1)} fusion(f32[128,2048]{1,0:T(8,128)S(1)} %convert_add_fusion, bf16[128,2048]{1,0:T(8,128)(2,1)} %collective-permute-done.23), kind=kLoop, calls=%fused_computation.2 | loop fusion | flops 786432 | bytes 2097152 | tf_op jit(solution)/shard_map/convert_element_type | solution.py:341
  (71 shorter events, 0.2 us)
Async XLA Ops:
  0.6 27.7 %collective-permute-start = (bf16[128,2048]{1,0:T(8,128)(2,1)}, bf16[128,2048]{1,0:T(8,128)(2,1)}, u32[]{:S(2)}, u32[]{:S(2)}) collective-permute-start(bf16[128,2048]{1,0:T(8,128)(2,1)} %c), channel_id=1, source_target_pairs={{0,8},{4,12},{8,0},{12,4},{1,9},{5,13},{9,1},{13,5},{2,10},{6,14},... | collective-permute-start | bytes 1572872 | tf_op jit(solution)/shard_map/c2/ppermute | solution.py:21
  4.7 23.6 %collective-permute-start.2 = (bf16[128,2048]{1,0:T(8,128)(2,1)}, bf16[128,2048]{1,0:T(8,128)(2,1)}, u32[]{:S(2)}, u32[]{:S(2)}) collective-permute-start(bf16[128,2048]{1,0:T(8,128)(2,1)} %c), channel_id=1, source_target_pairs={{0,2},{2,0},{1,3},{3,1},{4,6},{6,4},{5,7},{7,5},{8,10},{10,8},{9,1... | collective-permute-start | bytes 1572872 | tf_op jit(solution)/shard_map/x0/ppermute | solution.py:21
  6.2 3.3 %copy-start.1 = (bf16[2048,256]{1,0:T(8,128)(2,1)S(1)}, bf16[2048,256]{1,0:T(8,128)(2,1)}, u32[]{:S(2)}) copy-start(bf16[2048,256]{1,0:T(8,128)(2,1)} %basis.9) | copy-start | bytes 3145732
  6.2 4.6 %copy-start.10 = (bf16[128,2048]{1,0:T(8,128)(2,1)S(1)}, bf16[128,2048]{1,0:T(8,128)(2,1)}, u32[]{:S(2)}) copy-start(bf16[128,2048]{1,0:T(8,128)(2,1)} %c) | copy-start | bytes 1572868
  10.3 19.2 %collective-permute-start.3 = (bf16[1024,256]{1,0:T(8,128)(2,1)}, bf16[1024,256]{1,0:T(8,128)(2,1)S(1)}, u32[]{:S(2)}, u32[]{:S(2)}) collective-permute-start(bf16[1024,256]{1,0:T(8,128)(2,1)} %constant_dynamic-slice_fusion.2), channel_id=1, source_target_pairs={{0,2},{2,0},{1,3},{3,1},{4,6},{6,4},{5,7},{7,5},{8,10},{10,8},{9,1... | collective-permute-start | bytes 1572872 | tf_op jit(solution)/shard_map/half/ppermute | solution.py:21
  10.9 23.0 %collective-permute-start.1 = (bf16[128,2048]{1,0:T(8,128)(2,1)S(1)}, bf16[128,2048]{1,0:T(8,128)(2,1)}, u32[]{:S(2)}, u32[]{:S(2)}) collective-permute-start(bf16[128,2048]{1,0:T(8,128)(2,1)S(1)} %copy-done.10), channel_id=1, source_target_pairs={{0,4},{4,0},{8,12},{12,8},{1,5},{5,1},{9,13},{13,9},{2,6},{6,2},{1... | collective-permute-start | bytes 1572872 | tf_op jit(solution)/shard_map/c1/ppermute | solution.py:21
  12.5 4.2 %copy-start = (bf16[1376,4096]{1,0:T(8,128)(2,1)S(1)}, bf16[1376,4096]{1,0:T(8,128)(2,1)}, u32[]{:S(2)}) copy-start(bf16[1376,4096]{1,0:T(8,128)(2,1)} %w.15) | copy-start | bytes 33816580
  16.7 14.3 %copy-start.24 = (bf16[128,1376]{1,0:T(8,128)(2,1)S(1)}, bf16[128,1376]{1,0:T(8,128)(2,1)}, u32[]{:S(2)}) copy-start(bf16[128,1376]{1,0:T(8,128)(2,1)} %get-tuple-element.66) | copy-start | bytes 1056772
  19.1 20.7 %copy-start.4 = (f32[128,2048]{1,0:T(8,128)}, f32[128,2048]{1,0:T(8,128)S(1)}, u32[]{:S(2)}) copy-start(f32[128,2048]{1,0:T(8,128)S(1)} %get-tuple-element.102) | copy-start | bytes 3145732
  29.6 4.3 %collective-permute-start.4 = (bf16[1024,256]{1,0:T(8,128)(2,1)S(1)}, bf16[1024,256]{1,0:T(8,128)(2,1)S(1)}, u32[]{:S(2)}, u32[]{:S(2)}) collective-permute-start(bf16[1024,256]{1,0:T(8,128)(2,1)S(1)} %collective-permute-done.3.got), channel_id=1, source_target_pairs={{0,1},{1,0},{2,3},{3,2},{4,5},{5,4},{6,7},{7,6},{8,9},{9,8},{10,11... | collective-permute-start | bytes 1572872 | tf_op jit(solution)/shard_map/basis/ppermute | solution.py:21
  29.6 14.9 %collective-permute-start.5 = (bf16[128,2048]{1,0:T(8,128)(2,1)}, bf16[128,2048]{1,0:T(8,128)(2,1)S(1)}, u32[]{:S(2)}, u32[]{:S(2)}) collective-permute-start(bf16[128,2048]{1,0:T(8,128)(2,1)} %collective-permute-done.c), channel_id=1, source_target_pairs={{0,2},{2,0},{1,3},{3,1},{4,6},{6,4},{5,7},{7,5},{8,10},{10,8},{9,1... | collective-permute-start | bytes 1572872 | tf_op jit(solution)/shard_map/x2/ppermute | solution.py:21
  31.1 18.6 %collective-permute-start.6 = (bf16[128,1376]{1,0:T(8,128)(2,1)S(1)}, bf16[128,1376]{1,0:T(8,128)(2,1)S(1)}, u32[]{:S(2)}, u32[]{:S(2)}) collective-permute-start(bf16[128,1376]{1,0:T(8,128)(2,1)S(1)} %copy-done.24), channel_id=1, source_target_pairs={{0,12},{4,8},{8,4},{12,0},{1,13},{5,9},{9,5},{13,1},{2,14},{6,10},... | collective-permute-start | bytes 1056776 | tf_op jit(solution)/shard_map/h3/ppermute | solution.py:21
  33.4 23.7 %collective-permute-start.9 = (bf16[128,2048]{1,0:T(8,128)(2,1)}, bf16[128,2048]{1,0:T(8,128)(2,1)S(1)}, u32[]{:S(2)}, u32[]{:S(2)}) collective-permute-start(bf16[128,2048]{1,0:T(8,128)(2,1)} %collective-permute-done.c), channel_id=1, source_target_pairs={{0,4},{4,0},{8,12},{12,8},{1,5},{5,1},{9,13},{13,9},{2,6},{6,2},{1... | collective-permute-start | bytes 1572872 | tf_op jit(solution)/shard_map/c3/ppermute | solution.py:21
  33.9 23.3 %collective-permute-start.10 = (bf16[128,2048]{1,0:T(8,128)(2,1)}, bf16[128,2048]{1,0:T(8,128)(2,1)S(1)}, u32[]{:S(2)}, u32[]{:S(2)}) collective-permute-start(bf16[128,2048]{1,0:T(8,128)(2,1)} %collective-permute-done.1.c), channel_id=1, source_target_pairs={{0,2},{2,0},{1,3},{3,1},{4,6},{6,4},{5,7},{7,5},{8,10},{10,8},{9,1... | collective-permute-start | bytes 1572872 | tf_op jit(solution)/shard_map/x1/ppermute | solution.py:21
  39.8 9.1 %copy-start.11 = (bf16[1376,128]{1,0:T(8,128)(2,1)}, bf16[1376,128]{1,0:T(8,128)(2,1)S(1)}, u32[]{:S(2)}) copy-start(bf16[1376,128]{1,0:T(8,128)(2,1)S(1)} %get-tuple-element.99) | copy-start | bytes 1056772
  39.9 9.1 %copy-start.13 = (bf16[128,256]{1,0:T(8,128)(2,1)}, bf16[128,256]{1,0:T(8,128)(2,1)S(1)}, u32[]{:S(2)}) copy-start(bf16[128,256]{1,0:T(8,128)(2,1)S(1)} %get-tuple-element.87.refs_4_) | copy-start | bytes 196612
  44.5 5.1 %copy-start.23 = (bf16[128,1376]{1,0:T(8,128)(2,1)S(1)}, bf16[128,1376]{1,0:T(8,128)(2,1)}, u32[]{:S(2)}) copy-start(bf16[128,1376]{1,0:T(8,128)(2,1)} %get-tuple-element.68) | copy-start | bytes 1056772
  44.5 6.1 %copy-start.22 = (bf16[128,1376]{1,0:T(8,128)(2,1)S(1)}, bf16[128,1376]{1,0:T(8,128)(2,1)}, u32[]{:S(2)}) copy-start(bf16[128,1376]{1,0:T(8,128)(2,1)} %get-tuple-element.67) | copy-start | bytes 1056772
  49.0 0.6 copy-start.15
  49.6 18.4 %collective-permute-start.8 = (bf16[128,1376]{1,0:T(8,128)(2,1)S(1)}, bf16[128,1376]{1,0:T(8,128)(2,1)S(1)}, u32[]{:S(2)}, u32[]{:S(2)}) collective-permute-start(bf16[128,1376]{1,0:T(8,128)(2,1)S(1)} %copy-done.23), channel_id=1, source_target_pairs={{0,8},{4,12},{8,0},{12,4},{1,9},{5,13},{9,1},{13,5},{2,10},{6,14},... | collective-permute-start | bytes 1056776 | tf_op jit(solution)/shard_map/h2/ppermute | solution.py:21
  50.6 22.4 %collective-permute-start.7 = (bf16[128,1376]{1,0:T(8,128)(2,1)S(1)}, bf16[128,1376]{1,0:T(8,128)(2,1)S(1)}, u32[]{:S(2)}, u32[]{:S(2)}) collective-permute-start(bf16[128,1376]{1,0:T(8,128)(2,1)S(1)} %copy-done.22), channel_id=1, source_target_pairs={{0,4},{4,0},{8,12},{12,8},{1,5},{5,1},{9,13},{13,9},{2,6},{6,2},{1... | collective-permute-start | bytes 1056776 | tf_op jit(solution)/shard_map/h1/ppermute | solution.py:21
  57.2 22.0 %collective-permute-start.11 = (bf16[128,2048]{1,0:T(8,128)(2,1)S(1)}, bf16[128,2048]{1,0:T(8,128)(2,1)S(1)}, u32[]{:S(2)}, u32[]{:S(2)}) collective-permute-start(bf16[128,2048]{1,0:T(8,128)(2,1)S(1)} %collective-permute-done.9.c), channel_id=1, source_target_pairs={{0,2},{2,0},{1,3},{3,1},{4,6},{6,4},{5,7},{7,5},{8,10},{10,8},{9,1... | collective-permute-start | bytes 1572872 | tf_op jit(solution)/shard_map/x3/ppermute | solution.py:21
  57.2 18.7 %slice-start = ((s8[11272192]{0:T(1024)(128)(4,1)}), s8[4194304]{0:T(1024)(128)(4,1)S(1)}, s32[]{:S(2)}) async-start(s8[11272192]{0:T(1024)(128)(4,1)} %bitcast.16), calls=%async_computation | async-start | bytes 8388608
  57.2 18.7 %slice-start.1 = ((s8[11272192]{0:T(1024)(128)(4,1)}), s8[4194304]{0:T(1024)(128)(4,1)S(1)}, s32[]{:S(2)}) async-start(s8[11272192]{0:T(1024)(128)(4,1)} %bitcast.16), calls=%async_computation.1 | async-start | bytes 8388608
  61.8 0.6 copy-start.17
  68.1 7.8 %slice-start.2 = ((s8[11272192]{0:T(1024)(128)(4,1)}), s8[2883584]{0:T(1024)(128)(4,1)S(1)}, s32[]{:S(2)}) async-start(s8[11272192]{0:T(1024)(128)(4,1)} %bitcast.16), calls=%async_computation.2 | async-start | bytes 5767168
  68.1 21.9 %collective-permute-start.12 = (bf16[128,2048]{1,0:T(8,128)(2,1)S(1)}, bf16[128,2048]{1,0:T(8,128)(2,1)S(1)}, u32[]{:S(2)}, u32[]{:S(2)}) collective-permute-start(bf16[128,2048]{1,0:T(8,128)(2,1)S(1)} %get-tuple-element.83), channel_id=1, source_target_pairs={{0,2},{2,0},{1,3},{3,1},{4,6},{6,4},{5,7},{7,5},{8,10},{10,8},{9,1... | collective-permute-start | bytes 1572872 | tf_op jit(solution)/shard_map/y3/ppermute | solution.py:21
  69.6 16.8 %collective-permute-start.13 = (bf16[1376,128]{1,0:T(8,128)(2,1)S(1)}, bf16[1376,128]{1,0:T(8,128)(2,1)S(1)}, u32[]{:S(2)}, u32[]{:S(2)}) collective-permute-start(bf16[1376,128]{1,0:T(8,128)(2,1)S(1)} %get-tuple-element.84), channel_id=1, source_target_pairs={{0,8},{4,12},{8,0},{12,4},{1,9},{5,13},{9,1},{13,5},{2,10},{6,14},... | collective-permute-start | bytes 1056776 | tf_op jit(solution)/shard_map/a2/ppermute | solution.py:21
  72.1 1.0 copy-start.6
  73.1 16.9 %collective-permute-start.14 = (bf16[1376,128]{1,0:T(8,128)(2,1)S(1)}, bf16[1376,128]{1,0:T(8,128)(2,1)S(1)}, u32[]{:S(2)}, u32[]{:S(2)}) collective-permute-start(bf16[1376,128]{1,0:T(8,128)(2,1)S(1)} %get-tuple-element.85), channel_id=1, source_target_pairs={{0,4},{4,0},{8,12},{12,8},{1,5},{5,1},{9,13},{13,9},{2,6},{6,2},{1... | collective-permute-start | bytes 1056776 | tf_op jit(solution)/shard_map/a1/ppermute | solution.py:21
  78.2 1.0 copy-start.8
  79.2 19.4 %collective-permute-start.17 = (bf16[128,2048]{1,0:T(8,128)(2,1)}, bf16[128,2048]{1,0:T(8,128)(2,1)}, u32[]{:S(2)}, u32[]{:S(2)}) collective-permute-start(bf16[128,2048]{1,0:T(8,128)(2,1)} %get-tuple-element.96), channel_id=1, source_target_pairs={{0,2},{2,0},{1,3},{3,1},{4,6},{6,4},{5,7},{7,5},{8,10},{10,8},{9,1... | collective-permute-start | bytes 1572872 | tf_op jit(solution)/shard_map/y2/ppermute | solution.py:21
  83.7 0.6 copy-start.19
  84.3 6.9 %copy-start.21 = (bf16[1376,128]{1,0:T(8,128)(2,1)}, bf16[1376,128]{1,0:T(8,128)(2,1)S(1)}, u32[]{:S(2)}) copy-start(bf16[1376,128]{1,0:T(8,128)(2,1)S(1)} %get-tuple-element.82) | copy-start | bytes 1056772
  86.3 4.8 %copy-start.25 = (bf16[1376,128]{1,0:T(8,128)(2,1)}, bf16[1376,128]{1,0:T(8,128)(2,1)S(1)}, u32[]{:S(2)}) copy-start(bf16[1376,128]{1,0:T(8,128)(2,1)S(1)} %collective-permute-done.13) | copy-start | bytes 1056772
  89.9 1.2 copy-start.27
  89.9 14.8 %collective-permute-start.16 = (bf16[128,2048]{1,0:T(8,128)(2,1)}, bf16[128,2048]{1,0:T(8,128)(2,1)}, u32[]{:S(2)}, u32[]{:S(2)}) collective-permute-start(bf16[128,2048]{1,0:T(8,128)(2,1)} %get-tuple-element.95), channel_id=1, source_target_pairs={{0,2},{2,0},{1,3},{3,1},{4,6},{6,4},{5,7},{7,5},{8,10},{10,8},{9,1... | collective-permute-start | bytes 1572872 | tf_op jit(solution)/shard_map/y1/ppermute | solution.py:21
  91.2 18.6 %collective-permute-start.18 = (bf16[128,2048]{1,0:T(8,128)(2,1)}, bf16[128,2048]{1,0:T(8,128)(2,1)}, u32[]{:S(2)}, u32[]{:S(2)}) collective-permute-start(bf16[128,2048]{1,0:T(8,128)(2,1)} %add_convert_fusion.3), channel_id=1, source_target_pairs={{0,4},{4,0},{8,12},{12,8},{1,5},{5,1},{9,13},{13,9},{2,6},{6,2},{1... | collective-permute-start | bytes 1572872 | tf_op jit(solution)/shard_map/r3/ppermute | solution.py:21
  91.3 13.5 %copy-start.9 = (f32[128,2048]{1,0:T(8,128)S(1)}, f32[128,2048]{1,0:T(8,128)}, u32[]{:S(2)}) copy-start(f32[128,2048]{1,0:T(8,128)} %copy-done.8) | copy-start | bytes 3145732
  91.3 20.8 %collective-permute-start.19 = (bf16[1376,128]{1,0:T(8,128)(2,1)}, bf16[1376,128]{1,0:T(8,128)(2,1)S(1)}, u32[]{:S(2)}, u32[]{:S(2)}) collective-permute-start(bf16[1376,128]{1,0:T(8,128)(2,1)} %copy-done.21), channel_id=1, source_target_pairs={{0,12},{4,8},{8,4},{12,0},{1,13},{5,9},{9,5},{13,1},{2,14},{6,10},... | collective-permute-start | bytes 1056776 | tf_op jit(solution)/shard_map/a3/ppermute | solution.py:21
  92.9 0.8 copy-start.14
  93.7 0.8 copy-start.16
  94.5 0.8 copy-start.18
  95.4 0.8 copy-start.20
  98.6 11.2 %copy-start.7 = (f32[128,2048]{1,0:T(8,128)S(1)}, f32[128,2048]{1,0:T(8,128)}, u32[]{:S(2)}) copy-start(f32[128,2048]{1,0:T(8,128)} %copy-done.6) | copy-start | bytes 3145732
  98.6 20.6 %collective-permute-start.20 = (f32[688,256]{1,0:T(8,128)}, f32[688,256]{1,0:T(8,128)}, u32[]{:S(2)}, u32[]{:S(2)}) collective-permute-start(f32[688,256]{1,0:T(8,128)} %get-tuple-element.92.h_low), channel_id=1, source_target_pairs={{0,1},{1,0},{2,3},{3,2},{4,5},{5,4},{6,7},{7,6},{8,9},{9,8},{10,11... | collective-permute-start | bytes 2113544 | tf_op jit(solution)/shard_map/rows/ppermute | solution.py:21
  98.6 20.6 %collective-permute-start.15 = (f32[688,256]{1,0:T(8,128)}, f32[688,256]{1,0:T(8,128)}, u32[]{:S(2)}, u32[]{:S(2)}) collective-permute-start(f32[688,256]{1,0:T(8,128)} %get-tuple-element.91.h_up), channel_id=1, source_target_pairs={{0,1},{1,0},{2,3},{3,2},{4,5},{5,4},{6,7},{7,6},{8,9},{9,8},{10,11... | collective-permute-start | bytes 2113544 | tf_op jit(solution)/shard_map/rows/ppermute | solution.py:21
  106.7 8.4 %copy-start.12 = (bf16[1376,128]{1,0:T(8,128)(2,1)S(1)}, bf16[1376,128]{1,0:T(8,128)(2,1)}, u32[]{:S(2)}) copy-start(bf16[1376,128]{1,0:T(8,128)(2,1)} %copy-done.11) | copy-start | bytes 1056772
  106.7 8.4 %copy-start.26 = (bf16[1376,128]{1,0:T(8,128)(2,1)S(1)}, bf16[1376,128]{1,0:T(8,128)(2,1)}, u32[]{:S(2)}) copy-start(bf16[1376,128]{1,0:T(8,128)(2,1)} %copy-done.25) | copy-start | bytes 1056772
  106.7 8.4 %copy-start.28 = (bf16[1376,128]{1,0:T(8,128)(2,1)S(1)}, bf16[1376,128]{1,0:T(8,128)(2,1)}, u32[]{:S(2)}) copy-start(bf16[1376,128]{1,0:T(8,128)(2,1)} %copy-done.27) | copy-start | bytes 1056772
  106.7 24.8 %collective-permute-start.22 = (bf16[128,2048]{1,0:T(8,128)(2,1)}, bf16[128,2048]{1,0:T(8,128)(2,1)}, u32[]{:S(2)}, u32[]{:S(2)}) collective-permute-start(bf16[128,2048]{1,0:T(8,128)(2,1)} %add_convert_fusion.2), channel_id=1, source_target_pairs={{0,4},{4,0},{8,12},{12,8},{1,5},{5,1},{9,13},{13,9},{2,6},{6,2},{1... | collective-permute-start | bytes 1572872 | tf_op jit(solution)/shard_map/r1/ppermute | solution.py:21
  112.0 22.5 %collective-permute-start.23 = (bf16[128,2048]{1,0:T(8,128)(2,1)}, bf16[128,2048]{1,0:T(8,128)(2,1)}, u32[]{:S(2)}, u32[]{:S(2)}) collective-permute-start(bf16[128,2048]{1,0:T(8,128)(2,1)} %add_convert_fusion.1), channel_id=1, source_target_pairs={{0,8},{4,12},{8,0},{12,4},{1,9},{5,13},{9,1},{13,5},{2,10},{6,14},... | collective-permute-start | bytes 1572872 | tf_op jit(solution)/shard_map/r2/ppermute | solution.py:21
  112.1 19.4 %collective-permute-start.21 = (bf16[128,2048]{1,0:T(8,128)(2,1)}, bf16[128,2048]{1,0:T(8,128)(2,1)}, u32[]{:S(2)}, u32[]{:S(2)}) collective-permute-start(bf16[128,2048]{1,0:T(8,128)(2,1)} %get-tuple-element.103), channel_id=1, source_target_pairs={{0,2},{2,0},{1,3},{3,1},{4,6},{6,4},{5,7},{7,5},{8,10},{10,8},{9,1... | collective-permute-start | bytes 1572872 | tf_op jit(solution)/shard_map/y0/ppermute | solution.py:21
  116.6 2.6 %copy-start.2 = (f32[1376,256]{1,0:T(8,128)S(1)}, f32[1376,256]{1,0:T(8,128)}, u32[]{:S(2)}) copy-start(f32[1376,256]{1,0:T(8,128)} %first.1) | copy-start | bytes 4227076
  119.2 1.4 copy-start.3
  120.6 11.0 %copy-start.5 = (f32[128,2048]{1,0:T(8,128)S(1)}, f32[128,2048]{1,0:T(8,128)}, u32[]{:S(2)}) copy-start(f32[128,2048]{1,0:T(8,128)} %copy-done.4) | copy-start | bytes 3145732
